TPU v7x, 32 devices: a whole 2x2x4 slice. The times are simulated.
32 devices in a mesh: row: 8 (over z, x), col: 4 (over y, core).
Axes of the slice: x: 2, y: 2, z: 4, core: 2. Of those that a mesh axis runs over, the one named last changes fastest.
Arguments:
- amplitudes: bfloat16 [1024, 8192], P('row', 'col'), may hold values from -6 to 6
- integrals: bfloat16 [8192, 16384], P('col', 'row'), may hold values from -0.125 to 0.125
- tile_irrep: int32 [24], replicated, may hold values from 0 to 3
- product_pairs: int32 [64, 2], P('row'), may hold values from 0 to 23, as said below
- summed_pairs: int32 [32, 2], P('col'), may hold values from 0 to 23, as said below
Outputs:
- residual: bfloat16 [1024, 16384], P('col', 'row')
Inputs may be any that keep to these rules, and one draw needn't show every extreme that they name: `product_pairs`: for p < 32, entry p + 32 holds the two tiles of entry p in swapped order; the two tiles of an entry differ; no entry repeats. `summed_pairs`: no entry repeats.
All inputs are finite; a program needn't handle non-finite values.
Results may differ from a plain program's by a relative error of at most 0.001.
Values may be sent and summed in bfloat16 or wider, within the bound.
No kernel may reach another device: no remote copies, remote signals or barrier semaphores. Data moves between devices by JAX's collectives and lax.ppermute only.
A program may use at most 192 MiB of HBM per device.

v0:
```python
import jax
import jax.numpy as jnp
from jax import lax
from jax.sharding import PartitionSpec as P

TS = 16
OT = 32


def from_partner(value, axis, distance):
    mask = 2**distance
    pairs = [(source, source ^ mask) for source in range(lax.axis_size(axis))]
    return lax.ppermute(value, axis, pairs)


def pair_symmetry(tile_irrep, pairs):
    return jnp.bitwise_xor(tile_irrep[pairs[:, 0]], tile_irrep[pairs[:, 1]])


def on_device(amplitudes, integrals, tile_irrep, product_pairs, summed_pairs):
    product_sym = pair_symmetry(tile_irrep, product_pairs)
    summed_sym = pair_symmetry(tile_irrep, summed_pairs)
    allowed = summed_sym[:, None] == product_sym[None, :]
    summed_count = summed_pairs.shape[0]
    product_count = product_pairs.shape[0]
    pair_size = TS * TS
    keep = allowed.astype(integrals.dtype)
    masked = (
        integrals.reshape(summed_count, pair_size, product_count, pair_size)
        * keep[:, None, :, None]
    ).reshape(integrals.shape)
    half_bit = lax.axis_size("row").bit_length() - 2
    ladder = jnp.dot(
        lax.all_gather(amplitudes, "row", axis=0, tiled=True),
        masked,
        preferred_element_type=jnp.float32,
    )
    partner = from_partner(ladder, "row", half_bit)
    partner = partner.reshape(OT, OT, product_count, TS, TS)
    partner = jnp.transpose(partner, (1, 0, 2, 4, 3)).reshape(ladder.shape)
    summed = lax.psum_scatter(ladder + partner, "col", scatter_dimension=0, tiled=True)
    return summed.astype(jnp.bfloat16)


def solution(mesh):
    return jax.shard_map(
        on_device,
        mesh=mesh,
        in_specs=(P("row", "col"), P("col", "row"), P(), P("row", None), P("col", None)),
        out_specs=P("col", "row"),
        check_vma=False,
    )
```

profile of v0, /device:TPU:0, one launch (start us, length us, event | category | flops | bytes accessed | tf_op | source)
XLA Modules:
  0.0 636.8 jit_solution(7007078687383593365)
XLA Ops:
  6.5 0.0 copy-start
  6.5 0.0 all-gather.2.cloned.1.call-start
  6.5 0.7 all-gather.2.cloned.1.call-update
  7.3 0.0 reduce-scatter.2.cloned.1.call-start
  7.3 0.8 fusion.6
  8.1 0.0 copy-done
  8.1 0.6 gather_fusion.1
  8.7 0.6 gather_fusion
  9.4 0.8 fusion.8
  10.1 0.6 gather_fusion.3
  10.8 0.6 gather_fusion.2
  11.5 0.1 compare_convert_fusion
  11.5 3.9 mul.11
  15.4 10.3 %copy.10 = bf16[256,8,8,256]{3,1,2,0:T(8,128)(2,1)} copy(bf16[256,8,8,256]{3,2,1,0:T(8,128)(2,1)} %bitcast.22) | data formatting | bytes 16777216
  25.7 60.0 %all-gather.2.cloned.1.call-done = bf16[1024,2048]{1,0:T(8,128)(2,1)} async-done(((bf16[128,2048]{1,0:T(8,128)(2,1)}), bf16[1024,2048]{1,0:T(8,128)(2,1)}) %all-gather.2.cloned.1.call-update) | async-done | bytes 4194320 | tf_op jit(solution)/shard_map/all_gather | solution.py:34
  85.6 13.1 %fusion.2 = f32[1024,2048]{0,1:T(8,128)S(1)} fusion(bf16[1024,2048]{1,0:T(8,128)(2,1)} %all-gather.2.cloned.1.call-done, bf16[2048,2048]{1,0:T(8,128)(2,1)} %param.6, bf16[2048,2048]{1,0:T(8,128)(2,1)} %bitcast.23), kind=kOutput, calls=%fused_computation.6 | convolution fusion | flops 8594128896 | bytes 29360128 | tf_op jit(solution)/shard_map/dot_general | solution.py:33
  98.7 0.0 copy-start.2
  98.7 3.2 copy-done.2
  101.9 1.6 collective-permute-start
  103.5 360.2 %collective-permute-done = f32[1024,2048]{0,1:T(8,128)} collective-permute-done((f32[1024,2048]{0,1:T(8,128)S(1)}, f32[1024,2048]{0,1:T(8,128)}, u32[]{:S(2)}, u32[]{:S(2)}) %collective-permute-start) | collective-permute-done | bytes 8388640 | tf_op jit(solution)/shard_map/ppermute | solution.py:13
  463.7 21.7 %reshape.46 = f32[32,32,8,16,16]{1,0,4,3,2:T(8,128)} reshape(f32[1024,2048]{0,1:T(8,128)} %collective-permute-done) | data formatting | bytes 16777216 | tf_op jit(solution)/shard_map/reshape | solution.py:39
  485.4 31.8 %copy.8 = f32[32,32,8,16,16]{0,1,3,4,2:T(8,128)} copy(f32[32,32,8,16,16]{1,0,4,3,2:T(8,128)} %reshape.46) | data formatting | bytes 16777216 | tf_op jit(solution)/shard_map/reshape | solution.py:39
  517.2 26.1 %reshape.47 = f32[1024,2048]{0,1:T(8,128)} reshape(f32[32,32,8,16,16]{1,0,4,3,2:T(8,128)} %bitcast.21) | data formatting | bytes 16777216 | tf_op jit(solution)/shard_map/reshape | solution.py:40
  543.3 0.0 copy-start.1
  543.3 12.0 %add.25 = f32[1024,2048]{0,1:T(8,128)} add(f32[1024,2048]{0,1:T(8,128)} %copy-done.2, f32[1024,2048]{0,1:T(8,128)} %reshape.47) | non-fusion elementwise | flops 2097152 | bytes 25165824 | tf_op jit(solution)/shard_map/add | solution.py:41
  555.3 0.0 reduce-scatter.2.cloned.1.call-update
  555.3 71.5 %reduce-scatter.2.cloned.1.call-done = f32[256,2048]{0,1:T(8,128)} async-done(((f32[1024,2048]{0,1:T(8,128)}), f32[256,2048]{0,1:T(8,128)}) %reduce-scatter.2.cloned.1.call-update) | async-done | bytes 2097168 | tf_op jit(solution)/shard_map/reduce_scatter | solution.py:41
  626.8 1.7 convert_element_type.11
  628.5 1.4 copy.9
  629.9 0.0 copy-done.1
  (4 shorter events, 0.0 us)
Async XLA Ops:
  6.5 1.5 copy-start
  6.5 79.1 %all-gather.2.cloned.1.call-start = ((), (), s32[]{:S(2)}) async-start(), calls=%async_computation.1 | async-start | bytes 4718592 | tf_op jit(solution)/shard_map/all_gather | solution.py:34
  7.3 619.6 %reduce-scatter.2.cloned.1.call-start = ((), (), s32[]{:S(2)}) async-start(), calls=%async_computation.2 | async-start | bytes 10485760 | tf_op jit(solution)/shard_map/reduce_scatter | solution.py:41
  98.7 3.2 copy-start.2
  101.9 361.8 %collective-permute-start = (f32[1024,2048]{0,1:T(8,128)S(1)}, f32[1024,2048]{0,1:T(8,128)}, u32[]{:S(2)}, u32[]{:S(2)}) collective-permute-start(f32[1024,2048]{0,1:T(8,128)S(1)} %fusion.2), channel_id=1, source_target_pairs={{0,16},{4,20},{8,24},{12,28},{16,0},{20,4},{24,8},{28,12},{1,17},{... | collective-permute-start | bytes 25165832 | tf_op jit(solution)/shard_map/ppermute | solution.py:13
  543.3 86.6 %copy-start.1 = (s32[24]{0:T(128)S(1)}, s32[24]{0:T(128)}, u32[]{:S(2)}) copy-start(s32[24]{0:T(128)} %param.7) | copy-start | bytes 292
Sparse Core Ops, SparseCore 0:
  9.5 76.0 all-gather.1
  555.5 71.3 reduce-scatter.1
where the time goes:
time: 639 us; the launch traced here: 637 us
  waiting for transfers between devices  492 us (77%)
  local copies, waits for them, and re-layouts  101 us (16%)
  other arithmetic  15.3 us (2%)
  between operations  13.4 us (2%)
  matrix products  13.1 us (2%)
    ppermute x1, waiting for transfers between devices, from_partner(): return lax.ppermute(value, axis, pairs)  360 us
    reduce_scatter x1, waiting for transfers between devices, on_device(): lax.psum_scatter(ladder + partner, 'col', scatter_dimension=0, tiled=True)  71.5 us
    all_gather x1, waiting for transfers between devices, on_device(): lax.all_gather(amplitudes, 'row', axis=0, tiled=True)  60 us
    reshape x2, local copies, waits for them, and re-layouts, on_device(): partner = partner.reshape(OT, OT, product_count, TS, TS)  53.5 us
    reshape x1, local copies, waits for them, and re-layouts, on_device(): partner = jnp.transpose(partner, (1, 0, 2, 4, 3)).reshape(ladder.shape)  26.1 us
    unnamed x7, local copies, waits for them, and re-layouts  13.5 us
    dot_general x1, matrix products, on_device(): jnp.dot(lax.all_gather(amplitudes, 'row', axis=0, tiled=True), masked, pr...  13.1 us
  transfers between devices with their start and end apart: 3, of which 3 were waited for; matrix products, arithmetic and copies ran while one was open for 3% of the time, Pallas kernels for 0%

commit v1 on v0

--- a/solution.py
+++ b/solution.py
@@ -1,10 +1,18 @@
+import functools
+
 import jax
 import jax.numpy as jnp
+import numpy as np
 from jax import lax
+from jax.experimental import pallas as pl
+from jax.experimental.pallas import tpu as pltpu
 from jax.sharding import PartitionSpec as P
 
 TS = 16
+TP = TS * TS
 OT = 32
+WIRE = jnp.float16
+LADDER_VMEM = 16 * 2**20
 
 
 def from_partner(value, axis, distance):
@@ -17,16 +25,15 @@
     return jnp.bitwise_xor(tile_irrep[pairs[:, 0]], tile_irrep[pairs[:, 1]])
 
 
-def on_device(amplitudes, integrals, tile_irrep, product_pairs, summed_pairs):
+def plain(amplitudes, integrals, tile_irrep, product_pairs, summed_pairs):
     product_sym = pair_symmetry(tile_irrep, product_pairs)
     summed_sym = pair_symmetry(tile_irrep, summed_pairs)
     allowed = summed_sym[:, None] == product_sym[None, :]
     summed_count = summed_pairs.shape[0]
     product_count = product_pairs.shape[0]
-    pair_size = TS * TS
     keep = allowed.astype(integrals.dtype)
     masked = (
-        integrals.reshape(summed_count, pair_size, product_count, pair_size)
+        integrals.reshape(summed_count, TP, product_count, TP)
         * keep[:, None, :, None]
     ).reshape(integrals.shape)
     half_bit = lax.axis_size("row").bit_length() - 2
@@ -42,9 +49,247 @@
     return summed.astype(jnp.bfloat16)
 
 
+NZ, NX, NY, NC = 4, 2, 2, 2
+ROWS = 128
+PART = 64
+OWNED = 256
+PLANES = ((0, 1, 2, 3), (1, 0, 2, 3), (2, 3, 1, 0), (3, 2, 1, 0))
+
+
+def selection(source_of_row):
+    n = len(source_of_row)
+    matrix = np.zeros((n, n), np.float32)
+    matrix[np.arange(n), source_of_row] = 1
+    return matrix
+
+
+def order_of(extents, axes):
+    return np.arange(int(np.prod(extents))).reshape(extents).transpose(axes).reshape(-1)
+
+
+BLOCK = selection(order_of((4, 32), (1, 0)))
+ALIGN = selection(order_of((2, 2, 4, 4), (1, 0, 3, 2)))
+NATURAL = selection(order_of((4, 2, 8, 4), (1, 3, 0, 2)))
+SWAP = selection(order_of((16, 16), (1, 0)))
+
+
+def send(value, target):
+    pairs = []
+    for n, (z, x, y, k) in enumerate(np.ndindex(NZ, NX, NY, NC)):
+        to = target(z, x, y, k)
+        if to is not None:
+            pairs.append((n, int(np.ravel_multi_index(to, (NZ, NX, NY, NC)))))
+    return lax.ppermute(value, ("row", "col"), pairs)
+
+
+def along_z(value, moves):
+    return send(value, lambda z, x, y, k: (moves[z], x, y, k) if z in moves else None)
+
+
+def across_x(value):
+    return send(value, lambda z, x, y, k: (z, 1 - x, y, k))
+
+
+def across_y(value):
+    return send(value, lambda z, x, y, k: (z, x, 1 - y, k))
+
+
+def across_core(value):
+    return send(value, lambda z, x, y, k: (z, x, y, 1 - k))
+
+
+def to_partner(value):
+    return send(value, lambda z, x, y, k: (z ^ 2, x, y, k))
+
+
+def to_owner(value, step):
+    def target(z, x, y, k):
+        plane = PLANES[z][step]
+        return (z, x, 1 - y, k) if (1 - y, k) == (plane // NC, plane % NC) else None
+
+    return send(value, target)
+
+
+def matmul(a, b):
+    return jnp.dot(a, b, preferred_element_type=jnp.float32)
+
+
+def part_at(distance):
+    return distance ^ (distance >> 1)
+
+
+def ladder_kernel(place, irrep, product, summed, here, beside, block_order, integrals, *refs):
+    out, rows = refs[-2:]
+    x, col = place[0] % NX, place[1]
+    for block, at in ((here, x), (beside, 1 - x)):
+        start = pl.multiple_of(at * ROWS, ROWS)
+        rows[pl.ds(start, ROWS), :] = matmul(block_order[...], block[...]).astype(jnp.bfloat16)
+    for panel in range(8):
+        wanted = irrep[product[panel, 0]] ^ irrep[product[panel, 1]]
+        kept = []
+        for q in range(8):
+            same = (irrep[summed[q, 0]] ^ irrep[summed[q, 1]]) == wanted
+            value = rows[:, q * TP : (q + 1) * TP]
+            kept.append(jnp.where(same, value, jnp.zeros_like(value)))
+        cut = slice(panel * TP, (panel + 1) * TP)
+        total = matmul(jnp.concatenate(kept, axis=1), integrals[:, cut])
+        for to in range(4):
+            for at in range(2):
+                start = at * ROWS + to * 32
+                out[part_at(to ^ col), at * 32 : (at + 1) * 32, cut] = total[start : start + 32, :]
+
+
+def partial_ladder(place, irrep, product, summed, here, beside, integrals, after):
+    vmem = pl.BlockSpec(memory_space=pltpu.VMEM)
+    smem = pl.BlockSpec(memory_space=pltpu.SMEM)
+    return pl.pallas_call(
+        ladder_kernel,
+        in_specs=[smem] * 4 + [vmem] * 4 + [pl.BlockSpec(memory_space=pl.ANY)] * len(after),
+        out_specs=vmem,
+        scratch_shapes=[pltpu.VMEM((2 * ROWS, 2048), jnp.bfloat16)],
+        out_shape=jax.ShapeDtypeStruct((4, PART, 2048), jnp.float32),
+        compiler_params=pltpu.CompilerParams(vmem_limit_bytes=LADDER_VMEM),
+        cost_estimate=pl.CostEstimate(flops=1000, bytes_accessed=1000, transcendentals=0),
+        name="partial_ladder",
+    )(place, irrep, product, summed, here, beside, jnp.asarray(BLOCK, jnp.bfloat16), integrals, *after)
+
+
+def turn(arrived, align, swap):
+    high = arrived.astype(jnp.bfloat16)
+    low = (arrived - high.astype(jnp.float32)).astype(jnp.bfloat16)
+    both = jnp.concatenate([high, low], axis=0)
+    cuts = [both[:, p * TP : (p + 1) * TP] for p in range(8)]
+    both = jnp.concatenate([matmul(cut, swap).astype(jnp.bfloat16) for cut in cuts], axis=1)
+    return matmul(align, both[:PART]) + matmul(align, both[PART:])
+
+
+def turn_kernel(arrived, align, swap, out):
+    out[...] = turn(arrived[...], align[...], swap[...])
+
+
+def turned(arrived):
+    return pl.pallas_call(
+        turn_kernel,
+        out_shape=jax.ShapeDtypeStruct((PART, 2048), jnp.float32),
+        compiler_params=pltpu.CompilerParams(vmem_limit_bytes=12 * 2**20),
+        name="turn",
+    )(arrived, *(jnp.asarray(m, jnp.bfloat16) for m in (ALIGN, SWAP)))
+
+
+def finish_kernel(place, *refs):
+    pairs, mines, (rest, turned0, turned1, turned2, last, align, natural, swap, out, own, other, total, sems) = refs[:4], refs[4:8], refs[8:]
+    z, col = place[0] // NX, place[1]
+
+    def plane_of(side, step):
+        plane = PLANES[0][step]
+        for at in (1, 2, 3):
+            plane = jnp.where(side == at, PLANES[at][step], plane)
+        return plane
+
+    def copies(step):
+        return (
+            pltpu.make_async_copy(pairs[step].at[1:4], own.at[1:4], sems.at[0]),
+            pltpu.make_async_copy(mines[step], own.at[0], sems.at[1]),
+        )
+
+    for step in range(4):
+
+        @pl.when(plane_of(z, step) == col)
+        def _(step=step):
+            for copy in copies(step):
+                copy.start()
+
+    for step, ref in enumerate((turned0, turned1, turned2, None)):
+        value = turn(last[...], align[...], swap[...]) if ref is None else ref[...]
+        other[plane_of(z ^ 2, step)] = value
+    for copy in copies(0):
+        copy.wait()
+    for n in range(4):
+        plane = part_at(n) ^ col
+        value = own[n] + other[plane]
+        if n > 0:
+            value += rest[3 - n]
+        total[pl.ds(pl.multiple_of(plane * PART, PART), PART), :] = value.astype(jnp.bfloat16)
+    for p in range(8):
+        cut = slice(p * TP, (p + 1) * TP)
+        out[:, cut] = matmul(natural[...], total[:, cut]).astype(jnp.bfloat16)
+
+
+def finish(place, pairs, mines, rest, done, last):
+    vmem = pl.BlockSpec(memory_space=pltpu.VMEM)
+    return pl.pallas_call(
+        finish_kernel,
+        in_specs=[pl.BlockSpec(memory_space=pltpu.SMEM)] + [pl.BlockSpec(memory_space=pl.ANY)] * 8 + [vmem] * 8,
+        out_specs=vmem,
+        out_shape=jax.ShapeDtypeStruct((OWNED, 2048), jnp.bfloat16),
+        scratch_shapes=[
+            pltpu.VMEM((4, PART, 2048), jnp.float32),
+            pltpu.VMEM((4, PART, 2048), jnp.float32),
+            pltpu.VMEM((OWNED, 2048), jnp.bfloat16),
+            pltpu.SemaphoreType.DMA((2,)),
+        ],
+        compiler_params=pltpu.CompilerParams(vmem_limit_bytes=24 * 2**20),
+        name="finish",
+    )(place, *pairs, *mines, rest, *done, last, *(jnp.asarray(m, jnp.bfloat16) for m in (ALIGN, NATURAL, SWAP)))
+
+
+def encode(value):
+    return value.astype(WIRE)
+
+
+def decode(value):
+    return value.astype(jnp.float32)
+
+
+def after(value, *tokens):
+    return lax.optimization_barrier((value, *tokens))[0]
+
+
+def on_device(amplitudes, integrals, tile_irrep, product_pairs, summed_pairs):
+    row, col = lax.axis_index("row"), lax.axis_index("col")
+    z = row // NX
+    place = jnp.stack([row, col]).astype(jnp.int32)
+    inner = (z == 1) | (z == 2)
+
+    here, beside = [amplitudes], [across_x(amplitudes)]
+    near = along_z(amplitudes, {0: 1, 1: 0, 2: 3, 3: 2})
+    middle = along_z(amplitudes, {1: 2, 2: 1})
+    here.append(near)
+    beside.append(across_x(near))
+    crossed = along_z(near, {1: 2, 2: 1})
+    here.append(jnp.where(inner, middle, along_z(middle, {1: 0, 2: 3})))
+    beside.append(across_x(here[2]))
+    here.append(jnp.where(inner, crossed, along_z(crossed, {1: 0, 2: 3})))
+    beside.append(across_x(here[3]))
+    arrived = ((near, middle), (here[2], crossed), (here[3],), ())
+
+    pairs, mines, others = [], [], []
+    rest = 0
+    tokens = ()
+    for step in range(4):
+        part = partial_ladder(place, tile_irrep, product_pairs, summed_pairs, here[step], beside[step], integrals, arrived[step] + tokens)
+        sibling = across_core(part)
+        if step > 0:
+            mines.append(pairs[-1][0] + decode(over_y))
+            sent = encode(mines[-1])
+            others.append(to_partner(sent))
+            part = after(part, sent)
+        part = (part.reshape(2, 2, PART, 2048) + sibling.reshape(2, 2, PART, 2048)[:, ::-1]).reshape(part.shape)
+        pairs.append(part)
+        sent = encode(part[3])
+        tokens = (part,)
+        over_y = across_y(sent)
+        rest = rest + to_owner(encode(part[:3]), step)
+    mines.append(pairs[-1][0] + decode(over_y))
+    others.append(to_partner(encode(mines[-1])))
+    done = [turned(decode(other)) for other in others[:3]]
+    return finish(place, pairs, mines, decode(rest), done, decode(others[3]))
+
+
 def solution(mesh):
+    body = on_device if (mesh.shape["row"], mesh.shape["col"]) == (NZ * NX, NY * NC) else plain
     return jax.shard_map(
-        on_device,
+        body,
         mesh=mesh,
         in_specs=(P("row", "col"), P("col", "row"), P(), P("row", None), P("col", None)),
         out_specs=P("col", "row"),

time: 639 us -> 156 us (0.24)
  waiting for transfers between devices: 492 us -> 90.7 us
  local copies, waits for them, and re-layouts: 101 us -> 13.7 us
  starting transfers between devices: 1.63 us -> 26.2 us
  Pallas kernels: 0 us -> 18.6 us
  matrix products: 13.1 us -> 0 us
  between operations: 13.4 us -> 0.73 us
  other arithmetic: 15.3 us -> 5.83 us
    ppermute x1 -> x25, waiting for transfers between devices: 360 us -> 90.7 us  [send(): return lax.ppermute(value, ('row', 'col'), pairs)]
    reshape x3 -> x0, local copies, waits for them, and re-layouts: 79.6 us -> none  [the longest x2 53.5 us: on_device(): partner = partner.reshape(OT, OT, product_count, TS, TS)]
    reduce_scatter x1 -> x0, waiting for transfers between devices: 71.5 us -> none  [on_device(): lax.psum_scatter(ladder + partner, 'col', scatter_dimension=0, tiled=True)]
    all_gather x1 -> x0, waiting for transfers between devices: 60 us -> none  [on_device(): lax.all_gather(amplitudes, 'row', axis=0, tiled=True)]
    ppermute x1 -> x25, starting transfers between devices: 1.59 us -> 26.2 us  [send(): return lax.ppermute(value, ('row', 'col'), pairs)]
    pallas_call x0 -> x8, Pallas kernels: none -> 18.6 us  [the longest x4 13.8 us: partial_ladder(): pl.pallas_call(ladder_kernel, in_specs=[smem] * 4 + [vmem] * 4 + [pl.Bloc...]
    dot_general x1 -> x0, matrix products: 13.1 us -> none  [on_device(): jnp.dot(lax.all_gather(amplitudes, 'row', axis=0, tiled=True), masked, pr...]
    add x1 -> x4, other arithmetic: 12 us -> 2.86 us  [on_device(): part.reshape(2, 2, PART, 2048) + sibling.reshape(2, 2, PART, 2048)[:, ::-1]]
  transfers between devices with their start and end apart: 3 -> 25, of which waited for: 3 -> 11; matrix products, arithmetic and copies ran while one was open for 3% -> 5% of each run, Pallas kernels for 0% -> 1%
where the time goes in v1:
time: 156 us
  waiting for transfers between devices  90.7 us (58%)
  starting transfers between devices  26.2 us (17%)
  Pallas kernels  18.6 us (12%)
  local copies, waits for them, and re-layouts  13.7 us (9%)
  other arithmetic  5.83 us (4%)
    ppermute x25, waiting for transfers between devices, send(): return lax.ppermute(value, ('row', 'col'), pairs)  90.7 us
    ppermute x25, starting transfers between devices, send(): return lax.ppermute(value, ('row', 'col'), pairs)  26.2 us
    pallas_call x4, Pallas kernels, partial_ladder(): pl.pallas_call(ladder_kernel, in_specs=[smem] * 4 + [vmem] * 4 + [pl.Bloc...  13.8 us
    unnamed x30, local copies, waits for them, and re-layouts  12.8 us
    pallas_call x1, Pallas kernels, finish(): pl.pallas_call(finish_kernel, in_specs=[pl.BlockSpec(memory_space=pltpu.S...  3.19 us
  transfers between devices with their start and end apart: 25, of which 11 were waited for; matrix products, arithmetic and copies ran while one was open for 5% of the time, Pallas kernels for 1%

profile of v1, /device:TPU:0, one launch (start us, length us, event | category | flops | bytes accessed | tf_op | source)
XLA Modules:
  0.0 155.7 jit_solution(14904163304992754462)
XLA Ops:
  0.0 3.0 %collective-permute-start.1 = (bf16[128,2048]{1,0:T(8,128)(2,1)}, bf16[128,2048]{1,0:T(8,128)(2,1)S(1)}, u32[]{:S(2)}, u32[]{:S(2)}) collective-permute-start(bf16[128,2048]{1,0:T(8,128)(2,1)} %here.1), channel_id=1, source_target_pairs={{0,8},{1,9},{2,10},{3,11},{4,12},{5,13},{6,14},{7,15},{8,0},{9,1},... | collective-permute-start | bytes 1572872 | tf_op jit(solution)/shard_map/ppermute | solution.py:82
  3.0 1.5 collective-permute-start
  4.5 0.7 collective-permute-start.2
  5.2 0.8 copy.19.product
  6.0 0.8 copy.20.summed
  6.8 8.4 %collective-permute-done.1.refs_0_.here = bf16[128,2048]{1,0:T(8,128)(2,1)S(1)} collective-permute-done((bf16[128,2048]{1,0:T(8,128)(2,1)}, bf16[128,2048]{1,0:T(8,128)(2,1)S(1)}, u32[]{:S(2)}, u32[]{:S(2)}) %collective-permute-start.1) | collective-permute-done | bytes 524320 | tf_op jit(solution)/shard_map/ppermute | solution.py:82
  15.2 1.5 collective-permute-done.beside
  16.6 0.8 copy-done.6
  17.4 3.4 %copy-done = bf16[2048,2048]{1,0:T(8,128)(2,1)S(1)} copy-done((bf16[2048,2048]{1,0:T(8,128)(2,1)S(1)}, bf16[2048,2048]{1,0:T(8,128)(2,1)}, u32[]{:S(2)}) %copy-start) | copy-done | bytes 8388632
  20.8 0.8 copy-done.3
  21.6 1.0 copy-done.5
  22.6 1.0 copy-done.7
  23.6 0.7 copy-done.10
  24.3 3.5 %partial_ladder.4 = f32[4,64,2048]{2,1,0:T(8,128)S(1)} custom-call(s32[2]{0:T(128)S(1)} %pad_add_fusion.place, s32[24]{0:T(128)S(1)} %copy-done.10, s32[8,2]{1,0:T(8,128)S(1)} %copy.19.product, s32[8,2]{1,0:T(8,128)S(1)} %copy.20.summed, bf16[128,2048]{1,0:T(8,128)(2,1)S(1)} %copy-done.5, bf16[128,2048]{1,0:T(8,128)(2,1)S(1)} %copy-done.7, ...), custom_call_target="tpu_custom_call" | custom-call | flops 1000 | bytes 1000 | tf_op jit(solution)/shard_map/partial_ladder/pallas_call | solution.py:145
  27.8 1.3 collective-permute-start.5
  29.2 0.7 collective-permute-start.6
  29.9 1.6 %collective-permute-start.4 = (bf16[128,2048]{1,0:T(8,128)(2,1)S(1)}, bf16[128,2048]{1,0:T(8,128)(2,1)S(1)}, u32[]{:S(2)}, u32[]{:S(2)}) collective-permute-start(bf16[128,2048]{1,0:T(8,128)(2,1)S(1)} %collective-permute-done.1.refs_0_.here), channel_id=1, source_target_pairs={{0,4},{1,5},{2,6},{3,7},{4,0},{5,1},{6,2},{7,3},{8,12},{9,13},{10,... | collective-permute-start | bytes 1572872 | tf_op jit(solution)/shard_map/ppermute | solution.py:82
  31.4 14.1 %collective-permute-done.5 = bf16[128,2048]{1,0:T(8,128)(2,1)} collective-permute-done((bf16[128,2048]{1,0:T(8,128)(2,1)S(1)}, bf16[128,2048]{1,0:T(8,128)(2,1)}, u32[]{:S(2)}, u32[]{:S(2)}) %collective-permute-start.5) | collective-permute-done | bytes 524320 | tf_op jit(solution)/shard_map/ppermute | solution.py:82
  45.5 1.2 broadcast_select_fusion.1.refs_0_.here
  46.8 2.0 %reverse_add_fusion.3 = f32[2,2,64,2048]{3,2,1,0:T(8,128)S(1)} fusion(f32[2,2,64,2048]{3,2,1,0:T(8,128)S(1)} %bitcast.62, f32[2,2,64,2048]{3,2,1,0:T(8,128)} %bitcast.3), kind=kLoop, calls=%fused_computation.3 | loop fusion | flops 524288 | bytes 6291456 | tf_op jit(solution)/shard_map/add | solution.py:277
  48.8 3.4 %copy-done.1 = bf16[2048,2048]{1,0:T(8,128)(2,1)S(1)} copy-done((bf16[2048,2048]{1,0:T(8,128)(2,1)S(1)}, bf16[2048,2048]{1,0:T(8,128)(2,1)}, u32[]{:S(2)}) %copy-start.1) | copy-done | bytes 8388632
  52.2 3.5 %partial_ladder.5 = f32[4,64,2048]{2,1,0:T(8,128)S(1)} custom-call(s32[2]{0:T(128)S(1)} %pad_add_fusion.place, s32[24]{0:T(128)S(1)} %copy-done.11, s32[8,2]{1,0:T(8,128)S(1)} %copy.19.product, s32[8,2]{1,0:T(8,128)S(1)} %copy.20.summed, bf16[128,2048]{1,0:T(8,128)(2,1)S(1)} %collective-permute-done.1.refs_0_.here, ...), custom_call_target="tpu_custom_call" | custom-call | flops 1000 | bytes 1000 | tf_op jit(solution)/shard_map/partial_ladder/pallas_call | solution.py:145
  55.7 0.6 collective-permute-start.9
  56.3 1.5 collective-permute-start.10
  58.0 1.6 %collective-permute-start.7 = (f16[64,2048]{1,0:T(8,128)(2,1)S(1)}, f16[64,2048]{1,0:T(8,128)(2,1)S(1)}, u32[]{:S(2)}, u32[]{:S(2)}) collective-permute-start(f16[64,2048]{1,0:T(8,128)(2,1)S(1)} %slice_bitcast_fusion.7), channel_id=1, source_target_pairs={{0,2},{1,3},{2,0},{3,1},{4,6},{5,7},{6,4},{7,5},{8,10},{9,11},{10,... | collective-permute-start | bytes 786440 | tf_op jit(solution)/shard_map/ppermute | solution.py:82
  59.6 12.9 %collective-permute-done.10 = bf16[128,2048]{1,0:T(8,128)(2,1)S(1)} collective-permute-done((bf16[128,2048]{1,0:T(8,128)(2,1)S(1)}, bf16[128,2048]{1,0:T(8,128)(2,1)S(1)}, u32[]{:S(2)}, u32[]{:S(2)}) %collective-permute-start.10) | collective-permute-done | bytes 524320 | tf_op jit(solution)/shard_map/ppermute | solution.py:82
  73.0 3.4 %partial_ladder.6 = f32[4,64,2048]{2,1,0:T(8,128)S(1)} custom-call(s32[2]{0:T(128)S(1)} %pad_add_fusion.place, s32[24]{0:T(128)S(1)} %copy-done.11, s32[8,2]{1,0:T(8,128)S(1)} %copy.19.product, s32[8,2]{1,0:T(8,128)S(1)} %copy.20.summed, bf16[128,2048]{1,0:T(8,128)(2,1)S(1)} %broadcast_select_fusion.1.refs_0_.here, ...), custom_call_target="tpu_custom_call" | custom-call | flops 1000 | bytes 1000 | tf_op jit(solution)/shard_map/partial_ladder/pallas_call | solution.py:145
  76.7 1.6 %collective-permute-start.11 = (f16[64,2048]{1,0:T(8,128)(2,1)S(1)}, f16[64,2048]{1,0:T(8,128)(2,1)S(1)}, u32[]{:S(2)}, u32[]{:S(2)}) collective-permute-start(f16[64,2048]{1,0:T(8,128)(2,1)S(1)} %slice_bitcast_fusion.6), channel_id=1, source_target_pairs={{0,2},{1,3},{2,0},{3,1},{4,6},{5,7},{6,4},{7,5},{8,10},{9,11},{10,... | collective-permute-start | bytes 786440 | tf_op jit(solution)/shard_map/ppermute | solution.py:82
  78.3 1.5 collective-permute-start.13
  79.7 5.7 %collective-permute-done.11 = f16[64,2048]{1,0:T(8,128)(2,1)S(1)} collective-permute-done((f16[64,2048]{1,0:T(8,128)(2,1)S(1)}, f16[64,2048]{1,0:T(8,128)(2,1)S(1)}, u32[]{:S(2)}, u32[]{:S(2)}) %collective-permute-start.11) | collective-permute-done | bytes 262176 | tf_op jit(solution)/shard_map/ppermute | solution.py:82
  85.8 6.5 %collective-permute-done.13.beside = bf16[128,2048]{1,0:T(8,128)(2,1)S(1)} collective-permute-done((bf16[128,2048]{1,0:T(8,128)(2,1)S(1)}, bf16[128,2048]{1,0:T(8,128)(2,1)S(1)}, u32[]{:S(2)}, u32[]{:S(2)}) %collective-permute-start.13) | collective-permute-done | bytes 524320 | tf_op jit(solution)/shard_map/ppermute | solution.py:82
  92.3 3.4 %partial_ladder.7 = f32[4,64,2048]{2,1,0:T(8,128)S(1)} custom-call(s32[2]{0:T(128)S(1)} %pad_add_fusion.place, s32[24]{0:T(128)S(1)} %copy-done.11, s32[8,2]{1,0:T(8,128)S(1)} %copy.19.product, s32[8,2]{1,0:T(8,128)S(1)} %copy.20.summed, bf16[128,2048]{1,0:T(8,128)(2,1)S(1)} %broadcast_select_fusion.refs_0_.here, ...), custom_call_target="tpu_custom_call" | custom-call | flops 1000 | bytes 1000 | tf_op jit(solution)/shard_map/partial_ladder/pallas_call | solution.py:145
  96.0 0.6 collective-permute-start.14
  97.1 2.5 %collective-permute-start.22 = (f16[64,2048]{1,0:T(8,128)(2,1)S(1)}, f16[64,2048]{1,0:T(8,128)(2,1)S(1)}, u32[]{:S(2)}, u32[]{:S(2)}) collective-permute-start(f16[64,2048]{1,0:T(8,128)(2,1)S(1)} %get-tuple-element.15), channel_id=1, source_target_pairs={{0,16},{1,17},{2,18},{3,19},{4,20},{5,21},{6,22},{7,23},{8,24},{9,... | collective-permute-start | bytes 786440 | tf_op jit(solution)/shard_map/ppermute | solution.py:82
  99.5 5.3 %collective-permute-done.14 = f16[64,2048]{1,0:T(8,128)(2,1)S(1)} collective-permute-done((f16[64,2048]{1,0:T(8,128)(2,1)S(1)}, f16[64,2048]{1,0:T(8,128)(2,1)S(1)}, u32[]{:S(2)}, u32[]{:S(2)}) %collective-permute-start.14) | collective-permute-done | bytes 262176 | tf_op jit(solution)/shard_map/ppermute | solution.py:82
  105.4 0.6 collective-permute-start.16
  106.1 1.3 collective-permute-start.17
  107.6 0.7 collective-permute-start.18
  108.7 8.3 %collective-permute-done.21 = f16[64,2048]{1,0:T(8,128)(2,1)S(1)} collective-permute-done((f16[64,2048]{1,0:T(8,128)(2,1)S(1)}, f16[64,2048]{1,0:T(8,128)(2,1)S(1)}, u32[]{:S(2)}, u32[]{:S(2)}) %collective-permute-start.21) | collective-permute-done | bytes 262176 | tf_op jit(solution)/shard_map/ppermute | solution.py:82
  117.0 3.5 %collective-permute-start.19 = (f16[3,64,2048]{2,1,0:T(8,128)(2,1)S(1)}, f16[3,64,2048]{2,1,0:T(8,128)(2,1)S(1)}, u32[]{:S(2)}, u32[]{:S(2)}) collective-permute-start(f16[3,64,2048]{2,1,0:T(8,128)(2,1)S(1)} %slice.66), channel_id=1, source_target_pairs={{0,2},{4,6},{8,10},{12,14},{19,17},{23,21},{27,25},{31,29}} | collective-permute-start | bytes 2359304 | tf_op jit(solution)/shard_map/ppermute | solution.py:82
  120.4 2.1 %collective-permute-done.22 = f16[64,2048]{1,0:T(8,128)(2,1)S(1)} collective-permute-done((f16[64,2048]{1,0:T(8,128)(2,1)S(1)}, f16[64,2048]{1,0:T(8,128)(2,1)S(1)}, u32[]{:S(2)}, u32[]{:S(2)}) %collective-permute-start.22) | collective-permute-done | bytes 262176 | tf_op jit(solution)/shard_map/ppermute | solution.py:82
  122.5 0.7 collective-permute-start.20
  123.5 14.7 %collective-permute-done.23 = f16[64,2048]{1,0:T(8,128)(2,1)S(1)} collective-permute-done((f16[64,2048]{1,0:T(8,128)(2,1)S(1)}, f16[64,2048]{1,0:T(8,128)(2,1)S(1)}, u32[]{:S(2)}, u32[]{:S(2)}) %collective-permute-start.23) | collective-permute-done | bytes 262176 | tf_op jit(solution)/shard_map/ppermute | solution.py:82
  138.2 0.6 turn.3.refs_9_
  138.9 0.6 turn.4.refs_10_
  140.0 11.4 %collective-permute-done.24 = f16[64,2048]{1,0:T(8,128)(2,1)S(1)} collective-permute-done((f16[64,2048]{1,0:T(8,128)(2,1)S(1)}, f16[64,2048]{1,0:T(8,128)(2,1)S(1)}, u32[]{:S(2)}, u32[]{:S(2)}) %collective-permute-start.24) | collective-permute-done | bytes 262176 | tf_op jit(solution)/shard_map/ppermute | solution.py:82
  151.5 0.6 add_convert_fusion.refs_8_
  152.3 3.2 %finish.1 = bf16[256,2048]{1,0:T(8,128)(2,1)} custom-call(s32[2]{0:T(128)S(1)} %pad_add_fusion.place, f32[4,64,2048]{2,1,0:T(8,128)S(1)} %bitcast.50, f32[4,64,2048]{2,1,0:T(8,128)S(1)} %bitcast.53, f32[4,64,2048]{2,1,0:T(8,128)S(1)} %bitcast.56, f32[4,64,2048]{2,1,0:T(8,128)S(1)} %bitcast.58, f32[64,2048]{1,0:T(8,128)S(1)} %get-tuple-element.18.refs_4_, ...), custom_call_target="tpu_custom_call" | custom-call | tf_op jit(solution)/shard_map/finish/pallas_call | solution.py:220
  (69 shorter events, 4.6 us)
Async XLA Ops:
  0.0 15.2 %collective-permute-start.1 = (bf16[128,2048]{1,0:T(8,128)(2,1)}, bf16[128,2048]{1,0:T(8,128)(2,1)S(1)}, u32[]{:S(2)}, u32[]{:S(2)}) collective-permute-start(bf16[128,2048]{1,0:T(8,128)(2,1)} %here.1), channel_id=1, source_target_pairs={{0,8},{1,9},{2,10},{3,11},{4,12},{5,13},{6,14},{7,15},{8,0},{9,1},... | collective-permute-start | bytes 1572872 | tf_op jit(solution)/shard_map/ppermute | solution.py:82
  3.0 13.6 %collective-permute-start = (bf16[128,2048]{1,0:T(8,128)(2,1)}, bf16[128,2048]{1,0:T(8,128)(2,1)S(1)}, u32[]{:S(2)}, u32[]{:S(2)}) collective-permute-start(bf16[128,2048]{1,0:T(8,128)(2,1)} %here.1), channel_id=1, source_target_pairs={{0,4},{1,5},{2,6},{3,7},{4,0},{5,1},{6,2},{7,3},{8,12},{9,13},{10,... | collective-permute-start | bytes 1572872 | tf_op jit(solution)/shard_map/ppermute | solution.py:82
  4.5 12.9 %collective-permute-start.2 = (bf16[128,2048]{1,0:T(8,128)(2,1)}, bf16[128,2048]{1,0:T(8,128)(2,1)S(1)}, u32[]{:S(2)}, u32[]{:S(2)}) collective-permute-start(bf16[128,2048]{1,0:T(8,128)(2,1)} %here.1), channel_id=1, source_target_pairs={{8,16},{9,17},{10,18},{11,19},{12,20},{13,21},{14,22},{15,23},{16,... | collective-permute-start | bytes 1572872 | tf_op jit(solution)/shard_map/ppermute | solution.py:82
  16.6 0.8 copy-start.6
  17.4 3.4 %copy-start = (bf16[2048,2048]{1,0:T(8,128)(2,1)S(1)}, bf16[2048,2048]{1,0:T(8,128)(2,1)}, u32[]{:S(2)}) copy-start(bf16[2048,2048]{1,0:T(8,128)(2,1)} %integrals.7) | copy-start | bytes 25165828
  20.8 0.8 copy-start.3
  21.6 1.0 copy-start.5
  22.6 1.0 copy-start.7
  23.6 0.7 copy-start.10
  27.8 19.0 %collective-permute-start.3 = (f32[4,64,2048]{2,1,0:T(8,128)S(1)}, f32[4,64,2048]{2,1,0:T(8,128)}, u32[]{:S(2)}, u32[]{:S(2)}) collective-permute-start(f32[4,64,2048]{2,1,0:T(8,128)S(1)} %partial_ladder.4), channel_id=1, source_target_pairs={{0,1},{1,0},{2,3},{3,2},{4,5},{5,4},{6,7},{7,6},{8,9},{9,8},{10,11... | collective-permute-start | bytes 6291464 | tf_op jit(solution)/shard_map/ppermute | solution.py:82
  27.8 17.7 %collective-permute-start.5 = (bf16[128,2048]{1,0:T(8,128)(2,1)S(1)}, bf16[128,2048]{1,0:T(8,128)(2,1)}, u32[]{:S(2)}, u32[]{:S(2)}) collective-permute-start(bf16[128,2048]{1,0:T(8,128)(2,1)S(1)} %collective-permute-done.2.refs_1_), channel_id=1, source_target_pairs={{8,0},{9,1},{10,2},{11,3},{12,4},{13,5},{14,6},{15,7},{16,24},{17,... | collective-permute-start | bytes 1572872 | tf_op jit(solution)/shard_map/ppermute | solution.py:82
  29.2 19.6 %collective-permute-start.6 = (bf16[128,2048]{1,0:T(8,128)(2,1)S(1)}, bf16[128,2048]{1,0:T(8,128)(2,1)S(1)}, u32[]{:S(2)}, u32[]{:S(2)}) collective-permute-start(bf16[128,2048]{1,0:T(8,128)(2,1)S(1)} %collective-permute-done.1.refs_0_.here), channel_id=1, source_target_pairs={{8,16},{9,17},{10,18},{11,19},{12,20},{13,21},{14,22},{15,23},{16,... | collective-permute-start | bytes 1572872 | tf_op jit(solution)/shard_map/ppermute | solution.py:82
  29.9 18.9 %collective-permute-start.4 = (bf16[128,2048]{1,0:T(8,128)(2,1)S(1)}, bf16[128,2048]{1,0:T(8,128)(2,1)S(1)}, u32[]{:S(2)}, u32[]{:S(2)}) collective-permute-start(bf16[128,2048]{1,0:T(8,128)(2,1)S(1)} %collective-permute-done.1.refs_0_.here), channel_id=1, source_target_pairs={{0,4},{1,5},{2,6},{3,7},{4,0},{5,1},{6,2},{7,3},{8,12},{9,13},{10,... | collective-permute-start | bytes 1572872 | tf_op jit(solution)/shard_map/ppermute | solution.py:82
  45.5 27.4 %slice-start = ((s8[8388608]{0:T(1024)(128)(4,1)}), s8[4194304]{0:T(1024)(128)(4,1)S(1)}, s32[]{:S(2)}) async-start(s8[8388608]{0:T(1024)(128)(4,1)} %bitcast.46), calls=%async_computation | async-start | bytes 8388608
  46.8 2.0 %copy-start.4 = (bf16[128,128]{1,0:T(8,128)(2,1)S(1)}, bf16[128,128]{1,0:T(8,128)(2,1)}, u32[]{:S(2)}) copy-start(bf16[128,128]{1,0:T(8,128)(2,1)} %constant.33.clone.block_order) | copy-start | bytes 98308
  46.8 2.0 %copy-start.11 = (s32[24]{0:T(128)S(1)}, s32[24]{0:T(128)}, u32[]{:S(2)}) copy-start(s32[24]{0:T(128)} %irrep.7) | copy-start | bytes 292
  48.8 3.4 %copy-start.1 = (bf16[2048,2048]{1,0:T(8,128)(2,1)S(1)}, bf16[2048,2048]{1,0:T(8,128)(2,1)}, u32[]{:S(2)}) copy-start(bf16[2048,2048]{1,0:T(8,128)(2,1)} %integrals.7) | copy-start | bytes 25165828
  52.2 20.7 %slice-start.1 = ((s8[8388608]{0:T(1024)(128)(4,1)}), s8[4194304]{0:T(1024)(128)(4,1)S(1)}, s32[]{:S(2)}) async-start(s8[8388608]{0:T(1024)(128)(4,1)} %bitcast.46), calls=%async_computation.1 | async-start | bytes 8388608
  55.7 16.9 %collective-permute-start.8 = (f32[4,64,2048]{2,1,0:T(8,128)S(1)}, f32[4,64,2048]{2,1,0:T(8,128)S(1)}, u32[]{:S(2)}, u32[]{:S(2)}) collective-permute-start(f32[4,64,2048]{2,1,0:T(8,128)S(1)} %partial_ladder.5), channel_id=1, source_target_pairs={{0,1},{1,0},{2,3},{3,2},{4,5},{5,4},{6,7},{7,6},{8,9},{9,8},{10,11... | collective-permute-start | bytes 6291464 | tf_op jit(solution)/shard_map/ppermute | solution.py:82
  55.7 17.2 %collective-permute-start.9 = (bf16[128,2048]{1,0:T(8,128)(2,1)S(1)}, bf16[128,2048]{1,0:T(8,128)(2,1)S(1)}, u32[]{:S(2)}, u32[]{:S(2)}) collective-permute-start(bf16[128,2048]{1,0:T(8,128)(2,1)S(1)} %broadcast_select_fusion.1.refs_0_.here), channel_id=1, source_target_pairs={{0,4},{1,5},{2,6},{3,7},{4,0},{5,1},{6,2},{7,3},{8,12},{9,13},{10,... | collective-permute-start | bytes 1572872 | tf_op jit(solution)/shard_map/ppermute | solution.py:82
  56.3 16.1 %collective-permute-start.10 = (bf16[128,2048]{1,0:T(8,128)(2,1)S(1)}, bf16[128,2048]{1,0:T(8,128)(2,1)S(1)}, u32[]{:S(2)}, u32[]{:S(2)}) collective-permute-start(bf16[128,2048]{1,0:T(8,128)(2,1)S(1)} %collective-permute-done.6.refs_1_), channel_id=1, source_target_pairs={{8,0},{9,1},{10,2},{11,3},{12,4},{13,5},{14,6},{15,7},{16,24},{17,... | collective-permute-start | bytes 1572872 | tf_op jit(solution)/shard_map/ppermute | solution.py:82
  58.0 14.5 %collective-permute-start.7 = (f16[64,2048]{1,0:T(8,128)(2,1)S(1)}, f16[64,2048]{1,0:T(8,128)(2,1)S(1)}, u32[]{:S(2)}, u32[]{:S(2)}) collective-permute-start(f16[64,2048]{1,0:T(8,128)(2,1)S(1)} %slice_bitcast_fusion.7), channel_id=1, source_target_pairs={{0,2},{1,3},{2,0},{3,1},{4,6},{5,7},{6,4},{7,5},{8,10},{9,11},{10,... | collective-permute-start | bytes 786440 | tf_op jit(solution)/shard_map/ppermute | solution.py:82
  76.4 9.1 %collective-permute-start.12 = (f32[4,64,2048]{2,1,0:T(8,128)S(1)}, f32[4,64,2048]{2,1,0:T(8,128)S(1)}, u32[]{:S(2)}, u32[]{:S(2)}) collective-permute-start(f32[4,64,2048]{2,1,0:T(8,128)S(1)} %partial_ladder.6), channel_id=1, source_target_pairs={{0,1},{1,0},{2,3},{3,2},{4,5},{5,4},{6,7},{7,6},{8,9},{9,8},{10,11... | collective-permute-start | bytes 6291464 | tf_op jit(solution)/shard_map/ppermute | solution.py:82
  76.7 8.8 %collective-permute-start.11 = (f16[64,2048]{1,0:T(8,128)(2,1)S(1)}, f16[64,2048]{1,0:T(8,128)(2,1)S(1)}, u32[]{:S(2)}, u32[]{:S(2)}) collective-permute-start(f16[64,2048]{1,0:T(8,128)(2,1)S(1)} %slice_bitcast_fusion.6), channel_id=1, source_target_pairs={{0,2},{1,3},{2,0},{3,1},{4,6},{5,7},{6,4},{7,5},{8,10},{9,11},{10,... | collective-permute-start | bytes 786440 | tf_op jit(solution)/shard_map/ppermute | solution.py:82
  78.3 14.0 %collective-permute-start.13 = (bf16[128,2048]{1,0:T(8,128)(2,1)S(1)}, bf16[128,2048]{1,0:T(8,128)(2,1)S(1)}, u32[]{:S(2)}, u32[]{:S(2)}) collective-permute-start(bf16[128,2048]{1,0:T(8,128)(2,1)S(1)} %broadcast_select_fusion.refs_0_.here), channel_id=1, source_target_pairs={{0,4},{1,5},{2,6},{3,7},{4,0},{5,1},{6,2},{7,3},{8,12},{9,13},{10,... | collective-permute-start | bytes 1572872 | tf_op jit(solution)/shard_map/ppermute | solution.py:82
  95.8 9.1 %collective-permute-start.15 = (f32[4,64,2048]{2,1,0:T(8,128)S(1)}, f32[4,64,2048]{2,1,0:T(8,128)S(1)}, u32[]{:S(2)}, u32[]{:S(2)}) collective-permute-start(f32[4,64,2048]{2,1,0:T(8,128)S(1)} %partial_ladder.7), channel_id=1, source_target_pairs={{0,1},{1,0},{2,3},{3,2},{4,5},{5,4},{6,7},{7,6},{8,9},{9,8},{10,11... | collective-permute-start | bytes 6291464 | tf_op jit(solution)/shard_map/ppermute | solution.py:82
  96.0 8.8 %collective-permute-start.14 = (f16[64,2048]{1,0:T(8,128)(2,1)S(1)}, f16[64,2048]{1,0:T(8,128)(2,1)S(1)}, u32[]{:S(2)}, u32[]{:S(2)}) collective-permute-start(f16[64,2048]{1,0:T(8,128)(2,1)S(1)} %slice_bitcast_fusion.5), channel_id=1, source_target_pairs={{0,2},{1,3},{2,0},{3,1},{4,6},{5,7},{6,4},{7,5},{8,10},{9,11},{10,... | collective-permute-start | bytes 786440 | tf_op jit(solution)/shard_map/ppermute | solution.py:82
  96.6 20.4 %collective-permute-start.21 = (f16[64,2048]{1,0:T(8,128)(2,1)S(1)}, f16[64,2048]{1,0:T(8,128)(2,1)S(1)}, u32[]{:S(2)}, u32[]{:S(2)}) collective-permute-start(f16[64,2048]{1,0:T(8,128)(2,1)S(1)} %get-tuple-element.17), channel_id=1, source_target_pairs={{0,16},{1,17},{2,18},{3,19},{4,20},{5,21},{6,22},{7,23},{8,24},{9,... | collective-permute-start | bytes 786440 | tf_op jit(solution)/shard_map/ppermute | solution.py:82
  97.1 25.5 %collective-permute-start.22 = (f16[64,2048]{1,0:T(8,128)(2,1)S(1)}, f16[64,2048]{1,0:T(8,128)(2,1)S(1)}, u32[]{:S(2)}, u32[]{:S(2)}) collective-permute-start(f16[64,2048]{1,0:T(8,128)(2,1)S(1)} %get-tuple-element.15), channel_id=1, source_target_pairs={{0,16},{1,17},{2,18},{3,19},{4,20},{5,21},{6,22},{7,23},{8,24},{9,... | collective-permute-start | bytes 786440 | tf_op jit(solution)/shard_map/ppermute | solution.py:82
  105.4 17.8 %collective-permute-start.16 = (f16[64,2048]{1,0:T(8,128)(2,1)S(1)}, f16[64,2048]{1,0:T(8,128)(2,1)S(1)}, u32[]{:S(2)}, u32[]{:S(2)}) collective-permute-start(f16[64,2048]{1,0:T(8,128)(2,1)S(1)} %slice_bitcast_fusion.4), channel_id=1, source_target_pairs={{0,2},{1,3},{2,0},{3,1},{4,6},{5,7},{6,4},{7,5},{8,10},{9,11},{10,... | collective-permute-start | bytes 786440 | tf_op jit(solution)/shard_map/ppermute | solution.py:82
  106.1 45.3 %collective-permute-start.17 = (f16[3,64,2048]{2,1,0:T(8,128)(2,1)S(1)}, f16[3,64,2048]{2,1,0:T(8,128)(2,1)S(1)}, u32[]{:S(2)}, u32[]{:S(2)}) collective-permute-start(f16[3,64,2048]{2,1,0:T(8,128)(2,1)S(1)} %slice.64), channel_id=1, source_target_pairs={{2,0},{6,4},{11,9},{15,13},{16,18},{20,22},{25,27},{29,31}} | collective-permute-start | bytes 2359304 | tf_op jit(solution)/shard_map/ppermute | solution.py:82
  107.6 43.8 %collective-permute-start.18 = (f16[3,64,2048]{2,1,0:T(8,128)(2,1)S(1)}, f16[3,64,2048]{2,1,0:T(8,128)(2,1)S(1)}, u32[]{:S(2)}, u32[]{:S(2)}) collective-permute-start(f16[3,64,2048]{2,1,0:T(8,128)(2,1)S(1)} %slice.65), channel_id=1, source_target_pairs={{3,1},{7,5},{10,8},{14,12},{17,19},{21,23},{24,26},{28,30}} | collective-permute-start | bytes 2359304 | tf_op jit(solution)/shard_map/ppermute | solution.py:82
  108.5 29.7 %copy-start.2 = (bf16[256,256]{1,0:T(8,128)(2,1)S(1)}, bf16[256,256]{1,0:T(8,128)(2,1)}, u32[]{:S(2)}) copy-start(bf16[256,256]{1,0:T(8,128)(2,1)} %constant.35.clone.swap.refs_15_) | copy-start | bytes 393220
  108.5 29.7 %copy-start.8 = (bf16[64,64]{1,0:T(8,128)(2,1)S(1)}, bf16[64,64]{1,0:T(8,128)(2,1)}, u32[]{:S(2)}) copy-start(bf16[64,64]{1,0:T(8,128)(2,1)} %constant.34.clone.align.refs_13_) | copy-start | bytes 24580
  117.0 34.5 %collective-permute-start.19 = (f16[3,64,2048]{2,1,0:T(8,128)(2,1)S(1)}, f16[3,64,2048]{2,1,0:T(8,128)(2,1)S(1)}, u32[]{:S(2)}, u32[]{:S(2)}) collective-permute-start(f16[3,64,2048]{2,1,0:T(8,128)(2,1)S(1)} %slice.66), channel_id=1, source_target_pairs={{0,2},{4,6},{8,10},{12,14},{19,17},{23,21},{27,25},{31,29}} | collective-permute-start | bytes 2359304 | tf_op jit(solution)/shard_map/ppermute | solution.py:82
  122.5 29.0 %collective-permute-start.20 = (f16[3,64,2048]{2,1,0:T(8,128)(2,1)S(1)}, f16[3,64,2048]{2,1,0:T(8,128)(2,1)S(1)}, u32[]{:S(2)}, u32[]{:S(2)}) collective-permute-start(f16[3,64,2048]{2,1,0:T(8,128)(2,1)S(1)} %slice.67), channel_id=1, source_target_pairs={{1,3},{5,7},{9,11},{13,15},{18,16},{22,20},{26,24},{30,28}} | collective-permute-start | bytes 2359304 | tf_op jit(solution)/shard_map/ppermute | solution.py:82
  123.2 14.9 %collective-permute-start.23 = (f16[64,2048]{1,0:T(8,128)(2,1)S(1)}, f16[64,2048]{1,0:T(8,128)(2,1)S(1)}, u32[]{:S(2)}, u32[]{:S(2)}) collective-permute-start(f16[64,2048]{1,0:T(8,128)(2,1)S(1)} %get-tuple-element.13), channel_id=1, source_target_pairs={{0,16},{1,17},{2,18},{3,19},{4,20},{5,21},{6,22},{7,23},{8,24},{9,... | collective-permute-start | bytes 786440 | tf_op jit(solution)/shard_map/ppermute | solution.py:82
  138.2 13.2 %collective-permute-start.24 = (f16[64,2048]{1,0:T(8,128)(2,1)S(1)}, f16[64,2048]{1,0:T(8,128)(2,1)S(1)}, u32[]{:S(2)}, u32[]{:S(2)}) collective-permute-start(f16[64,2048]{1,0:T(8,128)(2,1)S(1)} %get-tuple-element.11), channel_id=1, source_target_pairs={{0,16},{1,17},{2,18},{3,19},{4,20},{5,21},{6,22},{7,23},{8,24},{9,... | collective-permute-start | bytes 786440 | tf_op jit(solution)/shard_map/ppermute | solution.py:82
  151.4 0.9 copy-start.9

commit v2 on v0

v2 whole, which is shorter than its diff:
```python
import functools

import jax
import jax.numpy as jnp
import numpy as np
from jax import lax
from jax.experimental import pallas as pl
from jax.experimental.pallas import tpu as pltpu
from jax.sharding import PartitionSpec as P

TS = 16
TP = TS * TS
OT = 32
WIRE = jnp.float16


def from_partner(value, axis, distance):
    mask = 2**distance
    pairs = [(source, source ^ mask) for source in range(lax.axis_size(axis))]
    return lax.ppermute(value, axis, pairs)


def pair_symmetry(tile_irrep, pairs):
    return jnp.bitwise_xor(tile_irrep[pairs[:, 0]], tile_irrep[pairs[:, 1]])


def plain(amplitudes, integrals, tile_irrep, product_pairs, summed_pairs):
    product_sym = pair_symmetry(tile_irrep, product_pairs)
    summed_sym = pair_symmetry(tile_irrep, summed_pairs)
    allowed = summed_sym[:, None] == product_sym[None, :]
    summed_count = summed_pairs.shape[0]
    product_count = product_pairs.shape[0]
    keep = allowed.astype(integrals.dtype)
    masked = (
        integrals.reshape(summed_count, TP, product_count, TP)
        * keep[:, None, :, None]
    ).reshape(integrals.shape)
    half_bit = lax.axis_size("row").bit_length() - 2
    ladder = jnp.dot(
        lax.all_gather(amplitudes, "row", axis=0, tiled=True),
        masked,
        preferred_element_type=jnp.float32,
    )
    partner = from_partner(ladder, "row", half_bit)
    partner = partner.reshape(OT, OT, product_count, TS, TS)
    partner = jnp.transpose(partner, (1, 0, 2, 4, 3)).reshape(ladder.shape)
    summed = lax.psum_scatter(ladder + partner, "col", scatter_dimension=0, tiled=True)
    return summed.astype(jnp.bfloat16)


NZ, NX, NY, NC = 4, 2, 2, 2
ROWS = 128
PART = 64
OWNED = 256
WIDTH = 2048
PANELS = WIDTH // TP
LANES = 128
PLANES = ((0, 1, 2, 3), (1, 0, 2, 3), (2, 3, 1, 0), (3, 2, 1, 0))
PART_OF = (1, 2, 0, 3)


def params(mib):
    return pltpu.CompilerParams(vmem_limit_bytes=mib * 2**20)


def light():
    return pl.CostEstimate(flops=1000, bytes_accessed=1000, transcendentals=0)


def selection(extents, axes):
    n = int(np.prod(extents))
    row = lax.broadcasted_iota(jnp.int32, (n, n), 0)
    column = lax.broadcasted_iota(jnp.int32, (n, n), 1)
    strides = [int(np.prod(extents[axis + 1 :])) for axis in range(len(extents))]
    source, below = jnp.zeros_like(row), 1
    for axis in reversed(axes):
        source += row // below % extents[axis] * strides[axis]
        below *= extents[axis]
    return jnp.where(source == column, 1.0, 0.0).astype(jnp.bfloat16)


def block_order():
    return selection((4, 32), (1, 0))


def align_order():
    return selection((2, 2, 4, 4), (1, 0, 3, 2))


def natural_order():
    return selection((4, 2, 8, 4), (1, 3, 0, 2))


def swap_order():
    return selection((TS, TS), (1, 0))


def send(value, target):
    pairs = []
    for n, (z, x, y, k) in enumerate(np.ndindex(NZ, NX, NY, NC)):
        to = target(z, x, y, k)
        if to is not None:
            pairs.append((n, int(np.ravel_multi_index(to, (NZ, NX, NY, NC)))))
    return lax.ppermute(value, ("row", "col"), pairs)


def along_z(value, moves):
    return send(value, lambda z, x, y, k: (moves[z], x, y, k) if z in moves else None)


def across_x(value, planes=range(NZ)):
    return send(value, lambda z, x, y, k: (z, 1 - x, y, k) if z in planes else None)


def across_y(value):
    return send(value, lambda z, x, y, k: (z, x, 1 - y, k))


def across_core(value):
    return send(value, lambda z, x, y, k: (z, x, y, 1 - k))


def to_partner(value):
    return send(value, lambda z, x, y, k: (z ^ 2, x, y, k))


def to_owner(value, steps):
    def target(z, x, y, k):
        owned = [divmod(PLANES[z][step], NC) for step in steps]
        return (z, x, 1 - y, k) if (1 - y, k) in owned else None

    return send(value, target)


def matmul(a, b):
    return jnp.dot(a, b, preferred_element_type=jnp.float32)


def lookup(table, index):
    value = table[0]
    for n in range(1, len(table)):
        value = jnp.where(index == n, table[n], value)
    return value


def ladder_kernel(place, irrep, product, summed, here, beside, integrals, out, rows):
    x, col = place[0] % NX, place[1]
    order = block_order()
    for block, at in ((here, x), (beside, 1 - x)):
        start = pl.multiple_of(at * ROWS, ROWS)
        rows[pl.ds(start, ROWS), :] = matmul(order, block[...]).astype(jnp.bfloat16)
    for p in range(PANELS):
        wanted = irrep[product[p, 0]] ^ irrep[product[p, 1]]
        kept = []
        for q in range(WIDTH // TP):
            same = (irrep[summed[q, 0]] ^ irrep[summed[q, 1]]) == wanted
            value = rows[:, q * TP : (q + 1) * TP]
            kept.append(jnp.where(same, value, jnp.zeros_like(value)))
        cut = slice(p * TP, (p + 1) * TP)
        total = matmul(jnp.concatenate(kept, axis=1), integrals[:, cut])
        for to in range(4):
            for at in range(2):
                start = at * ROWS + to * 32
                out[lookup(PART_OF, to ^ col), at * 32 : (at + 1) * 32, cut] = total[start : start + 32, :]


def partial_ladder(tables, integrals, here, beside):
    vmem = pl.BlockSpec(memory_space=pltpu.VMEM)
    return pl.pallas_call(
        ladder_kernel,
        in_specs=[pl.BlockSpec(memory_space=pltpu.SMEM)] * 4 + [vmem] * 3,
        out_specs=vmem,
        scratch_shapes=[pltpu.VMEM((2 * ROWS, WIDTH), jnp.bfloat16)],
        out_shape=jax.ShapeDtypeStruct((4, PART, WIDTH), jnp.float32),
        compiler_params=params(14),
        cost_estimate=light(),
        name="partial_ladder",
    )(*tables, here, beside, integrals)


def turn(arrived):
    high = arrived.astype(jnp.bfloat16)
    low = (arrived - high.astype(jnp.float32)).astype(jnp.bfloat16)
    both = jnp.concatenate([high, low], axis=0)
    swap, align = swap_order(), align_order()
    cuts = [both[:, p * TP : (p + 1) * TP] for p in range(PANELS)]
    both = jnp.concatenate([matmul(cut, swap).astype(jnp.bfloat16) for cut in cuts], axis=1)
    return matmul(align, both[:PART]) + matmul(align, both[PART:])


def turn_kernel(arrived, out):
    out[...] = turn(decoded(arrived))


def turned(arrived):
    return pl.pallas_call(
        turn_kernel,
        out_shape=jax.ShapeDtypeStruct((PART, WIDTH), jnp.float32),
        compiler_params=params(12),
        cost_estimate=pl.CostEstimate(flops=2 * 10**9, bytes_accessed=10**6, transcendentals=0),
        name="turn",
    )(arrived)


def planes_of(side):
    return [lookup([planes[step] for planes in PLANES], side) for step in range(4)]


def sort_own_kernel(step, place, pair, mine, *refs):
    own, sems = refs[-2:]

    @pl.when(planes_of(place[0] // NX)[step] == place[1])
    def _():
        copies = [
            pltpu.make_async_copy(pair.at[0], own.at[0], sems.at[0]),
            pltpu.make_async_copy(mine, own.at[1], sems.at[1]),
            pltpu.make_async_copy(pair.at[pl.ds(2, 2)], own.at[pl.ds(2, 2)], sems.at[2]),
        ]
        for copy in copies:
            copy.start()
        for copy in copies:
            copy.wait()


def sort_owed_kernel(step, place, pair, *refs):
    owed, buffer, sem = refs[-3:]

    @pl.when(planes_of(place[0] // NX)[step] == place[1] ^ 2)
    def _():
        put_coded(buffer, pair[1:])
        copy = pltpu.make_async_copy(buffer, owed, sem)
        copy.start()
        copy.wait()


def sort(kernel, shape, scratch, place, step, values, before):
    vmem = pl.BlockSpec(memory_space=pltpu.VMEM)
    hbm = pl.BlockSpec(memory_space=pl.ANY)
    before = [] if before is None else [before]
    return pl.pallas_call(
        functools.partial(kernel, step),
        in_specs=[pl.BlockSpec(memory_space=pltpu.SMEM)] + [vmem] * len(values) + [hbm] * len(before),
        out_specs=hbm,
        out_shape=jax.ShapeDtypeStruct(shape, jnp.float32),
        scratch_shapes=scratch,
        input_output_aliases={1 + len(values): 0} if before else {},
        compiler_params=params(10),
        cost_estimate=light(),
        name="sort",
    )(place, *values, *before)


def sort_own(place, step, pair, mine, before=None):
    return sort(sort_own_kernel, (4, PART, WIDTH), [pltpu.SemaphoreType.DMA((3,))], place, step, (pair, mine), before)


def sort_owed(place, step, pair, before=None):
    shape = (3, PART, WIDTH + LANES)
    scratch = [pltpu.VMEM(shape, jnp.float32), pltpu.SemaphoreType.DMA]
    return sort(sort_owed_kernel, shape, scratch, place, step, (pair,), before)


def gather_kernel(place, own, rest, out):
    for part, (distance, came) in enumerate(((2, 0), (0, None), (1, 2), (3, 1))):
        value = own[part]
        if came is not None:
            value += decoded(rest.at[came])
        out[distance ^ place[1]] = value


def merge_kernel(place, sums, turned0, turned1, turned2, out):
    out[...] = sums[...]
    for step, ref in enumerate((turned0, turned1, turned2)):
        plane = planes_of(place[0] // NX ^ 2)[step]
        out[plane] = out[plane] + ref[...]


def gather(kernel, place, *values):
    vmem = pl.BlockSpec(memory_space=pltpu.VMEM)
    return pl.pallas_call(
        kernel,
        in_specs=[pl.BlockSpec(memory_space=pltpu.SMEM)] + [vmem] * len(values),
        out_specs=vmem,
        out_shape=jax.ShapeDtypeStruct((4, PART, WIDTH), jnp.float32),
        compiler_params=params(12),
        cost_estimate=light(),
        name="gather",
    )(place, *values)


def finish_kernel(place, sums, last, out, total):
    total[...] = sums[...].astype(jnp.bfloat16)
    plane = planes_of(place[0] // NX ^ 2)[3]
    total[plane] = (sums[plane] + turn(decoded(last))).astype(jnp.bfloat16)
    natural = natural_order()
    value = total[...].reshape(OWNED, WIDTH)
    for p in range(PANELS):
        cut = slice(p * TP, (p + 1) * TP)
        out[:, cut] = matmul(natural, value[:, cut]).astype(jnp.bfloat16)


def finish(place, sums, last):
    vmem = pl.BlockSpec(memory_space=pltpu.VMEM)
    return pl.pallas_call(
        finish_kernel,
        in_specs=[pl.BlockSpec(memory_space=pltpu.SMEM), vmem, vmem],
        out_specs=vmem,
        out_shape=jax.ShapeDtypeStruct((OWNED, WIDTH), jnp.bfloat16),
        scratch_shapes=[pltpu.VMEM((4, PART, WIDTH), jnp.bfloat16)],
        compiler_params=params(12),
        cost_estimate=light(),
        name="finish",
    )(place, sums, last)


def coded(value):
    largest = value
    while largest.ndim > 0 and largest.shape != (1,) * value.ndim:
        axis = next(n for n, size in enumerate(largest.shape) if size > 1)
        largest = jnp.max(jnp.abs(largest), axis=axis, keepdims=True)
    power = jnp.ceil(jnp.log2(jnp.maximum(largest, 1e-30)))
    scaled = value * jnp.exp2(7 - power)
    return scaled * jnp.abs(scaled), jnp.broadcast_to(power, (*value.shape[:-1], LANES))


def put_coded(ref, value):
    ref[..., :WIDTH], ref[..., WIDTH:] = coded(value)


def decoded(ref):
    value = ref[..., :WIDTH]
    power = ref[..., WIDTH : WIDTH + 1]
    root = jnp.sqrt(jnp.abs(value)) * jnp.exp2(power - 7)
    return jnp.where(value < 0, -root, root)


def wire(value):
    return value.astype(WIRE)


def unwire(value):
    return value.astype(jnp.float32)


def small_kernel(kernel, shapes, mib, name):
    vmem = pl.BlockSpec(memory_space=pltpu.VMEM)
    shapes = [jax.ShapeDtypeStruct(shape, jnp.float32) for shape in shapes]
    return pl.pallas_call(
        kernel,
        out_specs=[vmem] * len(shapes),
        out_shape=shapes,
        compiler_params=params(mib),
        cost_estimate=light(),
        name=name,
    )


def add_cores_kernel(part, sibling, pair, out):
    for n in (0, 1, 2, 3):
        pair[n] = part[n] + sibling[3 - n]
    put_coded(out, pair[0])


def add_cores(part):
    call = small_kernel(add_cores_kernel, [(4, PART, WIDTH), (PART, WIDTH + LANES)], 12, "add_cores")
    return call(part, across_core(part))


def add_chips_kernel(pair, over, mine, out):
    mine[...] = pair[1] + decoded(over)
    put_coded(out, mine[...])


def add_chips(pair, over):
    call = small_kernel(add_chips_kernel, [(PART, WIDTH), (PART, WIDTH + LANES)], 8, "add_chips")
    return call(pair, unwire(over))


def together(*values):
    return lax.optimization_barrier(values)


def on_device(amplitudes, integrals, tile_irrep, product_pairs, summed_pairs):
    row, col = lax.axis_index("row"), lax.axis_index("col")
    z = row // NX
    place = jnp.stack([row, col]).astype(jnp.int32)
    tables = (place, tile_irrep, product_pairs, summed_pairs)
    inner = (z == 1) | (z == 2)
    outward = {0: 1, 1: 0, 2: 3, 3: 2}
    inward = {1: 2, 2: 1}

    here0 = amplitudes
    beside0 = across_x(here0)
    here1 = along_z(here0, outward)
    middle = along_z(here0, inward)
    beside0, here1, middle = together(beside0, here1, middle)

    beside1 = across_x(here1)
    crossed = along_z(here1, inward)
    here2 = along_z(middle, outward)
    part0 = partial_ladder(tables, integrals, here0, beside0)
    beside1, crossed, here2, part0 = together(beside1, crossed, here2, part0)
    here2 = jnp.where(inner, middle, here2)

    beside2 = across_x(here2)
    here3 = along_z(crossed, outward)
    pair0, sent = add_cores(part0)
    over0 = across_y(wire(sent))
    part1 = partial_ladder(tables, integrals, here1, beside1)
    owed02 = sort_owed(place, 0, pair0)
    beside2, here3, pair0, over0, part1, owed02 = together(beside2, here3, pair0, over0, part1, owed02)
    here3 = jnp.where(inner, crossed, here3)

    beside3 = across_x(here3)
    mine0, sent = add_chips(pair0, over0)
    other0 = to_partner(wire(sent))
    pair1, sent = add_cores(part1)
    over1 = across_y(wire(sent))
    part2 = partial_ladder(tables, integrals, here2, beside2)
    own = sort_own(place, 0, pair0, mine0)
    owed13 = sort_owed(place, 1, pair1)
    beside3, other0, own, owed02, owed13, pair1, over1, part2 = together(
        beside3, other0, own, owed02, owed13, pair1, over1, part2
    )

    mine1, sent = add_chips(pair1, over1)
    other1 = to_partner(wire(sent))
    pair2, sent = add_cores(part2)
    over2 = across_y(wire(sent))
    part3 = partial_ladder(tables, integrals, here3, beside3)
    own = sort_own(place, 1, pair1, mine1, own)
    owed02 = wire(sort_owed(place, 2, pair2, owed02))
    other0, other1, own, owed02, owed13, pair2, over2, part3 = together(
        other0, other1, own, owed02, owed13, pair2, over2, part3
    )

    mine2, sent = add_chips(pair2, over2)
    sent, owed02 = together(wire(sent), owed02)
    other2 = to_partner(sent)
    came02 = to_owner(owed02, (0, 2))
    pair3, sent = add_cores(part3)
    over3 = across_y(wire(sent))
    own = sort_own(place, 2, pair2, mine2, own)
    owed13 = wire(sort_owed(place, 3, pair3, owed13))
    other0, other1, other2, own, came02, owed13, pair3, over3 = together(
        other0, other1, other2, own, came02, owed13, pair3, over3
    )

    mine3, sent = add_chips(pair3, over3)
    sent, other0, other1, other2 = together(sent, other0, other1, other2)
    other3 = to_partner(wire(sent))
    came13 = to_owner(owed13, (1, 3))
    own = sort_own(place, 3, pair3, mine3, own)
    done = [turned(unwire(other)) for other in (other0, other1, other2)]
    sums = gather(gather_kernel, place, own, unwire(came02 + came13))
    sums = gather(merge_kernel, place, sums, *done)
    return finish(place, sums, unwire(other3))


def solution(mesh):
    body = on_device if (mesh.shape["row"], mesh.shape["col"]) == (NZ * NX, NY * NC) else plain
    return jax.shard_map(
        body,
        mesh=mesh,
        in_specs=(P("row", "col"), P("col", "row"), P(), P("row", None), P("col", None)),
        out_specs=P("col", "row"),
        check_vma=False,
    )
```

time: 639 us -> 127 us (0.20)
  waiting for transfers between devices: 492 us -> 49.8 us
  local copies, waits for them, and re-layouts: 101 us -> 11.8 us
  Pallas kernels: 0 us -> 31 us
  starting transfers between devices: 1.63 us -> 30.8 us
  other arithmetic: 15.3 us -> 2.18 us
  matrix products: 13.1 us -> 0 us
  between operations: 13.4 us -> 0.52 us
    ppermute x1 -> x23, waiting for transfers between devices: 360 us -> 49.8 us  [send(): return lax.ppermute(value, ('row', 'col'), pairs)]
    reshape x3 -> x0, local copies, waits for them, and re-layouts: 79.6 us -> none  [the longest x2 53.5 us: on_device(): partner = partner.reshape(OT, OT, product_count, TS, TS)]
    reduce_scatter x1 -> x0, waiting for transfers between devices: 71.5 us -> none  [on_device(): lax.psum_scatter(ladder + partner, 'col', scatter_dimension=0, tiled=True)]
    all_gather x1 -> x0, waiting for transfers between devices: 60 us -> none  [on_device(): lax.all_gather(amplitudes, 'row', axis=0, tiled=True)]
    pallas_call x0 -> x26, Pallas kernels: none -> 31 us  [the longest x4 13.3 us: partial_ladder(): pl.pallas_call(ladder_kernel, in_specs=[pl.BlockSpec(memory_space=pltpu.S...]
    ppermute x1 -> x23, starting transfers between devices: 1.59 us -> 30.8 us  [send(): return lax.ppermute(value, ('row', 'col'), pairs)]
    dot_general x1 -> x0, matrix products: 13.1 us -> none  [on_device(): jnp.dot(lax.all_gather(amplitudes, 'row', axis=0, tiled=True), masked, pr...]
    add x1 -> x0, other arithmetic: 12 us -> none  [on_device(): ladder + partner]
  transfers between devices with their start and end apart: 3 -> 23, of which waited for: 3 -> 14; matrix products, arithmetic and copies ran while one was open for 3% -> 3% of each run, Pallas kernels for 0% -> 22%
where the time goes in v2:
time: 127 us; the launch traced here: 126 us
  waiting for transfers between devices  49.8 us (39%)
  Pallas kernels  31 us (24%)
  starting transfers between devices  30.8 us (24%)
  local copies, waits for them, and re-layouts  11.8 us (9%)
  other arithmetic  2.18 us (2%)
    ppermute x23, waiting for transfers between devices, send(): return lax.ppermute(value, ('row', 'col'), pairs)  49.8 us
    ppermute x23, starting transfers between devices, send(): return lax.ppermute(value, ('row', 'col'), pairs)  30.8 us
    pallas_call x4, Pallas kernels, partial_ladder(): pl.pallas_call(ladder_kernel, in_specs=[pl.BlockSpec(memory_space=pltpu.S...  13.3 us
    unnamed x20, local copies, waits for them, and re-layouts  11.8 us
    pallas_call x8, Pallas kernels, sort(): pl.pallas_call(functools.partial(kernel, step), in_specs=[pl.BlockSpec(me...  5.65 us
    pallas_call x4, Pallas kernels, add_cores(): return call(part, across_core(part))  3.1 us
    pallas_call x1, Pallas kernels, finish(): pl.pallas_call(finish_kernel, in_specs=[pl.BlockSpec(memory_space=pltpu.S...  2.74 us
  transfers between devices with their start and end apart: 23, of which 14 were waited for; matrix products, arithmetic and copies ran while one was open for 3% of the time, Pallas kernels for 22%

profile of v2, /device:TPU:0, one launch (start us, length us, event | category | flops | bytes accessed | tf_op | source)
XLA Modules:
  0.0 126.1 jit_solution(10472578835355260373)
XLA Ops:
  0.0 2.9 %collective-permute-start = (bf16[128,2048]{1,0:T(8,128)(2,1)}, bf16[128,2048]{1,0:T(8,128)(2,1)S(1)}, u32[]{:S(2)}, u32[]{:S(2)}) collective-permute-start(bf16[128,2048]{1,0:T(8,128)(2,1)} %here.1), channel_id=1, source_target_pairs={{0,4},{1,5},{2,6},{3,7},{4,0},{5,1},{6,2},{7,3},{8,12},{9,13},{10,... | collective-permute-start | bytes 1572872 | tf_op jit(solution)/shard_map/ppermute | solution.py:104
  2.9 1.6 %collective-permute-start.1 = (bf16[128,2048]{1,0:T(8,128)(2,1)}, bf16[128,2048]{1,0:T(8,128)(2,1)S(1)}, u32[]{:S(2)}, u32[]{:S(2)}) collective-permute-start(bf16[128,2048]{1,0:T(8,128)(2,1)} %here.1), channel_id=1, source_target_pairs={{0,8},{1,9},{2,10},{3,11},{4,12},{5,13},{6,14},{7,15},{8,0},{9,1},... | collective-permute-start | bytes 1572872 | tf_op jit(solution)/shard_map/ppermute | solution.py:104
  4.5 1.5 %collective-permute-start.2 = (bf16[128,2048]{1,0:T(8,128)(2,1)}, bf16[128,2048]{1,0:T(8,128)(2,1)}, u32[]{:S(2)}, u32[]{:S(2)}) collective-permute-start(bf16[128,2048]{1,0:T(8,128)(2,1)} %here.1), channel_id=1, source_target_pairs={{8,16},{9,17},{10,18},{11,19},{12,20},{13,21},{14,22},{15,23},{16,... | collective-permute-start | bytes 1572872 | tf_op jit(solution)/shard_map/ppermute | solution.py:104
  6.0 9.1 %collective-permute-done.beside = bf16[128,2048]{1,0:T(8,128)(2,1)S(1)} collective-permute-done((bf16[128,2048]{1,0:T(8,128)(2,1)}, bf16[128,2048]{1,0:T(8,128)(2,1)S(1)}, u32[]{:S(2)}, u32[]{:S(2)}) %collective-permute-start) | collective-permute-done | bytes 524320 | tf_op jit(solution)/shard_map/ppermute | solution.py:104
  15.1 0.8 copy-done.3
  16.5 1.1 collective-permute-start.3
  17.6 1.5 %collective-permute-start.4 = (bf16[128,2048]{1,0:T(8,128)(2,1)S(1)}, bf16[128,2048]{1,0:T(8,128)(2,1)}, u32[]{:S(2)}, u32[]{:S(2)}) collective-permute-start(bf16[128,2048]{1,0:T(8,128)(2,1)S(1)} %collective-permute-done.1.here), channel_id=1, source_target_pairs={{8,16},{9,17},{10,18},{11,19},{12,20},{13,21},{14,22},{15,23},{16,... | collective-permute-start | bytes 1572872 | tf_op jit(solution)/shard_map/ppermute | solution.py:104
  19.1 6.4 %collective-permute-start.5 = (bf16[128,2048]{1,0:T(8,128)(2,1)}, bf16[128,2048]{1,0:T(8,128)(2,1)}, u32[]{:S(2)}, u32[]{:S(2)}) collective-permute-start(bf16[128,2048]{1,0:T(8,128)(2,1)} %collective-permute-done.2), channel_id=1, source_target_pairs={{0,8},{1,9},{2,10},{3,11},{4,12},{5,13},{6,14},{7,15},{8,0},{9,1},... | collective-permute-start | bytes 1572872 | tf_op jit(solution)/shard_map/ppermute | solution.py:104
  25.5 0.8 copy.11.product
  26.2 0.8 copy.12.summed
  27.1 3.4 %copy-done = bf16[2048,2048]{1,0:T(8,128)(2,1)S(1)} copy-done((bf16[2048,2048]{1,0:T(8,128)(2,1)S(1)}, bf16[2048,2048]{1,0:T(8,128)(2,1)}, u32[]{:S(2)}) %copy-start) | copy-done | bytes 8388632
  30.4 1.0 copy-done.2
  31.5 1.0 copy-done.4
  33.2 3.3 %partial_ladder.4.part = f32[4,64,2048]{2,1,0:T(8,128)S(1)} custom-call(s32[2]{0:T(128)S(1)} %pad_add_fusion.place, s32[24]{0:T(128)S(1)} %copy-done.5, s32[8,2]{1,0:T(8,128)S(1)} %copy.11.product, s32[8,2]{1,0:T(8,128)S(1)} %copy.12.summed, bf16[128,2048]{1,0:T(8,128)(2,1)S(1)} %copy-done.2, bf16[128,2048]{1,0:T(8,128)(2,1)S(1)} %copy-done.4, ...), custom_call_target="tpu_custom_call" | custom-call | flops 1000 | bytes 1000 | tf_op jit(solution)/shard_map/partial_ladder/pallas_call | solution.py:169
  36.6 1.1 broadcast_select_fusion.1.here
  37.8 1.6 %collective-permute-start.6 = (bf16[128,2048]{1,0:T(8,128)(2,1)S(1)}, bf16[128,2048]{1,0:T(8,128)(2,1)S(1)}, u32[]{:S(2)}, u32[]{:S(2)}) collective-permute-start(bf16[128,2048]{1,0:T(8,128)(2,1)S(1)} %broadcast_select_fusion.1.here), channel_id=1, source_target_pairs={{0,4},{1,5},{2,6},{3,7},{4,0},{5,1},{6,2},{7,3},{8,12},{9,13},{10,... | collective-permute-start | bytes 1572872 | tf_op jit(solution)/shard_map/ppermute | solution.py:104
  39.3 0.8 collective-permute-start.7
  40.1 0.8 collective-permute-done.8.sibling
  40.9 2.0 %add_cores.4 = (f32[4,64,2048]{2,1,0:T(8,128)S(1)}, f32[64,2176]{1,0:T(8,128)S(1)}) custom-call(f32[4,64,2048]{2,1,0:T(8,128)S(1)} %partial_ladder.4.part, f32[4,64,2048]{2,1,0:T(8,128)} %collective-permute-done.8.sibling), custom_call_target="tpu_custom_call" | custom-call | flops 1000 | bytes 1000 | tf_op jit(solution)/shard_map/add_cores/pallas_call | solution.py:366
  42.9 1.6 %collective-permute-start.9 = (f16[64,2176]{1,0:T(8,128)(2,1)S(1)}, f16[64,2176]{1,0:T(8,128)(2,1)S(1)}, u32[]{:S(2)}, u32[]{:S(2)}) collective-permute-start(f16[64,2176]{1,0:T(8,128)(2,1)S(1)} %convert_element_type.57), channel_id=1, source_target_pairs={{0,2},{1,3},{2,0},{3,1},{4,6},{5,7},{6,4},{7,5},{8,10},{9,11},{10,... | collective-permute-start | bytes 835592 | tf_op jit(solution)/shard_map/ppermute | solution.py:104
  44.5 3.4 %copy-done.1 = bf16[2048,2048]{1,0:T(8,128)(2,1)S(1)} copy-done((bf16[2048,2048]{1,0:T(8,128)(2,1)S(1)}, bf16[2048,2048]{1,0:T(8,128)(2,1)}, u32[]{:S(2)}) %copy-start.1) | copy-done | bytes 8388632
  47.9 3.3 %partial_ladder.5.part = f32[4,64,2048]{2,1,0:T(8,128)S(1)} custom-call(s32[2]{0:T(128)S(1)} %pad_add_fusion.place, s32[24]{0:T(128)S(1)} %copy-done.6, s32[8,2]{1,0:T(8,128)S(1)} %copy.11.product, s32[8,2]{1,0:T(8,128)S(1)} %copy.12.summed, bf16[128,2048]{1,0:T(8,128)(2,1)S(1)} %collective-permute-done.1.here, ...), custom_call_target="tpu_custom_call" | custom-call | flops 1000 | bytes 1000 | tf_op jit(solution)/shard_map/partial_ladder/pallas_call | solution.py:169
  52.1 1.4 %collective-permute-done.7 = bf16[128,2048]{1,0:T(8,128)(2,1)S(1)} collective-permute-done((bf16[128,2048]{1,0:T(8,128)(2,1)}, bf16[128,2048]{1,0:T(8,128)(2,1)S(1)}, u32[]{:S(2)}, u32[]{:S(2)}) %collective-permute-start.7) | collective-permute-done | bytes 524320 | tf_op jit(solution)/shard_map/ppermute | solution.py:104
  54.8 2.1 %collective-permute-start.11 = (f16[64,2176]{1,0:T(8,128)(2,1)S(1)}, f16[64,2176]{1,0:T(8,128)(2,1)S(1)}, u32[]{:S(2)}, u32[]{:S(2)}) collective-permute-start(f16[64,2176]{1,0:T(8,128)(2,1)S(1)} %convert_element_type.59), channel_id=1, source_target_pairs={{0,16},{1,17},{2,18},{3,19},{4,20},{5,21},{6,22},{7,23},{8,24},{9,... | collective-permute-start | bytes 835592 | tf_op jit(solution)/shard_map/ppermute | solution.py:104
  56.9 0.8 collective-permute-done.12.sibling
  58.1 1.6 %collective-permute-start.13 = (f16[64,2176]{1,0:T(8,128)(2,1)S(1)}, f16[64,2176]{1,0:T(8,128)(2,1)S(1)}, u32[]{:S(2)}, u32[]{:S(2)}) collective-permute-start(f16[64,2176]{1,0:T(8,128)(2,1)S(1)} %convert_element_type.60), channel_id=1, source_target_pairs={{0,2},{1,3},{2,0},{3,1},{4,6},{5,7},{6,4},{7,5},{8,10},{9,11},{10,... | collective-permute-start | bytes 835592 | tf_op jit(solution)/shard_map/ppermute | solution.py:104
  59.7 0.7 sort.9.refs_0_
  60.5 3.3 %partial_ladder.6.part = f32[4,64,2048]{2,1,0:T(8,128)S(1)} custom-call(s32[2]{0:T(128)S(1)} %pad_add_fusion.place, s32[24]{0:T(128)S(1)} %copy-done.6, s32[8,2]{1,0:T(8,128)S(1)} %copy.11.product, s32[8,2]{1,0:T(8,128)S(1)} %copy.12.summed, bf16[128,2048]{1,0:T(8,128)(2,1)S(1)} %broadcast_select_fusion.1.here, ...), custom_call_target="tpu_custom_call" | custom-call | flops 1000 | bytes 1000 | tf_op jit(solution)/shard_map/partial_ladder/pallas_call | solution.py:169
  63.8 0.7 sort.10.refs_0_
  64.6 5.9 %collective-permute-done.11 = f16[64,2176]{1,0:T(8,128)(2,1)S(1)} collective-permute-done((f16[64,2176]{1,0:T(8,128)(2,1)S(1)}, f16[64,2176]{1,0:T(8,128)(2,1)S(1)}, u32[]{:S(2)}, u32[]{:S(2)}) %collective-permute-start.11) | collective-permute-done | bytes 278560 | tf_op jit(solution)/shard_map/ppermute | solution.py:104
  71.1 3.6 %collective-permute-done.15.sibling = f32[4,64,2048]{2,1,0:T(8,128)S(1)} collective-permute-done((f32[4,64,2048]{2,1,0:T(8,128)S(1)}, f32[4,64,2048]{2,1,0:T(8,128)S(1)}, u32[]{:S(2)}, u32[]{:S(2)}) %collective-permute-start.15) | collective-permute-done | bytes 2097184 | tf_op jit(solution)/shard_map/ppermute | solution.py:104
  75.1 1.6 %collective-permute-start.16 = (f16[64,2176]{1,0:T(8,128)(2,1)S(1)}, f16[64,2176]{1,0:T(8,128)(2,1)S(1)}, u32[]{:S(2)}, u32[]{:S(2)}) collective-permute-start(f16[64,2176]{1,0:T(8,128)(2,1)S(1)} %convert_element_type.64), channel_id=1, source_target_pairs={{0,2},{1,3},{2,0},{3,1},{4,6},{5,7},{6,4},{7,5},{8,10},{9,11},{10,... | collective-permute-start | bytes 835592 | tf_op jit(solution)/shard_map/ppermute | solution.py:104
  76.7 3.3 %partial_ladder.7.part = f32[4,64,2048]{2,1,0:T(8,128)S(1)} custom-call(s32[2]{0:T(128)S(1)} %pad_add_fusion.place, s32[24]{0:T(128)S(1)} %copy-done.6, s32[8,2]{1,0:T(8,128)S(1)} %copy.11.product, s32[8,2]{1,0:T(8,128)S(1)} %copy.12.summed, bf16[128,2048]{1,0:T(8,128)(2,1)S(1)} %broadcast_select_fusion.here, ...), custom_call_target="tpu_custom_call" | custom-call | flops 1000 | bytes 1000 | tf_op jit(solution)/shard_map/partial_ladder/pallas_call | solution.py:169
  80.6 1.3 %sort.12 = f32[3,64,2176]{2,1,0:T(8,128)S(1)} custom-call(s32[2]{0:T(128)S(1)} %pad_add_fusion.place, f32[4,64,2048]{2,1,0:T(8,128)S(1)} %get-tuple-element.97.pair, f32[3,64,2176]{2,1,0:T(8,128)S(1)} %sort.8.refs_0_), custom_call_target="tpu_custom_call", output_to_operand_aliasing={{}: (2, {})} | custom-call | flops 1000 | bytes 1000 | tf_op jit(solution)/shard_map/sort/pallas_call | solution.py:240
  82.0 4.1 %collective-permute-done.14 = f16[64,2176]{1,0:T(8,128)(2,1)S(1)} collective-permute-done((f16[64,2176]{1,0:T(8,128)(2,1)S(1)}, f16[64,2176]{1,0:T(8,128)(2,1)S(1)}, u32[]{:S(2)}, u32[]{:S(2)}) %collective-permute-start.14) | collective-permute-done | bytes 278560 | tf_op jit(solution)/shard_map/ppermute | solution.py:104
  86.7 3.4 %collective-permute-start.18 = (f16[3,64,2176]{2,1,0:T(8,128)(2,1)S(1)}, f16[3,64,2176]{2,1,0:T(8,128)(2,1)S(1)}, u32[]{:S(2)}, u32[]{:S(2)}) collective-permute-start(f16[3,64,2176]{2,1,0:T(8,128)(2,1)S(1)} %convert_element_type.63), channel_id=1, source_target_pairs={{0,2},{2,0},{4,6},{6,4},{8,10},{11,9},{12,14},{15,13},{16,18},{19,... | collective-permute-start | bytes 2506760 | tf_op jit(solution)/shard_map/ppermute | solution.py:104
  90.7 1.6 %collective-permute-start.20 = (f16[64,2176]{1,0:T(8,128)(2,1)S(1)}, f16[64,2176]{1,0:T(8,128)(2,1)S(1)}, u32[]{:S(2)}, u32[]{:S(2)}) collective-permute-start(f16[64,2176]{1,0:T(8,128)(2,1)S(1)} %convert_element_type.68), channel_id=1, source_target_pairs={{0,2},{1,3},{2,0},{3,1},{4,6},{5,7},{6,4},{7,5},{8,10},{9,11},{10,... | collective-permute-start | bytes 835592 | tf_op jit(solution)/shard_map/ppermute | solution.py:104
  93.5 9.8 %collective-permute-done.17 = f16[64,2176]{1,0:T(8,128)(2,1)S(1)} collective-permute-done((f16[64,2176]{1,0:T(8,128)(2,1)S(1)}, f16[64,2176]{1,0:T(8,128)(2,1)S(1)}, u32[]{:S(2)}, u32[]{:S(2)}) %collective-permute-start.17) | collective-permute-done | bytes 278560 | tf_op jit(solution)/shard_map/ppermute | solution.py:104
  103.3 0.7 collective-permute-done.18
  104.1 3.0 %collective-permute-done.20 = f16[64,2176]{1,0:T(8,128)(2,1)S(1)} collective-permute-done((f16[64,2176]{1,0:T(8,128)(2,1)S(1)}, f16[64,2176]{1,0:T(8,128)(2,1)S(1)}, u32[]{:S(2)}, u32[]{:S(2)}) %collective-permute-start.20) | collective-permute-done | bytes 278560 | tf_op jit(solution)/shard_map/ppermute | solution.py:104
  107.1 0.7 collective-permute-start.21
  109.1 0.7 turn.3.turned0
  109.8 0.7 turn.4.turned1
  110.8 0.7 turn.5.turned2
  111.5 1.5 %gather.2.sums = f32[4,64,2048]{2,1,0:T(8,128)S(1)} custom-call(s32[2]{0:T(128)S(1)} %pad_add_fusion.place, f32[4,64,2048]{2,1,0:T(8,128)S(1)} %sort.15.own, f32[3,64,2176]{2,1,0:T(8,128)S(1)} %add_convert_fusion.rest), custom_call_target="tpu_custom_call" | custom-call | flops 1000 | bytes 1000 | tf_op jit(solution)/shard_map/gather/pallas_call | solution.py:280
  113.0 9.4 %collective-permute-done.22 = f16[64,2176]{1,0:T(8,128)(2,1)S(1)} collective-permute-done((f16[64,2176]{1,0:T(8,128)(2,1)S(1)}, f16[64,2176]{1,0:T(8,128)(2,1)S(1)}, u32[]{:S(2)}, u32[]{:S(2)}) %collective-permute-start.22) | collective-permute-done | bytes 278560 | tf_op jit(solution)/shard_map/ppermute | solution.py:104
  122.5 0.8 gather.3.sums
  123.3 2.7 %finish.1 = bf16[256,2048]{1,0:T(8,128)(2,1)} custom-call(s32[2]{0:T(128)S(1)} %pad_add_fusion.place, f32[4,64,2048]{2,1,0:T(8,128)S(1)} %gather.3.sums, f32[64,2176]{1,0:T(8,128)S(1)} %convert_element_type.75.last), custom_call_target="tpu_custom_call" | custom-call | flops 1000 | bytes 1000 | tf_op jit(solution)/shard_map/finish/pallas_call | solution.py:304
  (67 shorter events, 9.5 us)
Async XLA Ops:
  0.0 15.1 %collective-permute-start = (bf16[128,2048]{1,0:T(8,128)(2,1)}, bf16[128,2048]{1,0:T(8,128)(2,1)S(1)}, u32[]{:S(2)}, u32[]{:S(2)}) collective-permute-start(bf16[128,2048]{1,0:T(8,128)(2,1)} %here.1), channel_id=1, source_target_pairs={{0,4},{1,5},{2,6},{3,7},{4,0},{5,1},{6,2},{7,3},{8,12},{9,13},{10,... | collective-permute-start | bytes 1572872 | tf_op jit(solution)/shard_map/ppermute | solution.py:104
  2.9 13.6 %collective-permute-start.1 = (bf16[128,2048]{1,0:T(8,128)(2,1)}, bf16[128,2048]{1,0:T(8,128)(2,1)S(1)}, u32[]{:S(2)}, u32[]{:S(2)}) collective-permute-start(bf16[128,2048]{1,0:T(8,128)(2,1)} %here.1), channel_id=1, source_target_pairs={{0,8},{1,9},{2,10},{3,11},{4,12},{5,13},{6,14},{7,15},{8,0},{9,1},... | collective-permute-start | bytes 1572872 | tf_op jit(solution)/shard_map/ppermute | solution.py:104
  4.5 12.0 %collective-permute-start.2 = (bf16[128,2048]{1,0:T(8,128)(2,1)}, bf16[128,2048]{1,0:T(8,128)(2,1)}, u32[]{:S(2)}, u32[]{:S(2)}) collective-permute-start(bf16[128,2048]{1,0:T(8,128)(2,1)} %here.1), channel_id=1, source_target_pairs={{8,16},{9,17},{10,18},{11,19},{12,20},{13,21},{14,22},{15,23},{16,... | collective-permute-start | bytes 1572872 | tf_op jit(solution)/shard_map/ppermute | solution.py:104
  15.1 0.8 copy-start.3
  16.5 20.0 %collective-permute-start.3 = (bf16[128,2048]{1,0:T(8,128)(2,1)S(1)}, bf16[128,2048]{1,0:T(8,128)(2,1)S(1)}, u32[]{:S(2)}, u32[]{:S(2)}) collective-permute-start(bf16[128,2048]{1,0:T(8,128)(2,1)S(1)} %collective-permute-done.1.here), channel_id=1, source_target_pairs={{0,4},{1,5},{2,6},{3,7},{4,0},{5,1},{6,2},{7,3},{8,12},{9,13},{10,... | collective-permute-start | bytes 1572872 | tf_op jit(solution)/shard_map/ppermute | solution.py:104
  17.6 18.9 %collective-permute-start.4 = (bf16[128,2048]{1,0:T(8,128)(2,1)S(1)}, bf16[128,2048]{1,0:T(8,128)(2,1)}, u32[]{:S(2)}, u32[]{:S(2)}) collective-permute-start(bf16[128,2048]{1,0:T(8,128)(2,1)S(1)} %collective-permute-done.1.here), channel_id=1, source_target_pairs={{8,16},{9,17},{10,18},{11,19},{12,20},{13,21},{14,22},{15,23},{16,... | collective-permute-start | bytes 1572872 | tf_op jit(solution)/shard_map/ppermute | solution.py:104
  19.1 17.5 %collective-permute-start.5 = (bf16[128,2048]{1,0:T(8,128)(2,1)}, bf16[128,2048]{1,0:T(8,128)(2,1)}, u32[]{:S(2)}, u32[]{:S(2)}) collective-permute-start(bf16[128,2048]{1,0:T(8,128)(2,1)} %collective-permute-done.2), channel_id=1, source_target_pairs={{0,8},{1,9},{2,10},{3,11},{4,12},{5,13},{6,14},{7,15},{8,0},{9,1},... | collective-permute-start | bytes 1572872 | tf_op jit(solution)/shard_map/ppermute | solution.py:104
  27.1 3.4 %copy-start = (bf16[2048,2048]{1,0:T(8,128)(2,1)S(1)}, bf16[2048,2048]{1,0:T(8,128)(2,1)}, u32[]{:S(2)}) copy-start(bf16[2048,2048]{1,0:T(8,128)(2,1)} %integrals.7) | copy-start | bytes 25165828
  30.4 1.0 copy-start.2
  31.5 1.0 copy-start.4
  32.5 0.7 copy-start.5
  36.6 4.4 %collective-permute-start.8 = (f32[4,64,2048]{2,1,0:T(8,128)S(1)}, f32[4,64,2048]{2,1,0:T(8,128)}, u32[]{:S(2)}, u32[]{:S(2)}) collective-permute-start(f32[4,64,2048]{2,1,0:T(8,128)S(1)} %partial_ladder.4.part), channel_id=1, source_target_pairs={{0,1},{1,0},{2,3},{3,2},{4,5},{5,4},{6,7},{7,6},{8,9},{9,8},{10,11... | collective-permute-start | bytes 6291464 | tf_op jit(solution)/shard_map/ppermute | solution.py:104
  37.8 6.7 %copy-start.6 = (s32[24]{0:T(128)S(1)}, s32[24]{0:T(128)}, u32[]{:S(2)}) copy-start(s32[24]{0:T(128)} %irrep.7) | copy-start | bytes 292
  37.8 14.4 %collective-permute-start.6 = (bf16[128,2048]{1,0:T(8,128)(2,1)S(1)}, bf16[128,2048]{1,0:T(8,128)(2,1)S(1)}, u32[]{:S(2)}, u32[]{:S(2)}) collective-permute-start(bf16[128,2048]{1,0:T(8,128)(2,1)S(1)} %broadcast_select_fusion.1.here), channel_id=1, source_target_pairs={{0,4},{1,5},{2,6},{3,7},{4,0},{5,1},{6,2},{7,3},{8,12},{9,13},{10,... | collective-permute-start | bytes 1572872 | tf_op jit(solution)/shard_map/ppermute | solution.py:104
  39.3 14.2 %collective-permute-start.7 = (bf16[128,2048]{1,0:T(8,128)(2,1)}, bf16[128,2048]{1,0:T(8,128)(2,1)S(1)}, u32[]{:S(2)}, u32[]{:S(2)}) collective-permute-start(bf16[128,2048]{1,0:T(8,128)(2,1)} %collective-permute-done.4), channel_id=1, source_target_pairs={{0,8},{1,9},{2,10},{3,11},{4,12},{5,13},{6,14},{7,15},{8,0},{9,1},... | collective-permute-start | bytes 1572872 | tf_op jit(solution)/shard_map/ppermute | solution.py:104
  42.9 10.6 %collective-permute-start.9 = (f16[64,2176]{1,0:T(8,128)(2,1)S(1)}, f16[64,2176]{1,0:T(8,128)(2,1)S(1)}, u32[]{:S(2)}, u32[]{:S(2)}) collective-permute-start(f16[64,2176]{1,0:T(8,128)(2,1)S(1)} %convert_element_type.57), channel_id=1, source_target_pairs={{0,2},{1,3},{2,0},{3,1},{4,6},{5,7},{6,4},{7,5},{8,10},{9,11},{10,... | collective-permute-start | bytes 835592 | tf_op jit(solution)/shard_map/ppermute | solution.py:104
  44.5 3.4 %copy-start.1 = (bf16[2048,2048]{1,0:T(8,128)(2,1)S(1)}, bf16[2048,2048]{1,0:T(8,128)(2,1)}, u32[]{:S(2)}) copy-start(bf16[2048,2048]{1,0:T(8,128)(2,1)} %integrals.7) | copy-start | bytes 25165828
  53.6 4.2 %collective-permute-start.12 = (f32[4,64,2048]{2,1,0:T(8,128)S(1)}, f32[4,64,2048]{2,1,0:T(8,128)S(1)}, u32[]{:S(2)}, u32[]{:S(2)}) collective-permute-start(f32[4,64,2048]{2,1,0:T(8,128)S(1)} %partial_ladder.5.part), channel_id=1, source_target_pairs={{0,1},{1,0},{2,3},{3,2},{4,5},{5,4},{6,7},{7,6},{8,9},{9,8},{10,11... | collective-permute-start | bytes 6291464 | tf_op jit(solution)/shard_map/ppermute | solution.py:104
  53.6 6.9 %slice-start = ((s8[8388608]{0:T(1024)(128)(4,1)}), s8[4194304]{0:T(1024)(128)(4,1)S(1)}, s32[]{:S(2)}) async-start(s8[8388608]{0:T(1024)(128)(4,1)} %bitcast.2), calls=%async_computation | async-start | bytes 8388608
  53.6 16.8 %collective-permute-start.10 = (bf16[128,2048]{1,0:T(8,128)(2,1)S(1)}, bf16[128,2048]{1,0:T(8,128)(2,1)S(1)}, u32[]{:S(2)}, u32[]{:S(2)}) collective-permute-start(bf16[128,2048]{1,0:T(8,128)(2,1)S(1)} %broadcast_select_fusion.here), channel_id=1, source_target_pairs={{0,4},{1,5},{2,6},{3,7},{4,0},{5,1},{6,2},{7,3},{8,12},{9,13},{10,... | collective-permute-start | bytes 1572872 | tf_op jit(solution)/shard_map/ppermute | solution.py:104
  54.8 5.7 %slice-start.1 = ((s8[8388608]{0:T(1024)(128)(4,1)}), s8[4194304]{0:T(1024)(128)(4,1)S(1)}, s32[]{:S(2)}) async-start(s8[8388608]{0:T(1024)(128)(4,1)} %bitcast.2), calls=%async_computation.1 | async-start | bytes 8388608
  54.8 15.7 %collective-permute-start.11 = (f16[64,2176]{1,0:T(8,128)(2,1)S(1)}, f16[64,2176]{1,0:T(8,128)(2,1)S(1)}, u32[]{:S(2)}, u32[]{:S(2)}) collective-permute-start(f16[64,2176]{1,0:T(8,128)(2,1)S(1)} %convert_element_type.59), channel_id=1, source_target_pairs={{0,16},{1,17},{2,18},{3,19},{4,20},{5,21},{6,22},{7,23},{8,24},{9,... | collective-permute-start | bytes 835592 | tf_op jit(solution)/shard_map/ppermute | solution.py:104
  58.1 12.3 %collective-permute-start.13 = (f16[64,2176]{1,0:T(8,128)(2,1)S(1)}, f16[64,2176]{1,0:T(8,128)(2,1)S(1)}, u32[]{:S(2)}, u32[]{:S(2)}) collective-permute-start(f16[64,2176]{1,0:T(8,128)(2,1)S(1)} %convert_element_type.60), channel_id=1, source_target_pairs={{0,2},{1,3},{2,0},{3,1},{4,6},{5,7},{6,4},{7,5},{8,10},{9,11},{10,... | collective-permute-start | bytes 835592 | tf_op jit(solution)/shard_map/ppermute | solution.py:104
  70.5 4.2 %collective-permute-start.15 = (f32[4,64,2048]{2,1,0:T(8,128)S(1)}, f32[4,64,2048]{2,1,0:T(8,128)S(1)}, u32[]{:S(2)}, u32[]{:S(2)}) collective-permute-start(f32[4,64,2048]{2,1,0:T(8,128)S(1)} %partial_ladder.6.part), channel_id=1, source_target_pairs={{0,1},{1,0},{2,3},{3,2},{4,5},{5,4},{6,7},{7,6},{8,9},{9,8},{10,11... | collective-permute-start | bytes 6291464 | tf_op jit(solution)/shard_map/ppermute | solution.py:104
  71.0 15.1 %collective-permute-start.14 = (f16[64,2176]{1,0:T(8,128)(2,1)S(1)}, f16[64,2176]{1,0:T(8,128)(2,1)S(1)}, u32[]{:S(2)}, u32[]{:S(2)}) collective-permute-start(f16[64,2176]{1,0:T(8,128)(2,1)S(1)} %convert_element_type.62), channel_id=1, source_target_pairs={{0,16},{1,17},{2,18},{3,19},{4,20},{5,21},{6,22},{7,23},{8,24},{9,... | collective-permute-start | bytes 835592 | tf_op jit(solution)/shard_map/ppermute | solution.py:104
  75.1 11.0 %collective-permute-start.16 = (f16[64,2176]{1,0:T(8,128)(2,1)S(1)}, f16[64,2176]{1,0:T(8,128)(2,1)S(1)}, u32[]{:S(2)}, u32[]{:S(2)}) collective-permute-start(f16[64,2176]{1,0:T(8,128)(2,1)S(1)} %convert_element_type.64), channel_id=1, source_target_pairs={{0,2},{1,3},{2,0},{3,1},{4,6},{5,7},{6,4},{7,5},{8,10},{9,11},{10,... | collective-permute-start | bytes 835592 | tf_op jit(solution)/shard_map/ppermute | solution.py:104
  86.1 4.2 %collective-permute-start.19 = (f32[4,64,2048]{2,1,0:T(8,128)S(1)}, f32[4,64,2048]{2,1,0:T(8,128)S(1)}, u32[]{:S(2)}, u32[]{:S(2)}) collective-permute-start(f32[4,64,2048]{2,1,0:T(8,128)S(1)} %partial_ladder.7.part), channel_id=1, source_target_pairs={{0,1},{1,0},{2,3},{3,2},{4,5},{5,4},{6,7},{7,6},{8,9},{9,8},{10,11... | collective-permute-start | bytes 6291464 | tf_op jit(solution)/shard_map/ppermute | solution.py:104
  86.7 17.4 %collective-permute-start.18 = (f16[3,64,2176]{2,1,0:T(8,128)(2,1)S(1)}, f16[3,64,2176]{2,1,0:T(8,128)(2,1)S(1)}, u32[]{:S(2)}, u32[]{:S(2)}) collective-permute-start(f16[3,64,2176]{2,1,0:T(8,128)(2,1)S(1)} %convert_element_type.63), channel_id=1, source_target_pairs={{0,2},{2,0},{4,6},{6,4},{8,10},{11,9},{12,14},{15,13},{16,18},{19,... | collective-permute-start | bytes 2506760 | tf_op jit(solution)/shard_map/ppermute | solution.py:104
  90.1 13.2 %collective-permute-start.17 = (f16[64,2176]{1,0:T(8,128)(2,1)S(1)}, f16[64,2176]{1,0:T(8,128)(2,1)S(1)}, u32[]{:S(2)}, u32[]{:S(2)}) collective-permute-start(f16[64,2176]{1,0:T(8,128)(2,1)S(1)} %convert_element_type.66), channel_id=1, source_target_pairs={{0,16},{1,17},{2,18},{3,19},{4,20},{5,21},{6,22},{7,23},{8,24},{9,... | collective-permute-start | bytes 835592 | tf_op jit(solution)/shard_map/ppermute | solution.py:104
  90.7 16.4 %collective-permute-start.20 = (f16[64,2176]{1,0:T(8,128)(2,1)S(1)}, f16[64,2176]{1,0:T(8,128)(2,1)S(1)}, u32[]{:S(2)}, u32[]{:S(2)}) collective-permute-start(f16[64,2176]{1,0:T(8,128)(2,1)S(1)} %convert_element_type.68), channel_id=1, source_target_pairs={{0,2},{1,3},{2,0},{3,1},{4,6},{5,7},{6,4},{7,5},{8,10},{9,11},{10,... | collective-permute-start | bytes 835592 | tf_op jit(solution)/shard_map/ppermute | solution.py:104
  107.1 3.5 %collective-permute-start.21 = (f16[3,64,2176]{2,1,0:T(8,128)(2,1)S(1)}, f16[3,64,2176]{2,1,0:T(8,128)(2,1)S(1)}, u32[]{:S(2)}, u32[]{:S(2)}) collective-permute-start(f16[3,64,2176]{2,1,0:T(8,128)(2,1)S(1)} %convert_element_type.67), channel_id=1, source_target_pairs={{1,3},{3,1},{5,7},{7,5},{9,11},{10,8},{13,15},{14,12},{17,19},{18,... | collective-permute-start | bytes 2506760 | tf_op jit(solution)/shard_map/ppermute | solution.py:104
  108.4 14.1 %collective-permute-start.22 = (f16[64,2176]{1,0:T(8,128)(2,1)S(1)}, f16[64,2176]{1,0:T(8,128)(2,1)S(1)}, u32[]{:S(2)}, u32[]{:S(2)}) collective-permute-start(f16[64,2176]{1,0:T(8,128)(2,1)S(1)} %convert_element_type.74), channel_id=1, source_target_pairs={{0,16},{1,17},{2,18},{3,19},{4,20},{5,21},{6,22},{7,23},{8,24},{9,... | collective-permute-start | bytes 835592 | tf_op jit(solution)/shard_map/ppermute | solution.py:104

commit v3 on v2

v3 whole, which is shorter than its diff:
```python
import functools

import jax
import jax.numpy as jnp
import numpy as np
from jax import lax
from jax.experimental import pallas as pl
from jax.experimental.pallas import tpu as pltpu
from jax.sharding import PartitionSpec as P

TS = 16
TP = TS * TS
OT = 32
WIRE = jnp.float16


def from_partner(value, axis, distance):
    mask = 2**distance
    pairs = [(source, source ^ mask) for source in range(lax.axis_size(axis))]
    return lax.ppermute(value, axis, pairs)


def pair_symmetry(tile_irrep, pairs):
    return jnp.bitwise_xor(tile_irrep[pairs[:, 0]], tile_irrep[pairs[:, 1]])


def plain(amplitudes, integrals, tile_irrep, product_pairs, summed_pairs):
    product_sym = pair_symmetry(tile_irrep, product_pairs)
    summed_sym = pair_symmetry(tile_irrep, summed_pairs)
    allowed = summed_sym[:, None] == product_sym[None, :]
    summed_count = summed_pairs.shape[0]
    product_count = product_pairs.shape[0]
    keep = allowed.astype(integrals.dtype)
    masked = (
        integrals.reshape(summed_count, TP, product_count, TP)
        * keep[:, None, :, None]
    ).reshape(integrals.shape)
    half_bit = lax.axis_size("row").bit_length() - 2
    ladder = jnp.dot(
        lax.all_gather(amplitudes, "row", axis=0, tiled=True),
        masked,
        preferred_element_type=jnp.float32,
    )
    partner = from_partner(ladder, "row", half_bit)
    partner = partner.reshape(OT, OT, product_count, TS, TS)
    partner = jnp.transpose(partner, (1, 0, 2, 4, 3)).reshape(ladder.shape)
    summed = lax.psum_scatter(ladder + partner, "col", scatter_dimension=0, tiled=True)
    return summed.astype(jnp.bfloat16)


NZ, NX, NY, NC = 4, 2, 2, 2
ROWS = 128
HALF = 32
PART = 2 * HALF
OWNED = 256
WIDTH = 2048
PANELS = WIDTH // TP
LANES = 128
PLANES = ((0, 1, 2, 3), (1, 0, 2, 3), (2, 3, 1, 0), (3, 2, 1, 0))
PART_OF = (1, 2, 0, 3)


CHUNKS = (((0, 0),), ((0, 1), (1, 0)), ((1, 1), (2, 0)), ((2, 1), (3, 0)), ((3, 1),))


def params(mib):
    return pltpu.CompilerParams(vmem_limit_bytes=mib * 2**20)


def light():
    return pl.CostEstimate(flops=1000, bytes_accessed=1000, transcendentals=0)


def selection(extents, axes):
    n = int(np.prod(extents))
    row = lax.broadcasted_iota(jnp.int32, (n, n), 0)
    column = lax.broadcasted_iota(jnp.int32, (n, n), 1)
    strides = [int(np.prod(extents[axis + 1 :])) for axis in range(len(extents))]
    source, below = jnp.zeros_like(row), 1
    for axis in reversed(axes):
        source += row // below % extents[axis] * strides[axis]
        below *= extents[axis]
    return jnp.where(source == column, 1.0, 0.0).astype(jnp.bfloat16)


def block_order():
    return selection((4, 32), (1, 0))


def align_order():
    return selection((2, 4, 4), (0, 2, 1))


def natural_order():
    return selection((4, 2, 8, 4), (1, 3, 0, 2))


def swap_order():
    return selection((TS, TS), (1, 0))


def send(value, target):
    pairs = []
    for n, (z, x, y, k) in enumerate(np.ndindex(NZ, NX, NY, NC)):
        to = target(z, x, y, k)
        if to is not None:
            pairs.append((n, int(np.ravel_multi_index(to, (NZ, NX, NY, NC)))))
    return lax.ppermute(value, ("row", "col"), pairs)


def along_z(value, moves):
    return send(value, lambda z, x, y, k: (moves[z], x, y, k) if z in moves else None)


def across_x(value, planes=range(NZ)):
    return send(value, lambda z, x, y, k: (z, 1 - x, y, k) if z in planes else None)


def across_y(value):
    return send(value, lambda z, x, y, k: (z, x, 1 - y, k))


def across_core(value):
    return send(value, lambda z, x, y, k: (z, x, y, 1 - k))


def to_partner(value):
    return send(value, lambda z, x, y, k: (z ^ 2, x, y, k))


def matmul(a, b):
    return jnp.dot(a, b, preferred_element_type=jnp.float32)


def lookup(table, index):
    value = table[0]
    for n in range(1, len(table)):
        value = jnp.where(index == n, table[n], value)
    return value


def ladder_kernel(place, irrep, product, summed, *refs):
    blocks, (integrals, out, rows) = refs[:-3], refs[-3:]
    order = block_order()
    for n, block in enumerate(blocks):
        rows[n * ROWS : (n + 1) * ROWS, :] = matmul(order, block[...]).astype(jnp.bfloat16)
    for p in range(PANELS):
        wanted = irrep[product[p, 0]] ^ irrep[product[p, 1]]
        kept = []
        for q in range(WIDTH // TP):
            same = (irrep[summed[q, 0]] ^ irrep[summed[q, 1]]) == wanted
            value = rows[:, q * TP : (q + 1) * TP]
            kept.append(jnp.where(same, value, jnp.zeros_like(value)))
        cut = slice(p * TP, (p + 1) * TP)
        total = matmul(jnp.concatenate(kept, axis=1), integrals[:, cut])
        for to in range(4):
            for n in range(len(blocks)):
                start = n * ROWS + to * HALF
                out[lookup(PART_OF, to ^ place[1]), n * HALF : (n + 1) * HALF, cut] = total[start : start + HALF, :]


def partial_ladder(tables, integrals, *blocks):
    vmem = pl.BlockSpec(memory_space=pltpu.VMEM)
    return pl.pallas_call(
        ladder_kernel,
        in_specs=[pl.BlockSpec(memory_space=pltpu.SMEM)] * 4 + [vmem] * (len(blocks) + 1),
        out_specs=vmem,
        scratch_shapes=[pltpu.VMEM((len(blocks) * ROWS, WIDTH), jnp.bfloat16)],
        out_shape=jax.ShapeDtypeStruct((4, len(blocks) * HALF, WIDTH), jnp.float32),
        compiler_params=params(14),
        cost_estimate=light(),
        name="partial_ladder",
    )(*tables, *blocks, integrals)


def turn(arrived):
    high = arrived.astype(jnp.bfloat16)
    low = (arrived - high.astype(jnp.float32)).astype(jnp.bfloat16)
    both = jnp.concatenate([high, low], axis=0)
    swap, align = swap_order(), align_order()
    cuts = [both[:, p * TP : (p + 1) * TP] for p in range(PANELS)]
    both = jnp.concatenate([matmul(cut, swap).astype(jnp.bfloat16) for cut in cuts], axis=1)
    halves = [matmul(align, both[n : n + HALF]) for n in range(0, both.shape[0], HALF)]
    count = len(halves) // 2
    return jnp.concatenate([high + low for high, low in zip(halves[:count], halves[count:], strict=True)], axis=0)


def turn_kernel(arrived, out):
    out[...] = turn(decoded(arrived))


def turned(arrived):
    return pl.pallas_call(
        turn_kernel,
        out_shape=jax.ShapeDtypeStruct((arrived.shape[0], WIDTH), jnp.float32),
        compiler_params=params(12),
        cost_estimate=pl.CostEstimate(flops=2 * 10**9, bytes_accessed=10**6, transcendentals=0),
        name="turn",
    )(arrived)


def planes_of(side):
    return [lookup([planes[step] for planes in PLANES], side) for step in range(4)]


def sort_own_kernel(steps, place, pair, mine, *refs):
    own, sems = refs[-2:]
    for n, (step, across) in enumerate(steps):

        @pl.when(planes_of(place[0] // NX)[step] == place[1])
        def _(n=n, across=across):
            rows = pl.ds(n * HALF, HALF)
            to = pl.ds(pl.multiple_of((place[0] % NX ^ across) * HALF, HALF), HALF)
            copies = [
                pltpu.make_async_copy(pair.at[0, rows], own.at[0, to], sems.at[0]),
                pltpu.make_async_copy(mine.at[rows], own.at[1, to], sems.at[1]),
                pltpu.make_async_copy(pair.at[pl.ds(2, 2), rows], own.at[pl.ds(2, 2), to], sems.at[2]),
            ]
            for copy in copies:
                copy.start()
            for copy in copies:
                copy.wait()


def sort_owed_kernel(steps, place, pair, *refs):
    owed, buffer, sem = refs[-3:]
    ((n, step),) = steps

    @pl.when(planes_of(place[0] // NX)[step] == place[1] ^ 2)
    def _():
        put_coded(buffer, pair[1:, n * HALF : (n + 1) * HALF])
        copy = pltpu.make_async_copy(buffer, owed, sem)
        copy.start()
        copy.wait()


def sort(kernel, shape, scratch, place, steps, values, before):
    vmem = pl.BlockSpec(memory_space=pltpu.VMEM)
    hbm = pl.BlockSpec(memory_space=pl.ANY)
    before = [] if before is None else [before]
    return pl.pallas_call(
        functools.partial(kernel, steps),
        in_specs=[pl.BlockSpec(memory_space=pltpu.SMEM)] + [vmem] * len(values) + [hbm] * len(before),
        out_specs=hbm,
        out_shape=jax.ShapeDtypeStruct(shape, jnp.float32),
        scratch_shapes=scratch,
        input_output_aliases={1 + len(values): 0} if before else {},
        compiler_params=params(10),
        cost_estimate=light(),
        name="sort",
    )(place, *values, *before)


def sort_own(place, steps, pair, mine, before=None):
    return sort(sort_own_kernel, (4, PART, WIDTH), [pltpu.SemaphoreType.DMA((3,))], place, steps, (pair, mine), before)


def sort_owed(place, step, pair, before=None, across=0):
    n = next(n for chunk in CHUNKS for n, block in enumerate(chunk) if block == (step, across))
    scratch = [pltpu.VMEM((3, HALF, WIDTH + LANES), jnp.float32), pltpu.SemaphoreType.DMA]
    return sort(sort_owed_kernel, (3, HALF, WIDTH + LANES), scratch, place, ((n, step),), (pair,), before)


def place_rest(place, ref, rest, across):
    rows = pl.ds(pl.multiple_of((place[0] % NX ^ across) * HALF, HALF), HALF)
    for came, distance in enumerate((0, 1, 3)):
        ref[distance ^ 2 ^ place[1], rows, :] += decoded(rest.at[came])


def places(place, step, across):
    x = place[0] % NX ^ across
    plane = planes_of(place[0] // NX ^ 2)[step]
    return plane, [pl.ds(pl.multiple_of(to * HALF + x * 16, 16), 16) for to in range(NX)]


def gather_kernel(place, own, rest, *refs):
    out = refs[-1]
    for part, distance in enumerate((2, 0, 1, 3)):
        out[distance ^ place[1]] = own[part]
    place_rest(place, out, rest, 0)
    for steps, ref in zip(CHUNKS, refs[:-1]):
        for n, (step, across) in enumerate(steps):
            plane, rows = places(place, step, across)
            for to in range(NX):
                out[plane, rows[to], :] += ref[pl.ds(n * HALF + to * 16, 16), :]


def gather(place, own, rest, done):
    vmem = pl.BlockSpec(memory_space=pltpu.VMEM)
    return pl.pallas_call(
        gather_kernel,
        in_specs=[pl.BlockSpec(memory_space=pltpu.SMEM)] + [vmem] * (2 + len(done)),
        out_specs=vmem,
        out_shape=jax.ShapeDtypeStruct((4, PART, WIDTH), jnp.float32),
        compiler_params=params(14),
        cost_estimate=light(),
        name="gather",
    )(place, own, rest, *done)


def finish_kernel(place, sums, rest, last, out, all_sums, total):
    all_sums[...] = sums[...]
    place_rest(place, all_sums, rest, 1)
    value = turn(decoded(last))
    for n, (step, across) in enumerate(CHUNKS[-1]):
        plane, rows = places(place, step, across)
        for to in range(NX):
            start = n * HALF + to * 16
            all_sums[plane, rows[to], :] += value[start : start + 16]
    total[...] = all_sums[...].astype(jnp.bfloat16)
    natural = natural_order()
    value = total[...].reshape(OWNED, WIDTH)
    for p in range(PANELS):
        cut = slice(p * TP, (p + 1) * TP)
        out[:, cut] = matmul(natural, value[:, cut]).astype(jnp.bfloat16)


def finish(place, sums, rest, last):
    vmem = pl.BlockSpec(memory_space=pltpu.VMEM)
    return pl.pallas_call(
        finish_kernel,
        in_specs=[pl.BlockSpec(memory_space=pltpu.SMEM), vmem, vmem, vmem],
        out_specs=vmem,
        out_shape=jax.ShapeDtypeStruct((OWNED, WIDTH), jnp.bfloat16),
        scratch_shapes=[pltpu.VMEM((4, PART, WIDTH), jnp.float32), pltpu.VMEM((4, PART, WIDTH), jnp.bfloat16)],
        compiler_params=params(14),
        cost_estimate=light(),
        name="finish",
    )(place, sums, rest, last)


def coded(value):
    largest = value
    while largest.ndim > 0 and largest.shape != (1,) * value.ndim:
        axis = next(n for n, size in enumerate(largest.shape) if size > 1)
        largest = jnp.max(jnp.abs(largest), axis=axis, keepdims=True)
    power = jnp.ceil(jnp.log2(jnp.maximum(largest, 1e-30)))
    scaled = value * jnp.exp2(7 - power)
    return scaled * jnp.abs(scaled), jnp.broadcast_to(power, (*value.shape[:-1], LANES))


def put_coded(ref, value):
    ref[..., :WIDTH], ref[..., WIDTH:] = coded(value)


def decoded(ref):
    value = ref[..., :WIDTH]
    power = ref[..., WIDTH : WIDTH + 1]
    root = jnp.sqrt(jnp.abs(value)) * jnp.exp2(power - 7)
    return jnp.where(value < 0, -root, root)


def wire(value):
    return value.astype(WIRE)


def unwire(value):
    return value.astype(jnp.float32)


def small_kernel(kernel, shapes, mib, name):
    vmem = pl.BlockSpec(memory_space=pltpu.VMEM)
    shapes = [jax.ShapeDtypeStruct(shape, jnp.float32) for shape in shapes]
    return pl.pallas_call(
        kernel,
        out_specs=[vmem] * len(shapes),
        out_shape=shapes,
        compiler_params=params(mib),
        cost_estimate=light(),
        name=name,
    )


def add_cores_kernel(part, sibling, pair, out):
    for n in (0, 1, 2, 3):
        pair[n] = part[n] + sibling[3 - n]
    put_coded(out, pair[0])


def add_cores(part):
    call = small_kernel(add_cores_kernel, [part.shape, (part.shape[1], WIDTH + LANES)], 12, "add_cores")
    return call(part, across_core(part))


def add_chips_kernel(pair, over, mine, out):
    mine[...] = pair[1] + decoded(over)
    put_coded(out, mine[...])


def add_chips(pair, over):
    call = small_kernel(add_chips_kernel, [pair.shape[1:], over.shape], 8, "add_chips")
    return call(pair, unwire(over))


def together(*values):
    return lax.optimization_barrier(values)


def on_device(amplitudes, integrals, tile_irrep, product_pairs, summed_pairs):
    row, col = lax.axis_index("row"), lax.axis_index("col")
    z = row // NX
    place = jnp.stack([row, col]).astype(jnp.int32)
    tables = (place, tile_irrep, product_pairs, summed_pairs)
    inner = (z == 1) | (z == 2)
    outward = {0: 1, 1: 0, 2: 3, 3: 2}
    inward = {1: 2, 2: 1}

    here0 = amplitudes
    beside0 = across_x(here0)
    here1 = along_z(here0, outward)
    middle = along_z(here0, inward)
    part0 = partial_ladder(tables, integrals, here0)
    beside0, here1, middle, part0 = together(beside0, here1, middle, part0)

    beside1 = across_x(here1)
    crossed = along_z(here1, inward)
    here2 = along_z(middle, outward)
    pair0, sent = add_cores(part0)
    over0 = across_y(wire(sent))
    part1 = partial_ladder(tables, integrals, beside0, here1)
    beside1, crossed, here2, pair0, over0, part1 = together(beside1, crossed, here2, pair0, over0, part1)
    here2 = jnp.where(inner, middle, here2)

    beside2 = across_x(here2)
    here3 = along_z(crossed, outward)
    mine0, sent = add_chips(pair0, over0)
    other0 = to_partner(wire(sent))
    pair1, sent = add_cores(part1)
    over1 = across_y(wire(sent))
    part2 = partial_ladder(tables, integrals, beside1, here2)
    own = sort_own(place, CHUNKS[0], pair0, mine0)
    owed_here = sort_owed(place, 0, pair0)
    beside2, here3, other0, own, owed_here, pair1, over1, part2 = together(
        beside2, here3, other0, own, owed_here, pair1, over1, part2
    )
    here3 = jnp.where(inner, crossed, here3)

    beside3 = across_x(here3)
    mine1, sent = add_chips(pair1, over1)
    other1 = to_partner(wire(sent))
    pair2, sent = add_cores(part2)
    over2 = across_y(wire(sent))
    part3 = partial_ladder(tables, integrals, beside2, here3)
    own = sort_own(place, CHUNKS[1], pair1, mine1, own)
    owed_beside = sort_owed(place, 0, pair1, across=1)
    owed_here = sort_owed(place, 1, pair1, owed_here)
    beside3, other0, other1, own, owed_here, owed_beside, pair2, over2, part3 = together(
        beside3, other0, other1, own, owed_here, owed_beside, pair2, over2, part3
    )

    mine2, sent = add_chips(pair2, over2)
    other2 = to_partner(wire(sent))
    pair3, sent = add_cores(part3)
    over3 = across_y(wire(sent))
    part4 = partial_ladder(tables, integrals, beside3)
    own = sort_own(place, CHUNKS[2], pair2, mine2, own)
    owed_beside = sort_owed(place, 1, pair2, owed_beside, across=1)
    owed_here = sort_owed(place, 2, pair2, owed_here)
    owed_beside = sort_owed(place, 2, pair3, owed_beside, across=1)
    owed_here = wire(sort_owed(place, 3, pair3, owed_here))
    other0, other1, other2, own, owed_here, owed_beside, pair3, over3, part4 = together(
        other0, other1, other2, own, owed_here, owed_beside, pair3, over3, part4
    )

    mine3, sent = add_chips(pair3, over3)
    sent, owed_here = together(wire(sent), owed_here)
    other3 = to_partner(sent)
    came_here = across_y(owed_here)
    pair4, sent = add_cores(part4)
    over4 = across_y(wire(sent))
    own = sort_own(place, CHUNKS[3], pair3, mine3, own)
    owed_beside = wire(sort_owed(place, 3, pair4, owed_beside, across=1))
    other0, other1, other2, other3, own, came_here, pair4, over4 = together(
        other0, other1, other2, other3, own, came_here, pair4, over4
    )

    mine4, sent = add_chips(pair4, over4)
    sent, *others = together(sent, other0, other1, other2, other3)
    other4 = to_partner(wire(sent))
    came_beside = across_y(owed_beside)
    own = sort_own(place, CHUNKS[4], pair4, mine4, own)
    done = [turned(unwire(other)) for other in others]
    sums = gather(place, own, unwire(came_here), done)
    return finish(place, sums, unwire(came_beside), unwire(other4))


def solution(mesh):
    body = on_device if (mesh.shape["row"], mesh.shape["col"]) == (NZ * NX, NY * NC) else plain
    return jax.shard_map(
        body,
        mesh=mesh,
        in_specs=(P("row", "col"), P("col", "row"), P(), P("row", None), P("col", None)),
        out_specs=P("col", "row"),
        check_vma=False,
    )
```

time: 127 us -> 121 us (0.953)
  waiting for transfers between devices: 49.8 us -> 38.8 us
  Pallas kernels: 31 us -> 35.1 us
    ppermute x23 -> x26, waiting for transfers between devices: 49.8 us -> 38.8 us  [send(): return lax.ppermute(value, ('row', 'col'), pairs)]
    pallas_call x13 -> x18, Pallas kernels: 10.2 us -> 12.8 us  [the longest x13 8.87 us: sort(): pl.pallas_call(functools.partial(kernel, steps), in_specs=[pl.BlockSpec(m...]
    ppermute x23 -> x26, starting transfers between devices: 30.8 us -> 31.8 us  [send(): return lax.ppermute(value, ('row', 'col'), pairs)]
    pallas_call x4 -> x5, Pallas kernels: 13.3 us -> 14.3 us  [partial_ladder(): pl.pallas_call(ladder_kernel, in_specs=[pl.BlockSpec(memory_space=pltpu.S...]
    pallas_call x4 -> x5, Pallas kernels: 3.1 us -> 3.24 us  [add_cores(): return call(part, across_core(part))]
    unnamed x20 -> x32, local copies, waits for them, and re-layouts: 11.8 us -> 11.9 us
  transfers between devices with their start and end apart: 23 -> 26, of which waited for: 14 -> 12; matrix products, arithmetic and copies ran while one was open for 3% -> 3% of each run, Pallas kernels for 22% -> 27%
where the time goes in v3:
time: 121 us; the launch traced here: 120 us
  waiting for transfers between devices  38.8 us (32%)
  Pallas kernels  35.1 us (29%)
  starting transfers between devices  31.8 us (26%)
  local copies, waits for them, and re-layouts  11.9 us (10%)
  other arithmetic  2.03 us (2%)
    ppermute x26, waiting for transfers between devices, send(): return lax.ppermute(value, ('row', 'col'), pairs)  38.8 us
    ppermute x26, starting transfers between devices, send(): return lax.ppermute(value, ('row', 'col'), pairs)  31.8 us
    pallas_call x5, Pallas kernels, partial_ladder(): pl.pallas_call(ladder_kernel, in_specs=[pl.BlockSpec(memory_space=pltpu.S...  14.3 us
    unnamed x32, local copies, waits for them, and re-layouts  11.9 us
    pallas_call x13, Pallas kernels, sort(): pl.pallas_call(functools.partial(kernel, steps), in_specs=[pl.BlockSpec(m...  8.87 us
    pallas_call x5, Pallas kernels, add_cores(): return call(part, across_core(part))  3.24 us
    pallas_call x1, Pallas kernels, finish(): pl.pallas_call(finish_kernel, in_specs=[pl.BlockSpec(memory_space=pltpu.S...  2.92 us
    pallas_call x4, Pallas kernels, turned(): pl.pallas_call(turn_kernel, out_shape=jax.ShapeDtypeStruct((arrived.shape...  2.67 us
  transfers between devices with their start and end apart: 26, of which 12 were waited for; matrix products, arithmetic and copies ran while one was open for 3% of the time, Pallas kernels for 27%

profile of v3, /device:TPU:0, one launch (start us, length us, event | category | flops | bytes accessed | tf_op | source)
XLA Modules:
  0.0 120.3 jit_solution(14522236311956830880)
XLA Ops:
  0.0 3.0 %collective-permute-start.1 = (bf16[128,2048]{1,0:T(8,128)(2,1)}, bf16[128,2048]{1,0:T(8,128)(2,1)}, u32[]{:S(2)}, u32[]{:S(2)}) collective-permute-start(bf16[128,2048]{1,0:T(8,128)(2,1)} %refs_0_.1), channel_id=1, source_target_pairs={{0,8},{1,9},{2,10},{3,11},{4,12},{5,13},{6,14},{7,15},{8,0},{9,1},... | collective-permute-start | bytes 1572872 | tf_op jit(solution)/shard_map/ppermute | solution.py:108
  3.0 1.5 %collective-permute-start = (bf16[128,2048]{1,0:T(8,128)(2,1)}, bf16[128,2048]{1,0:T(8,128)(2,1)S(1)}, u32[]{:S(2)}, u32[]{:S(2)}) collective-permute-start(bf16[128,2048]{1,0:T(8,128)(2,1)} %refs_0_.1), channel_id=1, source_target_pairs={{0,4},{1,5},{2,6},{3,7},{4,0},{5,1},{6,2},{7,3},{8,12},{9,13},{10,... | collective-permute-start | bytes 1572872 | tf_op jit(solution)/shard_map/ppermute | solution.py:108
  4.5 1.5 %collective-permute-start.2 = (bf16[128,2048]{1,0:T(8,128)(2,1)}, bf16[128,2048]{1,0:T(8,128)(2,1)}, u32[]{:S(2)}, u32[]{:S(2)}) collective-permute-start(bf16[128,2048]{1,0:T(8,128)(2,1)} %refs_0_.1), channel_id=1, source_target_pairs={{8,16},{9,17},{10,18},{11,19},{12,20},{13,21},{14,22},{15,23},{16,... | collective-permute-start | bytes 1572872 | tf_op jit(solution)/shard_map/ppermute | solution.py:108
  6.0 0.8 copy.16.product
  6.7 0.8 copy.17.summed
  7.6 3.4 %copy-done = bf16[2048,2048]{1,0:T(8,128)(2,1)S(1)} copy-done((bf16[2048,2048]{1,0:T(8,128)(2,1)S(1)}, bf16[2048,2048]{1,0:T(8,128)(2,1)}, u32[]{:S(2)}) %copy-start) | copy-done | bytes 8388632
  10.9 1.0 copy-done.3
  12.6 2.1 %partial_ladder.5.part = f32[4,32,2048]{2,1,0:T(8,128)S(1)} custom-call(s32[2]{0:T(128)S(1)} %pad_add_fusion.place, s32[24]{0:T(128)S(1)} %copy-done.8, s32[8,2]{1,0:T(8,128)S(1)} %copy.16.product, s32[8,2]{1,0:T(8,128)S(1)} %copy.17.summed, bf16[128,2048]{1,0:T(8,128)(2,1)S(1)} %copy-done.3, bf16[2048,2048]{1,0:T(8,128)(2,1)S(1)} %copy-done), custom_call_target="tpu_custom_call" | custom-call | flops 1000 | bytes 1000 | tf_op jit(solution)/shard_map/partial_ladder/pallas_call | solution.py:164
  15.3 1.4 %collective-permute-done.refs_0_ = bf16[128,2048]{1,0:T(8,128)(2,1)S(1)} collective-permute-done((bf16[128,2048]{1,0:T(8,128)(2,1)}, bf16[128,2048]{1,0:T(8,128)(2,1)S(1)}, u32[]{:S(2)}, u32[]{:S(2)}) %collective-permute-start) | collective-permute-done | bytes 524320 | tf_op jit(solution)/shard_map/ppermute | solution.py:108
  16.6 0.8 copy-done.6
  17.4 3.8 %collective-permute-start.5 = (bf16[128,2048]{1,0:T(8,128)(2,1)}, bf16[128,2048]{1,0:T(8,128)(2,1)S(1)}, u32[]{:S(2)}, u32[]{:S(2)}) collective-permute-start(bf16[128,2048]{1,0:T(8,128)(2,1)} %collective-permute-done.2), channel_id=1, source_target_pairs={{0,8},{1,9},{2,10},{3,11},{4,12},{5,13},{6,14},{7,15},{8,0},{9,1},... | collective-permute-start | bytes 1572872 | tf_op jit(solution)/shard_map/ppermute | solution.py:108
  21.2 0.7 collective-permute-start.4
  22.8 1.6 %collective-permute-start.7 = (f16[32,2176]{1,0:T(8,128)(2,1)S(1)}, f16[32,2176]{1,0:T(8,128)(2,1)S(1)}, u32[]{:S(2)}, u32[]{:S(2)}) collective-permute-start(f16[32,2176]{1,0:T(8,128)(2,1)S(1)} %convert_element_type.72), channel_id=1, source_target_pairs={{0,2},{1,3},{2,0},{3,1},{4,6},{5,7},{6,4},{7,5},{8,10},{9,11},{10,... | collective-permute-start | bytes 417800 | tf_op jit(solution)/shard_map/ppermute | solution.py:108
  24.4 3.7 %partial_ladder.6.part = f32[4,64,2048]{2,1,0:T(8,128)S(1)} custom-call(s32[2]{0:T(128)S(1)} %pad_add_fusion.place, s32[24]{0:T(128)S(1)} %copy-done.8, s32[8,2]{1,0:T(8,128)S(1)} %copy.16.product, s32[8,2]{1,0:T(8,128)S(1)} %copy.17.summed, bf16[128,2048]{1,0:T(8,128)(2,1)S(1)} %copy-done.7, bf16[128,2048]{1,0:T(8,128)(2,1)} %collective-permute-done.1.refs_1_, ...), custom_call_target="tpu_custom_call" | custom-call | flops 1000 | bytes 1000 | tf_op jit(solution)/shard_map/partial_ladder/pallas_call | solution.py:164
  28.1 6.0 %collective-permute-done.5 = bf16[128,2048]{1,0:T(8,128)(2,1)S(1)} collective-permute-done((bf16[128,2048]{1,0:T(8,128)(2,1)}, bf16[128,2048]{1,0:T(8,128)(2,1)S(1)}, u32[]{:S(2)}, u32[]{:S(2)}) %collective-permute-start.5) | collective-permute-done | bytes 524320 | tf_op jit(solution)/shard_map/ppermute | solution.py:108
  34.1 2.2 %collective-permute-done.3.refs_0_ = bf16[128,2048]{1,0:T(8,128)(2,1)S(1)} collective-permute-done((bf16[128,2048]{1,0:T(8,128)(2,1)}, bf16[128,2048]{1,0:T(8,128)(2,1)S(1)}, u32[]{:S(2)}, u32[]{:S(2)}) %collective-permute-start.3) | collective-permute-done | bytes 524320 | tf_op jit(solution)/shard_map/ppermute | solution.py:108
  36.3 0.8 copy-done.4
  37.2 1.1 broadcast_select_fusion.1.refs_1_
  38.9 2.9 %collective-permute-start.9 = (bf16[128,2048]{1,0:T(8,128)(2,1)}, bf16[128,2048]{1,0:T(8,128)(2,1)S(1)}, u32[]{:S(2)}, u32[]{:S(2)}) collective-permute-start(bf16[128,2048]{1,0:T(8,128)(2,1)} %copy-done.10), channel_id=1, source_target_pairs={{0,8},{1,9},{2,10},{3,11},{4,12},{5,13},{6,14},{7,15},{8,0},{9,1},... | collective-permute-start | bytes 1572872 | tf_op jit(solution)/shard_map/ppermute | solution.py:108
  41.8 2.0 %add_cores.6 = (f32[4,64,2048]{2,1,0:T(8,128)S(1)}, f32[64,2176]{1,0:T(8,128)S(1)}) custom-call(f32[4,64,2048]{2,1,0:T(8,128)S(1)} %partial_ladder.6.part, f32[4,64,2048]{2,1,0:T(8,128)} %collective-permute-done.11.sibling), custom_call_target="tpu_custom_call" | custom-call | flops 1000 | bytes 1000 | tf_op jit(solution)/shard_map/add_cores/pallas_call | solution.py:382
  43.9 1.6 %collective-permute-start.12 = (f16[64,2176]{1,0:T(8,128)(2,1)S(1)}, f16[64,2176]{1,0:T(8,128)(2,1)S(1)}, u32[]{:S(2)}, u32[]{:S(2)}) collective-permute-start(f16[64,2176]{1,0:T(8,128)(2,1)S(1)} %convert_element_type.75), channel_id=1, source_target_pairs={{0,2},{1,3},{2,0},{3,1},{4,6},{5,7},{6,4},{7,5},{8,10},{9,11},{10,... | collective-permute-start | bytes 835592 | tf_op jit(solution)/shard_map/ppermute | solution.py:108
  45.8 2.4 %collective-permute-start.10 = (f16[32,2176]{1,0:T(8,128)(2,1)S(1)}, f16[32,2176]{1,0:T(8,128)(2,1)S(1)}, u32[]{:S(2)}, u32[]{:S(2)}) collective-permute-start(f16[32,2176]{1,0:T(8,128)(2,1)S(1)} %convert_element_type.74), channel_id=1, source_target_pairs={{0,16},{1,17},{2,18},{3,19},{4,20},{5,21},{6,22},{7,23},{8,24},{9,... | collective-permute-start | bytes 417800 | tf_op jit(solution)/shard_map/ppermute | solution.py:108
  49.8 3.4 %copy-done.2 = bf16[2048,2048]{1,0:T(8,128)(2,1)S(1)} copy-done((bf16[2048,2048]{1,0:T(8,128)(2,1)S(1)}, bf16[2048,2048]{1,0:T(8,128)(2,1)}, u32[]{:S(2)}) %copy-start.2) | copy-done | bytes 8388632
  53.2 3.3 %partial_ladder.7.part = f32[4,64,2048]{2,1,0:T(8,128)S(1)} custom-call(s32[2]{0:T(128)S(1)} %pad_add_fusion.place, s32[24]{0:T(128)S(1)} %copy-done.9, s32[8,2]{1,0:T(8,128)S(1)} %copy.16.product, s32[8,2]{1,0:T(8,128)S(1)} %copy.17.summed, bf16[128,2048]{1,0:T(8,128)(2,1)S(1)} %copy-done.5, bf16[128,2048]{1,0:T(8,128)(2,1)S(1)} %broadcast_select_fusion.1.refs_1_, ...), custom_call_target="tpu_custom_call" | custom-call | flops 1000 | bytes 1000 | tf_op jit(solution)/shard_map/partial_ladder/pallas_call | solution.py:164
  56.6 0.7 collective-permute-done.9
  57.4 1.6 %collective-permute-start.13 = (bf16[128,2048]{1,0:T(8,128)(2,1)S(1)}, bf16[128,2048]{1,0:T(8,128)(2,1)S(1)}, u32[]{:S(2)}, u32[]{:S(2)}) collective-permute-start(bf16[128,2048]{1,0:T(8,128)(2,1)S(1)} %broadcast_select_fusion.refs_1_), channel_id=1, source_target_pairs={{0,4},{1,5},{2,6},{3,7},{4,0},{5,1},{6,2},{7,3},{8,12},{9,13},{10,... | collective-permute-start | bytes 1572872 | tf_op jit(solution)/shard_map/ppermute | solution.py:108
  59.5 2.8 %collective-permute-start.14 = (f16[64,2176]{1,0:T(8,128)(2,1)S(1)}, f16[64,2176]{1,0:T(8,128)(2,1)S(1)}, u32[]{:S(2)}, u32[]{:S(2)}) collective-permute-start(f16[64,2176]{1,0:T(8,128)(2,1)S(1)} %convert_element_type.77), channel_id=1, source_target_pairs={{0,16},{1,17},{2,18},{3,19},{4,20},{5,21},{6,22},{7,23},{8,24},{9,... | collective-permute-start | bytes 835592 | tf_op jit(solution)/shard_map/ppermute | solution.py:108
  62.7 1.6 %collective-permute-start.16 = (f16[64,2176]{1,0:T(8,128)(2,1)S(1)}, f16[64,2176]{1,0:T(8,128)(2,1)S(1)}, u32[]{:S(2)}, u32[]{:S(2)}) collective-permute-start(f16[64,2176]{1,0:T(8,128)(2,1)S(1)} %convert_element_type.78), channel_id=1, source_target_pairs={{0,2},{1,3},{2,0},{3,1},{4,6},{5,7},{6,4},{7,5},{8,10},{9,11},{10,... | collective-permute-start | bytes 835592 | tf_op jit(solution)/shard_map/ppermute | solution.py:108
  64.9 0.7 sort.16.refs_0_
  65.7 3.3 %partial_ladder.8.part = f32[4,64,2048]{2,1,0:T(8,128)S(1)} custom-call(s32[2]{0:T(128)S(1)} %pad_add_fusion.place, s32[24]{0:T(128)S(1)} %copy-done.9, s32[8,2]{1,0:T(8,128)S(1)} %copy.16.product, s32[8,2]{1,0:T(8,128)S(1)} %copy.17.summed, bf16[128,2048]{1,0:T(8,128)(2,1)S(1)} %collective-permute-done.8.refs_0_, ...), custom_call_target="tpu_custom_call" | custom-call | flops 1000 | bytes 1000 | tf_op jit(solution)/shard_map/partial_ladder/pallas_call | solution.py:164
  68.9 0.7 sort.15.refs_0_
  69.6 5.7 %collective-permute-done.14 = f16[64,2176]{1,0:T(8,128)(2,1)S(1)} collective-permute-done((f16[64,2176]{1,0:T(8,128)(2,1)S(1)}, f16[64,2176]{1,0:T(8,128)(2,1)S(1)}, u32[]{:S(2)}, u32[]{:S(2)}) %collective-permute-start.14) | collective-permute-done | bytes 278560 | tf_op jit(solution)/shard_map/ppermute | solution.py:108
  75.9 3.6 %collective-permute-done.18.sibling = f32[4,64,2048]{2,1,0:T(8,128)S(1)} collective-permute-done((f32[4,64,2048]{2,1,0:T(8,128)S(1)}, f32[4,64,2048]{2,1,0:T(8,128)S(1)}, u32[]{:S(2)}, u32[]{:S(2)}) %collective-permute-start.18) | collective-permute-done | bytes 2097184 | tf_op jit(solution)/shard_map/ppermute | solution.py:108
  79.9 1.6 %collective-permute-start.19 = (f16[64,2176]{1,0:T(8,128)(2,1)S(1)}, f16[64,2176]{1,0:T(8,128)(2,1)S(1)}, u32[]{:S(2)}, u32[]{:S(2)}) collective-permute-start(f16[64,2176]{1,0:T(8,128)(2,1)S(1)} %convert_element_type.82), channel_id=1, source_target_pairs={{0,2},{1,3},{2,0},{3,1},{4,6},{5,7},{6,4},{7,5},{8,10},{9,11},{10,... | collective-permute-start | bytes 835592 | tf_op jit(solution)/shard_map/ppermute | solution.py:108
  81.5 1.0 sort.19.refs_0_
  83.0 2.1 %partial_ladder.9.part = f32[4,32,2048]{2,1,0:T(8,128)S(1)} custom-call(s32[2]{0:T(128)S(1)} %pad_add_fusion.place, s32[24]{0:T(128)S(1)} %copy-done.9, s32[8,2]{1,0:T(8,128)S(1)} %copy.16.product, s32[8,2]{1,0:T(8,128)S(1)} %copy.17.summed, bf16[128,2048]{1,0:T(8,128)(2,1)S(1)} %collective-permute-done.13.refs_0_, bf16[2048,2048]{1,0:T(8,128)(2,1)S(1)} %bitcast.3), custom_call_target="tpu_custom_call" | custom-call | flops 1000 | bytes 1000 | tf_op jit(solution)/shard_map/partial_ladder/pallas_call | solution.py:164
  85.7 1.0 sort.22.refs_0_
  87.3 3.2 %collective-permute-done.17 = f16[64,2176]{1,0:T(8,128)(2,1)S(1)} collective-permute-done((f16[64,2176]{1,0:T(8,128)(2,1)S(1)}, f16[64,2176]{1,0:T(8,128)(2,1)S(1)}, u32[]{:S(2)}, u32[]{:S(2)}) %collective-permute-start.17) | collective-permute-done | bytes 278560 | tf_op jit(solution)/shard_map/ppermute | solution.py:108
  91.1 1.6 %collective-permute-start.21 = (f16[3,32,2176]{2,1,0:T(8,128)(2,1)S(1)}, f16[3,32,2176]{2,1,0:T(8,128)(2,1)S(1)}, u32[]{:S(2)}, u32[]{:S(2)}) collective-permute-start(f16[3,32,2176]{2,1,0:T(8,128)(2,1)S(1)} %convert_element_type.81), channel_id=1, source_target_pairs={{0,2},{1,3},{2,0},{3,1},{4,6},{5,7},{6,4},{7,5},{8,10},{9,11},{10,... | collective-permute-start | bytes 1253384 | tf_op jit(solution)/shard_map/ppermute | solution.py:108
  93.4 1.6 %collective-permute-start.23 = (f16[32,2176]{1,0:T(8,128)(2,1)S(1)}, f16[32,2176]{1,0:T(8,128)(2,1)S(1)}, u32[]{:S(2)}, u32[]{:S(2)}) collective-permute-start(f16[32,2176]{1,0:T(8,128)(2,1)S(1)} %convert_element_type.85), channel_id=1, source_target_pairs={{0,2},{1,3},{2,0},{3,1},{4,6},{5,7},{6,4},{7,5},{8,10},{9,11},{10,... | collective-permute-start | bytes 417800 | tf_op jit(solution)/shard_map/ppermute | solution.py:108
  96.9 11.2 %collective-permute-done.20 = f16[64,2176]{1,0:T(8,128)(2,1)S(1)} collective-permute-done((f16[64,2176]{1,0:T(8,128)(2,1)S(1)}, f16[64,2176]{1,0:T(8,128)(2,1)S(1)}, u32[]{:S(2)}, u32[]{:S(2)}) %collective-permute-start.20) | collective-permute-done | bytes 278560 | tf_op jit(solution)/shard_map/ppermute | solution.py:108
  109.1 0.7 turn.5.refs_1_
  109.8 0.8 sort.24.own
  110.8 0.7 turn.6.refs_2_
  111.5 0.7 turn.7.refs_3_
  112.3 1.3 %gather.1.sums = f32[4,64,2048]{2,1,0:T(8,128)S(1)} custom-call(s32[2]{0:T(128)S(1)} %pad_add_fusion.place, f32[4,64,2048]{2,1,0:T(8,128)S(1)} %sort.24.own, f32[3,32,2176]{2,1,0:T(8,128)S(1)} %convert_element_type.87.rest, f32[32,2048]{1,0:T(8,128)S(1)} %turn.4.refs_0_, f32[64,2048]{1,0:T(8,128)S(1)} %turn.5.refs_1_, f32[64,2048]{1,0:T(8,128)S(1)} %turn.6.refs_2_, ...), custom_call_target="tpu_custom_call" | custom-call | flops 1000 | bytes 1000 | tf_op jit(solution)/shard_map/gather/pallas_call | solution.py:290
  113.6 3.7 %collective-permute-done.25 = f16[32,2176]{1,0:T(8,128)(2,1)S(1)} collective-permute-done((f16[32,2176]{1,0:T(8,128)(2,1)S(1)}, f16[32,2176]{1,0:T(8,128)(2,1)S(1)}, u32[]{:S(2)}, u32[]{:S(2)}) %collective-permute-start.25) | collective-permute-done | bytes 139296 | tf_op jit(solution)/shard_map/ppermute | solution.py:108
  117.4 2.9 %finish.1 = bf16[256,2048]{1,0:T(8,128)(2,1)} custom-call(s32[2]{0:T(128)S(1)} %pad_add_fusion.place, f32[4,64,2048]{2,1,0:T(8,128)S(1)} %gather.1.sums, f32[3,32,2176]{2,1,0:T(8,128)S(1)} %convert_element_type.93.rest, f32[32,2176]{1,0:T(8,128)S(1)} %convert_element_type.95.last), custom_call_target="tpu_custom_call" | custom-call | flops 1000 | bytes 1000 | tf_op jit(solution)/shard_map/finish/pallas_call | solution.py:320
  (98 shorter events, 13.6 us)
Async XLA Ops:
  0.0 15.3 %collective-permute-start.1 = (bf16[128,2048]{1,0:T(8,128)(2,1)}, bf16[128,2048]{1,0:T(8,128)(2,1)}, u32[]{:S(2)}, u32[]{:S(2)}) collective-permute-start(bf16[128,2048]{1,0:T(8,128)(2,1)} %refs_0_.1), channel_id=1, source_target_pairs={{0,8},{1,9},{2,10},{3,11},{4,12},{5,13},{6,14},{7,15},{8,0},{9,1},... | collective-permute-start | bytes 1572872 | tf_op jit(solution)/shard_map/ppermute | solution.py:108
  3.0 13.6 %collective-permute-start = (bf16[128,2048]{1,0:T(8,128)(2,1)}, bf16[128,2048]{1,0:T(8,128)(2,1)S(1)}, u32[]{:S(2)}, u32[]{:S(2)}) collective-permute-start(bf16[128,2048]{1,0:T(8,128)(2,1)} %refs_0_.1), channel_id=1, source_target_pairs={{0,4},{1,5},{2,6},{3,7},{4,0},{5,1},{6,2},{7,3},{8,12},{9,13},{10,... | collective-permute-start | bytes 1572872 | tf_op jit(solution)/shard_map/ppermute | solution.py:108
  4.5 12.9 %collective-permute-start.2 = (bf16[128,2048]{1,0:T(8,128)(2,1)}, bf16[128,2048]{1,0:T(8,128)(2,1)}, u32[]{:S(2)}, u32[]{:S(2)}) collective-permute-start(bf16[128,2048]{1,0:T(8,128)(2,1)} %refs_0_.1), channel_id=1, source_target_pairs={{8,16},{9,17},{10,18},{11,19},{12,20},{13,21},{14,22},{15,23},{16,... | collective-permute-start | bytes 1572872 | tf_op jit(solution)/shard_map/ppermute | solution.py:108
  7.6 3.4 %copy-start = (bf16[2048,2048]{1,0:T(8,128)(2,1)S(1)}, bf16[2048,2048]{1,0:T(8,128)(2,1)}, u32[]{:S(2)}) copy-start(bf16[2048,2048]{1,0:T(8,128)(2,1)} %refs_1_.3) | copy-start | bytes 25165828
  10.9 1.0 copy-start.3
  12.0 0.7 copy-start.8
  12.6 11.8 %copy-start.1 = (bf16[2048,2048]{1,0:T(8,128)(2,1)S(1)}, bf16[2048,2048]{1,0:T(8,128)(2,1)}, u32[]{:S(2)}) copy-start(bf16[2048,2048]{1,0:T(8,128)(2,1)} %refs_1_.3) | copy-start | bytes 25165828
  16.6 0.8 copy-start.6
  17.4 7.0 %copy-start.7 = (bf16[128,2048]{1,0:T(8,128)(2,1)S(1)}, bf16[128,2048]{1,0:T(8,128)(2,1)}, u32[]{:S(2)}) copy-start(bf16[128,2048]{1,0:T(8,128)(2,1)} %copy-done.6) | copy-start | bytes 1572868
  17.4 5.1 %collective-permute-start.6 = (f32[4,32,2048]{2,1,0:T(8,128)S(1)}, f32[4,32,2048]{2,1,0:T(8,128)S(1)}, u32[]{:S(2)}, u32[]{:S(2)}) collective-permute-start(f32[4,32,2048]{2,1,0:T(8,128)S(1)} %partial_ladder.5.part), channel_id=1, source_target_pairs={{0,1},{1,0},{2,3},{3,2},{4,5},{5,4},{6,7},{7,6},{8,9},{9,8},{10,11... | collective-permute-start | bytes 3145736 | tf_op jit(solution)/shard_map/ppermute | solution.py:108
  17.4 16.6 %collective-permute-start.5 = (bf16[128,2048]{1,0:T(8,128)(2,1)}, bf16[128,2048]{1,0:T(8,128)(2,1)S(1)}, u32[]{:S(2)}, u32[]{:S(2)}) collective-permute-start(bf16[128,2048]{1,0:T(8,128)(2,1)} %collective-permute-done.2), channel_id=1, source_target_pairs={{0,8},{1,9},{2,10},{3,11},{4,12},{5,13},{6,14},{7,15},{8,0},{9,1},... | collective-permute-start | bytes 1572872 | tf_op jit(solution)/shard_map/ppermute | solution.py:108
  21.2 12.8 %collective-permute-start.4 = (bf16[128,2048]{1,0:T(8,128)(2,1)}, bf16[128,2048]{1,0:T(8,128)(2,1)S(1)}, u32[]{:S(2)}, u32[]{:S(2)}) collective-permute-start(bf16[128,2048]{1,0:T(8,128)(2,1)} %collective-permute-done.1.refs_1_), channel_id=1, source_target_pairs={{8,16},{9,17},{10,18},{11,19},{12,20},{13,21},{14,22},{15,23},{16,... | collective-permute-start | bytes 1572872 | tf_op jit(solution)/shard_map/ppermute | solution.py:108
  21.9 14.3 %collective-permute-start.3 = (bf16[128,2048]{1,0:T(8,128)(2,1)}, bf16[128,2048]{1,0:T(8,128)(2,1)S(1)}, u32[]{:S(2)}, u32[]{:S(2)}) collective-permute-start(bf16[128,2048]{1,0:T(8,128)(2,1)} %collective-permute-done.1.refs_1_), channel_id=1, source_target_pairs={{0,4},{1,5},{2,6},{3,7},{4,0},{5,1},{6,2},{7,3},{8,12},{9,13},{10,... | collective-permute-start | bytes 1572872 | tf_op jit(solution)/shard_map/ppermute | solution.py:108
  22.8 14.2 %collective-permute-start.7 = (f16[32,2176]{1,0:T(8,128)(2,1)S(1)}, f16[32,2176]{1,0:T(8,128)(2,1)S(1)}, u32[]{:S(2)}, u32[]{:S(2)}) collective-permute-start(f16[32,2176]{1,0:T(8,128)(2,1)S(1)} %convert_element_type.72), channel_id=1, source_target_pairs={{0,2},{1,3},{2,0},{3,1},{4,6},{5,7},{6,4},{7,5},{8,10},{9,11},{10,... | collective-permute-start | bytes 417800 | tf_op jit(solution)/shard_map/ppermute | solution.py:108
  34.0 3.0 %copy-start.12 = (bf16[128,2048]{1,0:T(8,128)(2,1)}, bf16[128,2048]{1,0:T(8,128)(2,1)S(1)}, u32[]{:S(2)}) copy-start(bf16[128,2048]{1,0:T(8,128)(2,1)S(1)} %collective-permute-done.5) | copy-start | bytes 1572868
  34.1 3.0 %copy-start.10 = (bf16[128,2048]{1,0:T(8,128)(2,1)}, bf16[128,2048]{1,0:T(8,128)(2,1)S(1)}, u32[]{:S(2)}) copy-start(bf16[128,2048]{1,0:T(8,128)(2,1)S(1)} %collective-permute-done.4) | copy-start | bytes 1572868
  36.3 0.8 copy-start.4
  37.1 4.8 %collective-permute-start.11 = (f32[4,64,2048]{2,1,0:T(8,128)S(1)}, f32[4,64,2048]{2,1,0:T(8,128)}, u32[]{:S(2)}, u32[]{:S(2)}) collective-permute-start(f32[4,64,2048]{2,1,0:T(8,128)S(1)} %partial_ladder.6.part), channel_id=1, source_target_pairs={{0,1},{1,0},{2,3},{3,2},{4,5},{5,4},{6,7},{7,6},{8,9},{9,8},{10,11... | collective-permute-start | bytes 6291464 | tf_op jit(solution)/shard_map/ppermute | solution.py:108
  38.3 18.3 %collective-permute-start.8 = (bf16[128,2048]{1,0:T(8,128)(2,1)S(1)}, bf16[128,2048]{1,0:T(8,128)(2,1)S(1)}, u32[]{:S(2)}, u32[]{:S(2)}) collective-permute-start(bf16[128,2048]{1,0:T(8,128)(2,1)S(1)} %broadcast_select_fusion.1.refs_1_), channel_id=1, source_target_pairs={{0,4},{1,5},{2,6},{3,7},{4,0},{5,1},{6,2},{7,3},{8,12},{9,13},{10,... | collective-permute-start | bytes 1572872 | tf_op jit(solution)/shard_map/ppermute | solution.py:108
  38.9 18.4 %collective-permute-start.9 = (bf16[128,2048]{1,0:T(8,128)(2,1)}, bf16[128,2048]{1,0:T(8,128)(2,1)S(1)}, u32[]{:S(2)}, u32[]{:S(2)}) collective-permute-start(bf16[128,2048]{1,0:T(8,128)(2,1)} %copy-done.10), channel_id=1, source_target_pairs={{0,8},{1,9},{2,10},{3,11},{4,12},{5,13},{6,14},{7,15},{8,0},{9,1},... | collective-permute-start | bytes 1572872 | tf_op jit(solution)/shard_map/ppermute | solution.py:108
  43.9 13.4 %collective-permute-start.12 = (f16[64,2176]{1,0:T(8,128)(2,1)S(1)}, f16[64,2176]{1,0:T(8,128)(2,1)S(1)}, u32[]{:S(2)}, u32[]{:S(2)}) collective-permute-start(f16[64,2176]{1,0:T(8,128)(2,1)S(1)} %convert_element_type.75), channel_id=1, source_target_pairs={{0,2},{1,3},{2,0},{3,1},{4,6},{5,7},{6,4},{7,5},{8,10},{9,11},{10,... | collective-permute-start | bytes 835592 | tf_op jit(solution)/shard_map/ppermute | solution.py:108
  45.8 10.8 %collective-permute-start.10 = (f16[32,2176]{1,0:T(8,128)(2,1)S(1)}, f16[32,2176]{1,0:T(8,128)(2,1)S(1)}, u32[]{:S(2)}, u32[]{:S(2)}) collective-permute-start(f16[32,2176]{1,0:T(8,128)(2,1)S(1)} %convert_element_type.74), channel_id=1, source_target_pairs={{0,16},{1,17},{2,18},{3,19},{4,20},{5,21},{6,22},{7,23},{8,24},{9,... | collective-permute-start | bytes 417800 | tf_op jit(solution)/shard_map/ppermute | solution.py:108
  48.8 1.0 copy-start.5
  48.8 1.0 copy-start.9
  49.8 3.4 %copy-start.2 = (bf16[2048,2048]{1,0:T(8,128)(2,1)S(1)}, bf16[2048,2048]{1,0:T(8,128)(2,1)}, u32[]{:S(2)}) copy-start(bf16[2048,2048]{1,0:T(8,128)(2,1)} %refs_1_.3) | copy-start | bytes 25165828
  53.2 4.1 %copy-start.11 = (bf16[128,2048]{1,0:T(8,128)(2,1)S(1)}, bf16[128,2048]{1,0:T(8,128)(2,1)}, u32[]{:S(2)}) copy-start(bf16[128,2048]{1,0:T(8,128)(2,1)} %copy-done.10) | copy-start | bytes 1572868
  57.3 5.0 %collective-permute-start.15 = (f32[4,64,2048]{2,1,0:T(8,128)S(1)}, f32[4,64,2048]{2,1,0:T(8,128)S(1)}, u32[]{:S(2)}, u32[]{:S(2)}) collective-permute-start(f32[4,64,2048]{2,1,0:T(8,128)S(1)} %partial_ladder.7.part), channel_id=1, source_target_pairs={{0,1},{1,0},{2,3},{3,2},{4,5},{5,4},{6,7},{7,6},{8,9},{9,8},{10,11... | collective-permute-start | bytes 6291464 | tf_op jit(solution)/shard_map/ppermute | solution.py:108
  57.4 17.9 %collective-permute-start.13 = (bf16[128,2048]{1,0:T(8,128)(2,1)S(1)}, bf16[128,2048]{1,0:T(8,128)(2,1)S(1)}, u32[]{:S(2)}, u32[]{:S(2)}) collective-permute-start(bf16[128,2048]{1,0:T(8,128)(2,1)S(1)} %broadcast_select_fusion.refs_1_), channel_id=1, source_target_pairs={{0,4},{1,5},{2,6},{3,7},{4,0},{5,1},{6,2},{7,3},{8,12},{9,13},{10,... | collective-permute-start | bytes 1572872 | tf_op jit(solution)/shard_map/ppermute | solution.py:108
  59.0 6.6 %slice-start = ((s8[8388608]{0:T(1024)(128)(4,1)}), s8[4194304]{0:T(1024)(128)(4,1)S(1)}, s32[]{:S(2)}) async-start(s8[8388608]{0:T(1024)(128)(4,1)} %bitcast.2), calls=%async_computation | async-start | bytes 8388608
  59.5 6.2 %slice-start.1 = ((s8[8388608]{0:T(1024)(128)(4,1)}), s8[4194304]{0:T(1024)(128)(4,1)S(1)}, s32[]{:S(2)}) async-start(s8[8388608]{0:T(1024)(128)(4,1)} %bitcast.2), calls=%async_computation.1 | async-start | bytes 8388608
  59.5 15.8 %collective-permute-start.14 = (f16[64,2176]{1,0:T(8,128)(2,1)S(1)}, f16[64,2176]{1,0:T(8,128)(2,1)S(1)}, u32[]{:S(2)}, u32[]{:S(2)}) collective-permute-start(f16[64,2176]{1,0:T(8,128)(2,1)S(1)} %convert_element_type.77), channel_id=1, source_target_pairs={{0,16},{1,17},{2,18},{3,19},{4,20},{5,21},{6,22},{7,23},{8,24},{9,... | collective-permute-start | bytes 835592 | tf_op jit(solution)/shard_map/ppermute | solution.py:108
  62.7 12.6 %collective-permute-start.16 = (f16[64,2176]{1,0:T(8,128)(2,1)S(1)}, f16[64,2176]{1,0:T(8,128)(2,1)S(1)}, u32[]{:S(2)}, u32[]{:S(2)}) collective-permute-start(f16[64,2176]{1,0:T(8,128)(2,1)S(1)} %convert_element_type.78), channel_id=1, source_target_pairs={{0,2},{1,3},{2,0},{3,1},{4,6},{5,7},{6,4},{7,5},{8,10},{9,11},{10,... | collective-permute-start | bytes 835592 | tf_op jit(solution)/shard_map/ppermute | solution.py:108
  75.3 4.2 %collective-permute-start.18 = (f32[4,64,2048]{2,1,0:T(8,128)S(1)}, f32[4,64,2048]{2,1,0:T(8,128)S(1)}, u32[]{:S(2)}, u32[]{:S(2)}) collective-permute-start(f32[4,64,2048]{2,1,0:T(8,128)S(1)} %partial_ladder.8.part), channel_id=1, source_target_pairs={{0,1},{1,0},{2,3},{3,2},{4,5},{5,4},{6,7},{7,6},{8,9},{9,8},{10,11... | collective-permute-start | bytes 6291464 | tf_op jit(solution)/shard_map/ppermute | solution.py:108
  75.8 14.7 %collective-permute-start.17 = (f16[64,2176]{1,0:T(8,128)(2,1)S(1)}, f16[64,2176]{1,0:T(8,128)(2,1)S(1)}, u32[]{:S(2)}, u32[]{:S(2)}) collective-permute-start(f16[64,2176]{1,0:T(8,128)(2,1)S(1)} %convert_element_type.80), channel_id=1, source_target_pairs={{0,16},{1,17},{2,18},{3,19},{4,20},{5,21},{6,22},{7,23},{8,24},{9,... | collective-permute-start | bytes 835592 | tf_op jit(solution)/shard_map/ppermute | solution.py:108
  79.9 10.6 %collective-permute-start.19 = (f16[64,2176]{1,0:T(8,128)(2,1)S(1)}, f16[64,2176]{1,0:T(8,128)(2,1)S(1)}, u32[]{:S(2)}, u32[]{:S(2)}) collective-permute-start(f16[64,2176]{1,0:T(8,128)(2,1)S(1)} %convert_element_type.82), channel_id=1, source_target_pairs={{0,2},{1,3},{2,0},{3,1},{4,6},{5,7},{6,4},{7,5},{8,10},{9,11},{10,... | collective-permute-start | bytes 835592 | tf_op jit(solution)/shard_map/ppermute | solution.py:108
  90.5 2.7 %collective-permute-start.22 = (f32[4,32,2048]{2,1,0:T(8,128)S(1)}, f32[4,32,2048]{2,1,0:T(8,128)S(1)}, u32[]{:S(2)}, u32[]{:S(2)}) collective-permute-start(f32[4,32,2048]{2,1,0:T(8,128)S(1)} %partial_ladder.9.part), channel_id=1, source_target_pairs={{0,1},{1,0},{2,3},{3,2},{4,5},{5,4},{6,7},{7,6},{8,9},{9,8},{10,11... | collective-permute-start | bytes 3145736 | tf_op jit(solution)/shard_map/ppermute | solution.py:108
  91.1 17.0 %collective-permute-start.21 = (f16[3,32,2176]{2,1,0:T(8,128)(2,1)S(1)}, f16[3,32,2176]{2,1,0:T(8,128)(2,1)S(1)}, u32[]{:S(2)}, u32[]{:S(2)}) collective-permute-start(f16[3,32,2176]{2,1,0:T(8,128)(2,1)S(1)} %convert_element_type.81), channel_id=1, source_target_pairs={{0,2},{1,3},{2,0},{3,1},{4,6},{5,7},{6,4},{7,5},{8,10},{9,11},{10,... | collective-permute-start | bytes 1253384 | tf_op jit(solution)/shard_map/ppermute | solution.py:108
  92.7 15.4 %collective-permute-start.20 = (f16[64,2176]{1,0:T(8,128)(2,1)S(1)}, f16[64,2176]{1,0:T(8,128)(2,1)S(1)}, u32[]{:S(2)}, u32[]{:S(2)}) collective-permute-start(f16[64,2176]{1,0:T(8,128)(2,1)S(1)} %convert_element_type.84), channel_id=1, source_target_pairs={{0,16},{1,17},{2,18},{3,19},{4,20},{5,21},{6,22},{7,23},{8,24},{9,... | collective-permute-start | bytes 835592 | tf_op jit(solution)/shard_map/ppermute | solution.py:108
  93.4 14.7 %collective-permute-start.23 = (f16[32,2176]{1,0:T(8,128)(2,1)S(1)}, f16[32,2176]{1,0:T(8,128)(2,1)S(1)}, u32[]{:S(2)}, u32[]{:S(2)}) collective-permute-start(f16[32,2176]{1,0:T(8,128)(2,1)S(1)} %convert_element_type.85), channel_id=1, source_target_pairs={{0,2},{1,3},{2,0},{3,1},{4,6},{5,7},{6,4},{7,5},{8,10},{9,11},{10,... | collective-permute-start | bytes 417800 | tf_op jit(solution)/shard_map/ppermute | solution.py:108
  96.3 21.0 %collective-permute-start.24 = (f16[3,32,2176]{2,1,0:T(8,128)(2,1)S(1)}, f16[3,32,2176]{2,1,0:T(8,128)(2,1)S(1)}, u32[]{:S(2)}, u32[]{:S(2)}) collective-permute-start(f16[3,32,2176]{2,1,0:T(8,128)(2,1)S(1)} %convert_element_type.92), channel_id=1, source_target_pairs={{0,2},{1,3},{2,0},{3,1},{4,6},{5,7},{6,4},{7,5},{8,10},{9,11},{10,... | collective-permute-start | bytes 1253384 | tf_op jit(solution)/shard_map/ppermute | solution.py:108
  109.0 8.3 %collective-permute-start.25 = (f16[32,2176]{1,0:T(8,128)(2,1)S(1)}, f16[32,2176]{1,0:T(8,128)(2,1)S(1)}, u32[]{:S(2)}, u32[]{:S(2)}) collective-permute-start(f16[32,2176]{1,0:T(8,128)(2,1)S(1)} %convert_element_type.94), channel_id=1, source_target_pairs={{0,16},{1,17},{2,18},{3,19},{4,20},{5,21},{6,22},{7,23},{8,24},{9,... | collective-permute-start | bytes 417800 | tf_op jit(solution)/shard_map/ppermute | solution.py:108

commit v4 on v3

--- a/solution.py
+++ b/solution.py
@@ -194,7 +194,7 @@
         turn_kernel,
         out_shape=jax.ShapeDtypeStruct((arrived.shape[0], WIDTH), jnp.float32),
         compiler_params=params(12),
-        cost_estimate=pl.CostEstimate(flops=2 * 10**9, bytes_accessed=10**6, transcendentals=0),
+        cost_estimate=pl.CostEstimate(flops=8 * 10**8, bytes_accessed=10**6, transcendentals=0),
         name="turn",
     )(arrived)
 

time: 121 us -> 120 us (level)
  no operation moved by 1% of the time
where the time goes in v4:
time: 120 us
  waiting for transfers between devices  38.3 us (32%)
  Pallas kernels  35.1 us (29%)
  starting transfers between devices  31.8 us (26%)
  local copies, waits for them, and re-layouts  11.9 us (10%)
  other arithmetic  2.03 us (2%)
    ppermute x26, waiting for transfers between devices, send(): return lax.ppermute(value, ('row', 'col'), pairs)  38.3 us
    ppermute x26, starting transfers between devices, send(): return lax.ppermute(value, ('row', 'col'), pairs)  31.8 us
    pallas_call x5, Pallas kernels, partial_ladder(): pl.pallas_call(ladder_kernel, in_specs=[pl.BlockSpec(memory_space=pltpu.S...  14.3 us
    unnamed x32, local copies, waits for them, and re-layouts  11.9 us
    pallas_call x13, Pallas kernels, sort(): pl.pallas_call(functools.partial(kernel, steps), in_specs=[pl.BlockSpec(m...  8.87 us
    pallas_call x5, Pallas kernels, add_cores(): return call(part, across_core(part))  3.24 us
    pallas_call x1, Pallas kernels, finish(): pl.pallas_call(finish_kernel, in_specs=[pl.BlockSpec(memory_space=pltpu.S...  2.93 us
    pallas_call x4, Pallas kernels, turned(): pl.pallas_call(turn_kernel, out_shape=jax.ShapeDtypeStruct((arrived.shape...  2.66 us
  transfers between devices with their start and end apart: 26, of which 12 were waited for; matrix products, arithmetic and copies ran while one was open for 3% of the time, Pallas kernels for 27%

profile of v4, /device:TPU:0, one launch (start us, length us, event | category | flops | bytes accessed | tf_op | source)
XLA Modules:
  0.0 119.7 jit_solution(15148323881837285910)
XLA Ops:
  0.0 3.0 %collective-permute-start.1 = (bf16[128,2048]{1,0:T(8,128)(2,1)}, bf16[128,2048]{1,0:T(8,128)(2,1)}, u32[]{:S(2)}, u32[]{:S(2)}) collective-permute-start(bf16[128,2048]{1,0:T(8,128)(2,1)} %refs_0_.1), channel_id=1, source_target_pairs={{0,8},{1,9},{2,10},{3,11},{4,12},{5,13},{6,14},{7,15},{8,0},{9,1},... | collective-permute-start | bytes 1572872 | tf_op jit(solution)/shard_map/ppermute | solution.py:108
  3.0 1.5 %collective-permute-start = (bf16[128,2048]{1,0:T(8,128)(2,1)}, bf16[128,2048]{1,0:T(8,128)(2,1)S(1)}, u32[]{:S(2)}, u32[]{:S(2)}) collective-permute-start(bf16[128,2048]{1,0:T(8,128)(2,1)} %refs_0_.1), channel_id=1, source_target_pairs={{0,4},{1,5},{2,6},{3,7},{4,0},{5,1},{6,2},{7,3},{8,12},{9,13},{10,... | collective-permute-start | bytes 1572872 | tf_op jit(solution)/shard_map/ppermute | solution.py:108
  4.5 1.5 %collective-permute-start.2 = (bf16[128,2048]{1,0:T(8,128)(2,1)}, bf16[128,2048]{1,0:T(8,128)(2,1)}, u32[]{:S(2)}, u32[]{:S(2)}) collective-permute-start(bf16[128,2048]{1,0:T(8,128)(2,1)} %refs_0_.1), channel_id=1, source_target_pairs={{8,16},{9,17},{10,18},{11,19},{12,20},{13,21},{14,22},{15,23},{16,... | collective-permute-start | bytes 1572872 | tf_op jit(solution)/shard_map/ppermute | solution.py:108
  6.0 0.8 copy.16.product
  6.7 0.8 copy.17.summed
  7.6 3.4 %copy-done = bf16[2048,2048]{1,0:T(8,128)(2,1)S(1)} copy-done((bf16[2048,2048]{1,0:T(8,128)(2,1)S(1)}, bf16[2048,2048]{1,0:T(8,128)(2,1)}, u32[]{:S(2)}) %copy-start) | copy-done | bytes 8388632
  10.9 1.0 copy-done.3
  12.6 2.1 %partial_ladder.5.part = f32[4,32,2048]{2,1,0:T(8,128)S(1)} custom-call(s32[2]{0:T(128)S(1)} %pad_add_fusion.place, s32[24]{0:T(128)S(1)} %copy-done.8, s32[8,2]{1,0:T(8,128)S(1)} %copy.16.product, s32[8,2]{1,0:T(8,128)S(1)} %copy.17.summed, bf16[128,2048]{1,0:T(8,128)(2,1)S(1)} %copy-done.3, bf16[2048,2048]{1,0:T(8,128)(2,1)S(1)} %copy-done), custom_call_target="tpu_custom_call" | custom-call | flops 1000 | bytes 1000 | tf_op jit(solution)/shard_map/partial_ladder/pallas_call | solution.py:164
  15.3 1.4 %collective-permute-done.refs_0_ = bf16[128,2048]{1,0:T(8,128)(2,1)S(1)} collective-permute-done((bf16[128,2048]{1,0:T(8,128)(2,1)}, bf16[128,2048]{1,0:T(8,128)(2,1)S(1)}, u32[]{:S(2)}, u32[]{:S(2)}) %collective-permute-start) | collective-permute-done | bytes 524320 | tf_op jit(solution)/shard_map/ppermute | solution.py:108
  16.6 0.8 copy-done.6
  17.4 3.8 %collective-permute-start.5 = (bf16[128,2048]{1,0:T(8,128)(2,1)}, bf16[128,2048]{1,0:T(8,128)(2,1)S(1)}, u32[]{:S(2)}, u32[]{:S(2)}) collective-permute-start(bf16[128,2048]{1,0:T(8,128)(2,1)} %collective-permute-done.2), channel_id=1, source_target_pairs={{0,8},{1,9},{2,10},{3,11},{4,12},{5,13},{6,14},{7,15},{8,0},{9,1},... | collective-permute-start | bytes 1572872 | tf_op jit(solution)/shard_map/ppermute | solution.py:108
  21.2 0.7 collective-permute-start.4
  22.8 1.6 %collective-permute-start.7 = (f16[32,2176]{1,0:T(8,128)(2,1)S(1)}, f16[32,2176]{1,0:T(8,128)(2,1)S(1)}, u32[]{:S(2)}, u32[]{:S(2)}) collective-permute-start(f16[32,2176]{1,0:T(8,128)(2,1)S(1)} %convert_element_type.72), channel_id=1, source_target_pairs={{0,2},{1,3},{2,0},{3,1},{4,6},{5,7},{6,4},{7,5},{8,10},{9,11},{10,... | collective-permute-start | bytes 417800 | tf_op jit(solution)/shard_map/ppermute | solution.py:108
  24.4 3.7 %partial_ladder.6.part = f32[4,64,2048]{2,1,0:T(8,128)S(1)} custom-call(s32[2]{0:T(128)S(1)} %pad_add_fusion.place, s32[24]{0:T(128)S(1)} %copy-done.8, s32[8,2]{1,0:T(8,128)S(1)} %copy.16.product, s32[8,2]{1,0:T(8,128)S(1)} %copy.17.summed, bf16[128,2048]{1,0:T(8,128)(2,1)S(1)} %copy-done.7, bf16[128,2048]{1,0:T(8,128)(2,1)} %collective-permute-done.1.refs_1_, ...), custom_call_target="tpu_custom_call" | custom-call | flops 1000 | bytes 1000 | tf_op jit(solution)/shard_map/partial_ladder/pallas_call | solution.py:164
  28.1 6.0 %collective-permute-done.5 = bf16[128,2048]{1,0:T(8,128)(2,1)S(1)} collective-permute-done((bf16[128,2048]{1,0:T(8,128)(2,1)}, bf16[128,2048]{1,0:T(8,128)(2,1)S(1)}, u32[]{:S(2)}, u32[]{:S(2)}) %collective-permute-start.5) | collective-permute-done | bytes 524320 | tf_op jit(solution)/shard_map/ppermute | solution.py:108
  34.1 2.2 %collective-permute-done.3.refs_0_ = bf16[128,2048]{1,0:T(8,128)(2,1)S(1)} collective-permute-done((bf16[128,2048]{1,0:T(8,128)(2,1)}, bf16[128,2048]{1,0:T(8,128)(2,1)S(1)}, u32[]{:S(2)}, u32[]{:S(2)}) %collective-permute-start.3) | collective-permute-done | bytes 524320 | tf_op jit(solution)/shard_map/ppermute | solution.py:108
  36.3 0.8 copy-done.4
  37.2 1.1 broadcast_select_fusion.1.refs_1_
  38.9 2.9 %collective-permute-start.9 = (bf16[128,2048]{1,0:T(8,128)(2,1)}, bf16[128,2048]{1,0:T(8,128)(2,1)S(1)}, u32[]{:S(2)}, u32[]{:S(2)}) collective-permute-start(bf16[128,2048]{1,0:T(8,128)(2,1)} %copy-done.10), channel_id=1, source_target_pairs={{0,8},{1,9},{2,10},{3,11},{4,12},{5,13},{6,14},{7,15},{8,0},{9,1},... | collective-permute-start | bytes 1572872 | tf_op jit(solution)/shard_map/ppermute | solution.py:108
  41.8 2.0 %add_cores.6 = (f32[4,64,2048]{2,1,0:T(8,128)S(1)}, f32[64,2176]{1,0:T(8,128)S(1)}) custom-call(f32[4,64,2048]{2,1,0:T(8,128)S(1)} %partial_ladder.6.part, f32[4,64,2048]{2,1,0:T(8,128)} %collective-permute-done.11.sibling), custom_call_target="tpu_custom_call" | custom-call | flops 1000 | bytes 1000 | tf_op jit(solution)/shard_map/add_cores/pallas_call | solution.py:382
  43.9 1.6 %collective-permute-start.12 = (f16[64,2176]{1,0:T(8,128)(2,1)S(1)}, f16[64,2176]{1,0:T(8,128)(2,1)S(1)}, u32[]{:S(2)}, u32[]{:S(2)}) collective-permute-start(f16[64,2176]{1,0:T(8,128)(2,1)S(1)} %convert_element_type.75), channel_id=1, source_target_pairs={{0,2},{1,3},{2,0},{3,1},{4,6},{5,7},{6,4},{7,5},{8,10},{9,11},{10,... | collective-permute-start | bytes 835592 | tf_op jit(solution)/shard_map/ppermute | solution.py:108
  45.8 2.4 %collective-permute-start.10 = (f16[32,2176]{1,0:T(8,128)(2,1)S(1)}, f16[32,2176]{1,0:T(8,128)(2,1)S(1)}, u32[]{:S(2)}, u32[]{:S(2)}) collective-permute-start(f16[32,2176]{1,0:T(8,128)(2,1)S(1)} %convert_element_type.74), channel_id=1, source_target_pairs={{0,16},{1,17},{2,18},{3,19},{4,20},{5,21},{6,22},{7,23},{8,24},{9,... | collective-permute-start | bytes 417800 | tf_op jit(solution)/shard_map/ppermute | solution.py:108
  49.8 3.4 %copy-done.2 = bf16[2048,2048]{1,0:T(8,128)(2,1)S(1)} copy-done((bf16[2048,2048]{1,0:T(8,128)(2,1)S(1)}, bf16[2048,2048]{1,0:T(8,128)(2,1)}, u32[]{:S(2)}) %copy-start.2) | copy-done | bytes 8388632
  53.2 3.3 %partial_ladder.7.part = f32[4,64,2048]{2,1,0:T(8,128)S(1)} custom-call(s32[2]{0:T(128)S(1)} %pad_add_fusion.place, s32[24]{0:T(128)S(1)} %copy-done.9, s32[8,2]{1,0:T(8,128)S(1)} %copy.16.product, s32[8,2]{1,0:T(8,128)S(1)} %copy.17.summed, bf16[128,2048]{1,0:T(8,128)(2,1)S(1)} %copy-done.5, bf16[128,2048]{1,0:T(8,128)(2,1)S(1)} %broadcast_select_fusion.1.refs_1_, ...), custom_call_target="tpu_custom_call" | custom-call | flops 1000 | bytes 1000 | tf_op jit(solution)/shard_map/partial_ladder/pallas_call | solution.py:164
  56.6 0.7 collective-permute-done.9
  57.4 1.6 %collective-permute-start.13 = (bf16[128,2048]{1,0:T(8,128)(2,1)S(1)}, bf16[128,2048]{1,0:T(8,128)(2,1)S(1)}, u32[]{:S(2)}, u32[]{:S(2)}) collective-permute-start(bf16[128,2048]{1,0:T(8,128)(2,1)S(1)} %broadcast_select_fusion.refs_1_), channel_id=1, source_target_pairs={{0,4},{1,5},{2,6},{3,7},{4,0},{5,1},{6,2},{7,3},{8,12},{9,13},{10,... | collective-permute-start | bytes 1572872 | tf_op jit(solution)/shard_map/ppermute | solution.py:108
  59.5 2.8 %collective-permute-start.14 = (f16[64,2176]{1,0:T(8,128)(2,1)S(1)}, f16[64,2176]{1,0:T(8,128)(2,1)S(1)}, u32[]{:S(2)}, u32[]{:S(2)}) collective-permute-start(f16[64,2176]{1,0:T(8,128)(2,1)S(1)} %convert_element_type.77), channel_id=1, source_target_pairs={{0,16},{1,17},{2,18},{3,19},{4,20},{5,21},{6,22},{7,23},{8,24},{9,... | collective-permute-start | bytes 835592 | tf_op jit(solution)/shard_map/ppermute | solution.py:108
  62.7 1.6 %collective-permute-start.16 = (f16[64,2176]{1,0:T(8,128)(2,1)S(1)}, f16[64,2176]{1,0:T(8,128)(2,1)S(1)}, u32[]{:S(2)}, u32[]{:S(2)}) collective-permute-start(f16[64,2176]{1,0:T(8,128)(2,1)S(1)} %convert_element_type.78), channel_id=1, source_target_pairs={{0,2},{1,3},{2,0},{3,1},{4,6},{5,7},{6,4},{7,5},{8,10},{9,11},{10,... | collective-permute-start | bytes 835592 | tf_op jit(solution)/shard_map/ppermute | solution.py:108
  64.9 0.7 sort.16.refs_0_
  65.7 3.3 %partial_ladder.8.part = f32[4,64,2048]{2,1,0:T(8,128)S(1)} custom-call(s32[2]{0:T(128)S(1)} %pad_add_fusion.place, s32[24]{0:T(128)S(1)} %copy-done.9, s32[8,2]{1,0:T(8,128)S(1)} %copy.16.product, s32[8,2]{1,0:T(8,128)S(1)} %copy.17.summed, bf16[128,2048]{1,0:T(8,128)(2,1)S(1)} %collective-permute-done.8.refs_0_, ...), custom_call_target="tpu_custom_call" | custom-call | flops 1000 | bytes 1000 | tf_op jit(solution)/shard_map/partial_ladder/pallas_call | solution.py:164
  68.9 0.7 sort.15.refs_0_
  69.6 5.7 %collective-permute-done.14 = f16[64,2176]{1,0:T(8,128)(2,1)S(1)} collective-permute-done((f16[64,2176]{1,0:T(8,128)(2,1)S(1)}, f16[64,2176]{1,0:T(8,128)(2,1)S(1)}, u32[]{:S(2)}, u32[]{:S(2)}) %collective-permute-start.14) | collective-permute-done | bytes 278560 | tf_op jit(solution)/shard_map/ppermute | solution.py:108
  75.9 3.6 %collective-permute-done.18.sibling = f32[4,64,2048]{2,1,0:T(8,128)S(1)} collective-permute-done((f32[4,64,2048]{2,1,0:T(8,128)S(1)}, f32[4,64,2048]{2,1,0:T(8,128)S(1)}, u32[]{:S(2)}, u32[]{:S(2)}) %collective-permute-start.18) | collective-permute-done | bytes 2097184 | tf_op jit(solution)/shard_map/ppermute | solution.py:108
  79.9 1.6 %collective-permute-start.19 = (f16[64,2176]{1,0:T(8,128)(2,1)S(1)}, f16[64,2176]{1,0:T(8,128)(2,1)S(1)}, u32[]{:S(2)}, u32[]{:S(2)}) collective-permute-start(f16[64,2176]{1,0:T(8,128)(2,1)S(1)} %convert_element_type.82), channel_id=1, source_target_pairs={{0,2},{1,3},{2,0},{3,1},{4,6},{5,7},{6,4},{7,5},{8,10},{9,11},{10,... | collective-permute-start | bytes 835592 | tf_op jit(solution)/shard_map/ppermute | solution.py:108
  81.5 1.0 sort.19.refs_0_
  83.0 2.1 %partial_ladder.9.part = f32[4,32,2048]{2,1,0:T(8,128)S(1)} custom-call(s32[2]{0:T(128)S(1)} %pad_add_fusion.place, s32[24]{0:T(128)S(1)} %copy-done.9, s32[8,2]{1,0:T(8,128)S(1)} %copy.16.product, s32[8,2]{1,0:T(8,128)S(1)} %copy.17.summed, bf16[128,2048]{1,0:T(8,128)(2,1)S(1)} %collective-permute-done.13.refs_0_, bf16[2048,2048]{1,0:T(8,128)(2,1)S(1)} %bitcast.3), custom_call_target="tpu_custom_call" | custom-call | flops 1000 | bytes 1000 | tf_op jit(solution)/shard_map/partial_ladder/pallas_call | solution.py:164
  85.7 1.0 sort.22.refs_0_
  87.3 3.2 %collective-permute-done.17 = f16[64,2176]{1,0:T(8,128)(2,1)S(1)} collective-permute-done((f16[64,2176]{1,0:T(8,128)(2,1)S(1)}, f16[64,2176]{1,0:T(8,128)(2,1)S(1)}, u32[]{:S(2)}, u32[]{:S(2)}) %collective-permute-start.17) | collective-permute-done | bytes 278560 | tf_op jit(solution)/shard_map/ppermute | solution.py:108
  91.1 1.6 %collective-permute-start.21 = (f16[3,32,2176]{2,1,0:T(8,128)(2,1)S(1)}, f16[3,32,2176]{2,1,0:T(8,128)(2,1)S(1)}, u32[]{:S(2)}, u32[]{:S(2)}) collective-permute-start(f16[3,32,2176]{2,1,0:T(8,128)(2,1)S(1)} %convert_element_type.81), channel_id=1, source_target_pairs={{0,2},{1,3},{2,0},{3,1},{4,6},{5,7},{6,4},{7,5},{8,10},{9,11},{10,... | collective-permute-start | bytes 1253384 | tf_op jit(solution)/shard_map/ppermute | solution.py:108
  93.4 1.6 %collective-permute-start.23 = (f16[32,2176]{1,0:T(8,128)(2,1)S(1)}, f16[32,2176]{1,0:T(8,128)(2,1)S(1)}, u32[]{:S(2)}, u32[]{:S(2)}) collective-permute-start(f16[32,2176]{1,0:T(8,128)(2,1)S(1)} %convert_element_type.85), channel_id=1, source_target_pairs={{0,2},{1,3},{2,0},{3,1},{4,6},{5,7},{6,4},{7,5},{8,10},{9,11},{10,... | collective-permute-start | bytes 417800 | tf_op jit(solution)/shard_map/ppermute | solution.py:108
  96.8 11.3 %collective-permute-done.20 = f16[64,2176]{1,0:T(8,128)(2,1)S(1)} collective-permute-done((f16[64,2176]{1,0:T(8,128)(2,1)S(1)}, f16[64,2176]{1,0:T(8,128)(2,1)S(1)}, u32[]{:S(2)}, u32[]{:S(2)}) %collective-permute-start.20) | collective-permute-done | bytes 278560 | tf_op jit(solution)/shard_map/ppermute | solution.py:108
  108.5 0.8 sort.24.own
  110.0 0.7 turn.5.refs_1_
  110.8 0.7 turn.6.refs_2_
  111.5 0.7 turn.7.refs_3_
  112.3 1.3 %gather.1.sums = f32[4,64,2048]{2,1,0:T(8,128)S(1)} custom-call(s32[2]{0:T(128)S(1)} %pad_add_fusion.place, f32[4,64,2048]{2,1,0:T(8,128)S(1)} %sort.24.own, f32[3,32,2176]{2,1,0:T(8,128)S(1)} %convert_element_type.87.rest, f32[32,2048]{1,0:T(8,128)S(1)} %turn.4.refs_0_, f32[64,2048]{1,0:T(8,128)S(1)} %turn.5.refs_1_, f32[64,2048]{1,0:T(8,128)S(1)} %turn.6.refs_2_, ...), custom_call_target="tpu_custom_call" | custom-call | flops 1000 | bytes 1000 | tf_op jit(solution)/shard_map/gather/pallas_call | solution.py:290
  113.6 3.2 %collective-permute-done.25 = f16[32,2176]{1,0:T(8,128)(2,1)S(1)} collective-permute-done((f16[32,2176]{1,0:T(8,128)(2,1)S(1)}, f16[32,2176]{1,0:T(8,128)(2,1)S(1)}, u32[]{:S(2)}, u32[]{:S(2)}) %collective-permute-start.25) | collective-permute-done | bytes 139296 | tf_op jit(solution)/shard_map/ppermute | solution.py:108
  116.8 2.9 %finish.1 = bf16[256,2048]{1,0:T(8,128)(2,1)} custom-call(s32[2]{0:T(128)S(1)} %pad_add_fusion.place, f32[4,64,2048]{2,1,0:T(8,128)S(1)} %gather.1.sums, f32[3,32,2176]{2,1,0:T(8,128)S(1)} %convert_element_type.93.rest, f32[32,2176]{1,0:T(8,128)S(1)} %convert_element_type.95.last), custom_call_target="tpu_custom_call" | custom-call | flops 1000 | bytes 1000 | tf_op jit(solution)/shard_map/finish/pallas_call | solution.py:320
  (98 shorter events, 13.5 us)
Async XLA Ops:
  0.0 15.3 %collective-permute-start.1 = (bf16[128,2048]{1,0:T(8,128)(2,1)}, bf16[128,2048]{1,0:T(8,128)(2,1)}, u32[]{:S(2)}, u32[]{:S(2)}) collective-permute-start(bf16[128,2048]{1,0:T(8,128)(2,1)} %refs_0_.1), channel_id=1, source_target_pairs={{0,8},{1,9},{2,10},{3,11},{4,12},{5,13},{6,14},{7,15},{8,0},{9,1},... | collective-permute-start | bytes 1572872 | tf_op jit(solution)/shard_map/ppermute | solution.py:108
  3.0 13.6 %collective-permute-start = (bf16[128,2048]{1,0:T(8,128)(2,1)}, bf16[128,2048]{1,0:T(8,128)(2,1)S(1)}, u32[]{:S(2)}, u32[]{:S(2)}) collective-permute-start(bf16[128,2048]{1,0:T(8,128)(2,1)} %refs_0_.1), channel_id=1, source_target_pairs={{0,4},{1,5},{2,6},{3,7},{4,0},{5,1},{6,2},{7,3},{8,12},{9,13},{10,... | collective-permute-start | bytes 1572872 | tf_op jit(solution)/shard_map/ppermute | solution.py:108
  4.5 12.9 %collective-permute-start.2 = (bf16[128,2048]{1,0:T(8,128)(2,1)}, bf16[128,2048]{1,0:T(8,128)(2,1)}, u32[]{:S(2)}, u32[]{:S(2)}) collective-permute-start(bf16[128,2048]{1,0:T(8,128)(2,1)} %refs_0_.1), channel_id=1, source_target_pairs={{8,16},{9,17},{10,18},{11,19},{12,20},{13,21},{14,22},{15,23},{16,... | collective-permute-start | bytes 1572872 | tf_op jit(solution)/shard_map/ppermute | solution.py:108
  7.6 3.4 %copy-start = (bf16[2048,2048]{1,0:T(8,128)(2,1)S(1)}, bf16[2048,2048]{1,0:T(8,128)(2,1)}, u32[]{:S(2)}) copy-start(bf16[2048,2048]{1,0:T(8,128)(2,1)} %refs_1_.3) | copy-start | bytes 25165828
  10.9 1.0 copy-start.3
  12.0 0.7 copy-start.8
  12.6 11.8 %copy-start.1 = (bf16[2048,2048]{1,0:T(8,128)(2,1)S(1)}, bf16[2048,2048]{1,0:T(8,128)(2,1)}, u32[]{:S(2)}) copy-start(bf16[2048,2048]{1,0:T(8,128)(2,1)} %refs_1_.3) | copy-start | bytes 25165828
  16.6 0.8 copy-start.6
  17.4 7.0 %copy-start.7 = (bf16[128,2048]{1,0:T(8,128)(2,1)S(1)}, bf16[128,2048]{1,0:T(8,128)(2,1)}, u32[]{:S(2)}) copy-start(bf16[128,2048]{1,0:T(8,128)(2,1)} %copy-done.6) | copy-start | bytes 1572868
  17.4 5.1 %collective-permute-start.6 = (f32[4,32,2048]{2,1,0:T(8,128)S(1)}, f32[4,32,2048]{2,1,0:T(8,128)S(1)}, u32[]{:S(2)}, u32[]{:S(2)}) collective-permute-start(f32[4,32,2048]{2,1,0:T(8,128)S(1)} %partial_ladder.5.part), channel_id=1, source_target_pairs={{0,1},{1,0},{2,3},{3,2},{4,5},{5,4},{6,7},{7,6},{8,9},{9,8},{10,11... | collective-permute-start | bytes 3145736 | tf_op jit(solution)/shard_map/ppermute | solution.py:108
  17.4 16.6 %collective-permute-start.5 = (bf16[128,2048]{1,0:T(8,128)(2,1)}, bf16[128,2048]{1,0:T(8,128)(2,1)S(1)}, u32[]{:S(2)}, u32[]{:S(2)}) collective-permute-start(bf16[128,2048]{1,0:T(8,128)(2,1)} %collective-permute-done.2), channel_id=1, source_target_pairs={{0,8},{1,9},{2,10},{3,11},{4,12},{5,13},{6,14},{7,15},{8,0},{9,1},... | collective-permute-start | bytes 1572872 | tf_op jit(solution)/shard_map/ppermute | solution.py:108
  21.2 12.8 %collective-permute-start.4 = (bf16[128,2048]{1,0:T(8,128)(2,1)}, bf16[128,2048]{1,0:T(8,128)(2,1)S(1)}, u32[]{:S(2)}, u32[]{:S(2)}) collective-permute-start(bf16[128,2048]{1,0:T(8,128)(2,1)} %collective-permute-done.1.refs_1_), channel_id=1, source_target_pairs={{8,16},{9,17},{10,18},{11,19},{12,20},{13,21},{14,22},{15,23},{16,... | collective-permute-start | bytes 1572872 | tf_op jit(solution)/shard_map/ppermute | solution.py:108
  21.9 14.3 %collective-permute-start.3 = (bf16[128,2048]{1,0:T(8,128)(2,1)}, bf16[128,2048]{1,0:T(8,128)(2,1)S(1)}, u32[]{:S(2)}, u32[]{:S(2)}) collective-permute-start(bf16[128,2048]{1,0:T(8,128)(2,1)} %collective-permute-done.1.refs_1_), channel_id=1, source_target_pairs={{0,4},{1,5},{2,6},{3,7},{4,0},{5,1},{6,2},{7,3},{8,12},{9,13},{10,... | collective-permute-start | bytes 1572872 | tf_op jit(solution)/shard_map/ppermute | solution.py:108
  22.8 14.2 %collective-permute-start.7 = (f16[32,2176]{1,0:T(8,128)(2,1)S(1)}, f16[32,2176]{1,0:T(8,128)(2,1)S(1)}, u32[]{:S(2)}, u32[]{:S(2)}) collective-permute-start(f16[32,2176]{1,0:T(8,128)(2,1)S(1)} %convert_element_type.72), channel_id=1, source_target_pairs={{0,2},{1,3},{2,0},{3,1},{4,6},{5,7},{6,4},{7,5},{8,10},{9,11},{10,... | collective-permute-start | bytes 417800 | tf_op jit(solution)/shard_map/ppermute | solution.py:108
  34.0 3.0 %copy-start.12 = (bf16[128,2048]{1,0:T(8,128)(2,1)}, bf16[128,2048]{1,0:T(8,128)(2,1)S(1)}, u32[]{:S(2)}) copy-start(bf16[128,2048]{1,0:T(8,128)(2,1)S(1)} %collective-permute-done.5) | copy-start | bytes 1572868
  34.1 3.0 %copy-start.10 = (bf16[128,2048]{1,0:T(8,128)(2,1)}, bf16[128,2048]{1,0:T(8,128)(2,1)S(1)}, u32[]{:S(2)}) copy-start(bf16[128,2048]{1,0:T(8,128)(2,1)S(1)} %collective-permute-done.4) | copy-start | bytes 1572868
  36.3 0.8 copy-start.4
  37.1 4.8 %collective-permute-start.11 = (f32[4,64,2048]{2,1,0:T(8,128)S(1)}, f32[4,64,2048]{2,1,0:T(8,128)}, u32[]{:S(2)}, u32[]{:S(2)}) collective-permute-start(f32[4,64,2048]{2,1,0:T(8,128)S(1)} %partial_ladder.6.part), channel_id=1, source_target_pairs={{0,1},{1,0},{2,3},{3,2},{4,5},{5,4},{6,7},{7,6},{8,9},{9,8},{10,11... | collective-permute-start | bytes 6291464 | tf_op jit(solution)/shard_map/ppermute | solution.py:108
  38.3 18.3 %collective-permute-start.8 = (bf16[128,2048]{1,0:T(8,128)(2,1)S(1)}, bf16[128,2048]{1,0:T(8,128)(2,1)S(1)}, u32[]{:S(2)}, u32[]{:S(2)}) collective-permute-start(bf16[128,2048]{1,0:T(8,128)(2,1)S(1)} %broadcast_select_fusion.1.refs_1_), channel_id=1, source_target_pairs={{0,4},{1,5},{2,6},{3,7},{4,0},{5,1},{6,2},{7,3},{8,12},{9,13},{10,... | collective-permute-start | bytes 1572872 | tf_op jit(solution)/shard_map/ppermute | solution.py:108
  38.9 18.4 %collective-permute-start.9 = (bf16[128,2048]{1,0:T(8,128)(2,1)}, bf16[128,2048]{1,0:T(8,128)(2,1)S(1)}, u32[]{:S(2)}, u32[]{:S(2)}) collective-permute-start(bf16[128,2048]{1,0:T(8,128)(2,1)} %copy-done.10), channel_id=1, source_target_pairs={{0,8},{1,9},{2,10},{3,11},{4,12},{5,13},{6,14},{7,15},{8,0},{9,1},... | collective-permute-start | bytes 1572872 | tf_op jit(solution)/shard_map/ppermute | solution.py:108
  43.9 13.4 %collective-permute-start.12 = (f16[64,2176]{1,0:T(8,128)(2,1)S(1)}, f16[64,2176]{1,0:T(8,128)(2,1)S(1)}, u32[]{:S(2)}, u32[]{:S(2)}) collective-permute-start(f16[64,2176]{1,0:T(8,128)(2,1)S(1)} %convert_element_type.75), channel_id=1, source_target_pairs={{0,2},{1,3},{2,0},{3,1},{4,6},{5,7},{6,4},{7,5},{8,10},{9,11},{10,... | collective-permute-start | bytes 835592 | tf_op jit(solution)/shard_map/ppermute | solution.py:108
  45.8 10.8 %collective-permute-start.10 = (f16[32,2176]{1,0:T(8,128)(2,1)S(1)}, f16[32,2176]{1,0:T(8,128)(2,1)S(1)}, u32[]{:S(2)}, u32[]{:S(2)}) collective-permute-start(f16[32,2176]{1,0:T(8,128)(2,1)S(1)} %convert_element_type.74), channel_id=1, source_target_pairs={{0,16},{1,17},{2,18},{3,19},{4,20},{5,21},{6,22},{7,23},{8,24},{9,... | collective-permute-start | bytes 417800 | tf_op jit(solution)/shard_map/ppermute | solution.py:108
  48.8 1.0 copy-start.5
  48.8 1.0 copy-start.9
  49.8 3.4 %copy-start.2 = (bf16[2048,2048]{1,0:T(8,128)(2,1)S(1)}, bf16[2048,2048]{1,0:T(8,128)(2,1)}, u32[]{:S(2)}) copy-start(bf16[2048,2048]{1,0:T(8,128)(2,1)} %refs_1_.3) | copy-start | bytes 25165828
  53.2 4.1 %copy-start.11 = (bf16[128,2048]{1,0:T(8,128)(2,1)S(1)}, bf16[128,2048]{1,0:T(8,128)(2,1)}, u32[]{:S(2)}) copy-start(bf16[128,2048]{1,0:T(8,128)(2,1)} %copy-done.10) | copy-start | bytes 1572868
  57.3 5.0 %collective-permute-start.15 = (f32[4,64,2048]{2,1,0:T(8,128)S(1)}, f32[4,64,2048]{2,1,0:T(8,128)S(1)}, u32[]{:S(2)}, u32[]{:S(2)}) collective-permute-start(f32[4,64,2048]{2,1,0:T(8,128)S(1)} %partial_ladder.7.part), channel_id=1, source_target_pairs={{0,1},{1,0},{2,3},{3,2},{4,5},{5,4},{6,7},{7,6},{8,9},{9,8},{10,11... | collective-permute-start | bytes 6291464 | tf_op jit(solution)/shard_map/ppermute | solution.py:108
  57.4 17.9 %collective-permute-start.13 = (bf16[128,2048]{1,0:T(8,128)(2,1)S(1)}, bf16[128,2048]{1,0:T(8,128)(2,1)S(1)}, u32[]{:S(2)}, u32[]{:S(2)}) collective-permute-start(bf16[128,2048]{1,0:T(8,128)(2,1)S(1)} %broadcast_select_fusion.refs_1_), channel_id=1, source_target_pairs={{0,4},{1,5},{2,6},{3,7},{4,0},{5,1},{6,2},{7,3},{8,12},{9,13},{10,... | collective-permute-start | bytes 1572872 | tf_op jit(solution)/shard_map/ppermute | solution.py:108
  59.0 6.6 %slice-start = ((s8[8388608]{0:T(1024)(128)(4,1)}), s8[4194304]{0:T(1024)(128)(4,1)S(1)}, s32[]{:S(2)}) async-start(s8[8388608]{0:T(1024)(128)(4,1)} %bitcast.2), calls=%async_computation | async-start | bytes 8388608
  59.5 6.2 %slice-start.1 = ((s8[8388608]{0:T(1024)(128)(4,1)}), s8[4194304]{0:T(1024)(128)(4,1)S(1)}, s32[]{:S(2)}) async-start(s8[8388608]{0:T(1024)(128)(4,1)} %bitcast.2), calls=%async_computation.1 | async-start | bytes 8388608
  59.5 15.8 %collective-permute-start.14 = (f16[64,2176]{1,0:T(8,128)(2,1)S(1)}, f16[64,2176]{1,0:T(8,128)(2,1)S(1)}, u32[]{:S(2)}, u32[]{:S(2)}) collective-permute-start(f16[64,2176]{1,0:T(8,128)(2,1)S(1)} %convert_element_type.77), channel_id=1, source_target_pairs={{0,16},{1,17},{2,18},{3,19},{4,20},{5,21},{6,22},{7,23},{8,24},{9,... | collective-permute-start | bytes 835592 | tf_op jit(solution)/shard_map/ppermute | solution.py:108
  62.7 12.6 %collective-permute-start.16 = (f16[64,2176]{1,0:T(8,128)(2,1)S(1)}, f16[64,2176]{1,0:T(8,128)(2,1)S(1)}, u32[]{:S(2)}, u32[]{:S(2)}) collective-permute-start(f16[64,2176]{1,0:T(8,128)(2,1)S(1)} %convert_element_type.78), channel_id=1, source_target_pairs={{0,2},{1,3},{2,0},{3,1},{4,6},{5,7},{6,4},{7,5},{8,10},{9,11},{10,... | collective-permute-start | bytes 835592 | tf_op jit(solution)/shard_map/ppermute | solution.py:108
  75.3 4.2 %collective-permute-start.18 = (f32[4,64,2048]{2,1,0:T(8,128)S(1)}, f32[4,64,2048]{2,1,0:T(8,128)S(1)}, u32[]{:S(2)}, u32[]{:S(2)}) collective-permute-start(f32[4,64,2048]{2,1,0:T(8,128)S(1)} %partial_ladder.8.part), channel_id=1, source_target_pairs={{0,1},{1,0},{2,3},{3,2},{4,5},{5,4},{6,7},{7,6},{8,9},{9,8},{10,11... | collective-permute-start | bytes 6291464 | tf_op jit(solution)/shard_map/ppermute | solution.py:108
  75.8 14.7 %collective-permute-start.17 = (f16[64,2176]{1,0:T(8,128)(2,1)S(1)}, f16[64,2176]{1,0:T(8,128)(2,1)S(1)}, u32[]{:S(2)}, u32[]{:S(2)}) collective-permute-start(f16[64,2176]{1,0:T(8,128)(2,1)S(1)} %convert_element_type.80), channel_id=1, source_target_pairs={{0,16},{1,17},{2,18},{3,19},{4,20},{5,21},{6,22},{7,23},{8,24},{9,... | collective-permute-start | bytes 835592 | tf_op jit(solution)/shard_map/ppermute | solution.py:108
  79.9 10.6 %collective-permute-start.19 = (f16[64,2176]{1,0:T(8,128)(2,1)S(1)}, f16[64,2176]{1,0:T(8,128)(2,1)S(1)}, u32[]{:S(2)}, u32[]{:S(2)}) collective-permute-start(f16[64,2176]{1,0:T(8,128)(2,1)S(1)} %convert_element_type.82), channel_id=1, source_target_pairs={{0,2},{1,3},{2,0},{3,1},{4,6},{5,7},{6,4},{7,5},{8,10},{9,11},{10,... | collective-permute-start | bytes 835592 | tf_op jit(solution)/shard_map/ppermute | solution.py:108
  90.5 2.7 %collective-permute-start.22 = (f32[4,32,2048]{2,1,0:T(8,128)S(1)}, f32[4,32,2048]{2,1,0:T(8,128)S(1)}, u32[]{:S(2)}, u32[]{:S(2)}) collective-permute-start(f32[4,32,2048]{2,1,0:T(8,128)S(1)} %partial_ladder.9.part), channel_id=1, source_target_pairs={{0,1},{1,0},{2,3},{3,2},{4,5},{5,4},{6,7},{7,6},{8,9},{9,8},{10,11... | collective-permute-start | bytes 3145736 | tf_op jit(solution)/shard_map/ppermute | solution.py:108
  91.1 17.0 %collective-permute-start.21 = (f16[3,32,2176]{2,1,0:T(8,128)(2,1)S(1)}, f16[3,32,2176]{2,1,0:T(8,128)(2,1)S(1)}, u32[]{:S(2)}, u32[]{:S(2)}) collective-permute-start(f16[3,32,2176]{2,1,0:T(8,128)(2,1)S(1)} %convert_element_type.81), channel_id=1, source_target_pairs={{0,2},{1,3},{2,0},{3,1},{4,6},{5,7},{6,4},{7,5},{8,10},{9,11},{10,... | collective-permute-start | bytes 1253384 | tf_op jit(solution)/shard_map/ppermute | solution.py:108
  92.7 15.4 %collective-permute-start.20 = (f16[64,2176]{1,0:T(8,128)(2,1)S(1)}, f16[64,2176]{1,0:T(8,128)(2,1)S(1)}, u32[]{:S(2)}, u32[]{:S(2)}) collective-permute-start(f16[64,2176]{1,0:T(8,128)(2,1)S(1)} %convert_element_type.84), channel_id=1, source_target_pairs={{0,16},{1,17},{2,18},{3,19},{4,20},{5,21},{6,22},{7,23},{8,24},{9,... | collective-permute-start | bytes 835592 | tf_op jit(solution)/shard_map/ppermute | solution.py:108
  93.4 14.7 %collective-permute-start.23 = (f16[32,2176]{1,0:T(8,128)(2,1)S(1)}, f16[32,2176]{1,0:T(8,128)(2,1)S(1)}, u32[]{:S(2)}, u32[]{:S(2)}) collective-permute-start(f16[32,2176]{1,0:T(8,128)(2,1)S(1)} %convert_element_type.85), channel_id=1, source_target_pairs={{0,2},{1,3},{2,0},{3,1},{4,6},{5,7},{6,4},{7,5},{8,10},{9,11},{10,... | collective-permute-start | bytes 417800 | tf_op jit(solution)/shard_map/ppermute | solution.py:108
  95.7 21.1 %collective-permute-start.24 = (f16[3,32,2176]{2,1,0:T(8,128)(2,1)S(1)}, f16[3,32,2176]{2,1,0:T(8,128)(2,1)S(1)}, u32[]{:S(2)}, u32[]{:S(2)}) collective-permute-start(f16[3,32,2176]{2,1,0:T(8,128)(2,1)S(1)} %convert_element_type.92), channel_id=1, source_target_pairs={{0,2},{1,3},{2,0},{3,1},{4,6},{5,7},{6,4},{7,5},{8,10},{9,11},{10,... | collective-permute-start | bytes 1253384 | tf_op jit(solution)/shard_map/ppermute | solution.py:108
  108.4 8.3 %collective-permute-start.25 = (f16[32,2176]{1,0:T(8,128)(2,1)S(1)}, f16[32,2176]{1,0:T(8,128)(2,1)S(1)}, u32[]{:S(2)}, u32[]{:S(2)}) collective-permute-start(f16[32,2176]{1,0:T(8,128)(2,1)S(1)} %convert_element_type.94), channel_id=1, source_target_pairs={{0,16},{1,17},{2,18},{3,19},{4,20},{5,21},{6,22},{7,23},{8,24},{9,... | collective-permute-start | bytes 417800 | tf_op jit(solution)/shard_map/ppermute | solution.py:108

commit v5 on v4

--- a/solution.py
+++ b/solution.py
@@ -56,6 +56,7 @@
 WIDTH = 2048
 PANELS = WIDTH // TP
 LANES = 128
+EXTRA = 16
 PLANES = ((0, 1, 2, 3), (1, 0, 2, 3), (2, 3, 1, 0), (3, 2, 1, 0))
 PART_OF = (1, 2, 0, 3)
 
@@ -192,7 +193,7 @@
 def turned(arrived):
     return pl.pallas_call(
         turn_kernel,
-        out_shape=jax.ShapeDtypeStruct((arrived.shape[0], WIDTH), jnp.float32),
+        out_shape=jax.ShapeDtypeStruct(((arrived.shape[0] - EXTRA) * LANES // WIDTH, WIDTH), jnp.float32),
         compiler_params=params(12),
         cost_estimate=pl.CostEstimate(flops=8 * 10**8, bytes_accessed=10**6, transcendentals=0),
         name="turn",
@@ -257,8 +258,8 @@
 
 def sort_owed(place, step, pair, before=None, across=0):
     n = next(n for chunk in CHUNKS for n, block in enumerate(chunk) if block == (step, across))
-    scratch = [pltpu.VMEM((3, HALF, WIDTH + LANES), jnp.float32), pltpu.SemaphoreType.DMA]
-    return sort(sort_owed_kernel, (3, HALF, WIDTH + LANES), scratch, place, ((n, step),), (pair,), before)
+    scratch = [pltpu.VMEM((3, wire_rows(HALF), LANES), jnp.float32), pltpu.SemaphoreType.DMA]
+    return sort(sort_owed_kernel, (3, wire_rows(HALF), LANES), scratch, place, ((n, step),), (pair,), before)
 
 
 def place_rest(place, ref, rest, across):
@@ -329,23 +330,28 @@
     )(place, sums, rest, last)
 
 
-def coded(value):
+def wire_rows(rows):
+    return rows * (WIDTH // LANES) + EXTRA
+
+
+def put_coded(ref, value):
     largest = value
-    while largest.ndim > 0 and largest.shape != (1,) * value.ndim:
+    while largest.shape != (1,) * value.ndim:
         axis = next(n for n, size in enumerate(largest.shape) if size > 1)
         largest = jnp.max(jnp.abs(largest), axis=axis, keepdims=True)
     power = jnp.ceil(jnp.log2(jnp.maximum(largest, 1e-30)))
     scaled = value * jnp.exp2(7 - power)
-    return scaled * jnp.abs(scaled), jnp.broadcast_to(power, (*value.shape[:-1], LANES))
-
-
-def put_coded(ref, value):
-    ref[..., :WIDTH], ref[..., WIDTH:] = coded(value)
+    scaled = scaled * jnp.abs(scaled)
+    rows = value.shape[-2]
+    for n in range(WIDTH // LANES):
+        ref[..., n * rows : (n + 1) * rows, :] = scaled[..., n * LANES : (n + 1) * LANES]
+    ref[..., ref.shape[-2] - EXTRA :, :] = jnp.broadcast_to(power, (*value.shape[:-2], EXTRA, LANES))
 
 
 def decoded(ref):
-    value = ref[..., :WIDTH]
-    power = ref[..., WIDTH : WIDTH + 1]
+    rows = (ref.shape[0] - EXTRA) * LANES // WIDTH
+    value = jnp.concatenate([ref[n * rows : (n + 1) * rows, :] for n in range(WIDTH // LANES)], axis=1)
+    power = ref[ref.shape[0] - EXTRA : ref.shape[0] - EXTRA + 1, 0:1]
     root = jnp.sqrt(jnp.abs(value)) * jnp.exp2(power - 7)
     return jnp.where(value < 0, -root, root)
 
@@ -378,7 +384,7 @@
 
 
 def add_cores(part):
-    call = small_kernel(add_cores_kernel, [part.shape, (part.shape[1], WIDTH + LANES)], 12, "add_cores")
+    call = small_kernel(add_cores_kernel, [part.shape, (wire_rows(part.shape[1]), LANES)], 12, "add_cores")
     return call(part, across_core(part))
 
 
@@ -418,8 +424,8 @@
     pair0, sent = add_cores(part0)
     over0 = across_y(wire(sent))
     part1 = partial_ladder(tables, integrals, beside0, here1)
+    here2 = jnp.where(inner, middle, here2)
     beside1, crossed, here2, pair0, over0, part1 = together(beside1, crossed, here2, pair0, over0, part1)
-    here2 = jnp.where(inner, middle, here2)
 
     beside2 = across_x(here2)
     here3 = along_z(crossed, outward)
@@ -470,12 +476,12 @@
     over4 = across_y(wire(sent))
     own = sort_own(place, CHUNKS[3], pair3, mine3, own)
     owed_beside = wire(sort_owed(place, 3, pair4, owed_beside, across=1))
-    other0, other1, other2, other3, own, came_here, pair4, over4 = together(
-        other0, other1, other2, other3, own, came_here, pair4, over4
-    )
-
-    mine4, sent = add_chips(pair4, over4)
-    sent, *others = together(sent, other0, other1, other2, other3)
+    mine4, ready4 = add_chips(pair4, over4)
+    other0, other1, other2, other3, own, came_here, pair4, mine4, ready4 = together(
+        other0, other1, other2, other3, own, came_here, pair4, mine4, ready4
+    )
+
+    sent, *others = together(ready4, other0, other1, other2, other3)
     other4 = to_partner(wire(sent))
     came_beside = across_y(owed_beside)
     own = sort_own(place, CHUNKS[4], pair4, mine4, own)

time: 120 us -> 116 us (0.967)
  waiting for transfers between devices: 38.3 us -> 35.1 us
  Pallas kernels: 35.1 us -> 33.1 us
  starting transfers between devices: 31.8 us -> 33.2 us
    ppermute x26, waiting for transfers between devices: 38.3 us -> 35.1 us  [send(): return lax.ppermute(value, ('row', 'col'), pairs)]
    ppermute x26, starting transfers between devices: 31.8 us -> 33.2 us  [send(): return lax.ppermute(value, ('row', 'col'), pairs)]
    pallas_call x5, Pallas kernels: 3.24 us -> 1.81 us  [add_cores(): return call(part, across_core(part))]
    unnamed x32 -> x20, local copies, waits for them, and re-layouts: 11.9 us -> 11.8 us
  transfers between devices with their start and end apart: 26 -> 26, of which waited for: 12 -> 14; matrix products, arithmetic and copies ran while one was open for 3% -> 3% of each run, Pallas kernels for 27% -> 26%
where the time goes in v5:
time: 116 us
  waiting for transfers between devices  35.1 us (30%)
  starting transfers between devices  33.2 us (29%)
  Pallas kernels  33.1 us (29%)
  local copies, waits for them, and re-layouts  11.8 us (10%)
  other arithmetic  2.08 us (2%)
    ppermute x26, waiting for transfers between devices, send(): return lax.ppermute(value, ('row', 'col'), pairs)  35.1 us
    ppermute x26, starting transfers between devices, send(): return lax.ppermute(value, ('row', 'col'), pairs)  33.2 us
    pallas_call x5, Pallas kernels, partial_ladder(): pl.pallas_call(ladder_kernel, in_specs=[pl.BlockSpec(memory_space=pltpu.S...  13.9 us
    unnamed x20, local copies, waits for them, and re-layouts  11.8 us
    pallas_call x13, Pallas kernels, sort(): pl.pallas_call(functools.partial(kernel, steps), in_specs=[pl.BlockSpec(m...  8.84 us
    pallas_call x1, Pallas kernels, finish(): pl.pallas_call(finish_kernel, in_specs=[pl.BlockSpec(memory_space=pltpu.S...  2.76 us
    pallas_call x4, Pallas kernels, turned(): pl.pallas_call(turn_kernel, out_shape=jax.ShapeDtypeStruct(((arrived.shap...  2.64 us
  transfers between devices with their start and end apart: 26, of which 14 were waited for; matrix products, arithmetic and copies ran while one was open for 3% of the time, Pallas kernels for 26%

profile of v5, /device:TPU:0, one launch (start us, length us, event | category | flops | bytes accessed | tf_op | source)
XLA Modules:
  0.0 115.9 jit_solution(8648643690413182209)
XLA Ops:
  0.0 3.0 %collective-permute-start.1 = (bf16[128,2048]{1,0:T(8,128)(2,1)}, bf16[128,2048]{1,0:T(8,128)(2,1)S(1)}, u32[]{:S(2)}, u32[]{:S(2)}) collective-permute-start(bf16[128,2048]{1,0:T(8,128)(2,1)} %refs_0_.1), channel_id=1, source_target_pairs={{0,8},{1,9},{2,10},{3,11},{4,12},{5,13},{6,14},{7,15},{8,0},{9,1},... | collective-permute-start | bytes 1572872 | tf_op jit(solution)/shard_map/ppermute | solution.py:109
  3.0 1.5 %collective-permute-start = (bf16[128,2048]{1,0:T(8,128)(2,1)}, bf16[128,2048]{1,0:T(8,128)(2,1)S(1)}, u32[]{:S(2)}, u32[]{:S(2)}) collective-permute-start(bf16[128,2048]{1,0:T(8,128)(2,1)} %refs_0_.1), channel_id=1, source_target_pairs={{0,4},{1,5},{2,6},{3,7},{4,0},{5,1},{6,2},{7,3},{8,12},{9,13},{10,... | collective-permute-start | bytes 1572872 | tf_op jit(solution)/shard_map/ppermute | solution.py:109
  4.5 1.5 %collective-permute-start.2 = (bf16[128,2048]{1,0:T(8,128)(2,1)}, bf16[128,2048]{1,0:T(8,128)(2,1)}, u32[]{:S(2)}, u32[]{:S(2)}) collective-permute-start(bf16[128,2048]{1,0:T(8,128)(2,1)} %refs_0_.1), channel_id=1, source_target_pairs={{8,16},{9,17},{10,18},{11,19},{12,20},{13,21},{14,22},{15,23},{16,... | collective-permute-start | bytes 1572872 | tf_op jit(solution)/shard_map/ppermute | solution.py:109
  6.0 0.8 copy.16.product
  6.7 0.8 copy.17.summed
  7.6 3.4 %copy-done = bf16[2048,2048]{1,0:T(8,128)(2,1)S(1)} copy-done((bf16[2048,2048]{1,0:T(8,128)(2,1)S(1)}, bf16[2048,2048]{1,0:T(8,128)(2,1)}, u32[]{:S(2)}) %copy-start) | copy-done | bytes 8388632
  10.9 1.0 copy-done.2
  12.6 2.1 %partial_ladder.5.part = f32[4,32,2048]{2,1,0:T(8,128)S(1)} custom-call(s32[2]{0:T(128)S(1)} %pad_add_fusion.place, s32[24]{0:T(128)S(1)} %copy-done.5, s32[8,2]{1,0:T(8,128)S(1)} %copy.16.product, s32[8,2]{1,0:T(8,128)S(1)} %copy.17.summed, bf16[128,2048]{1,0:T(8,128)(2,1)S(1)} %copy-done.2, bf16[2048,2048]{1,0:T(8,128)(2,1)S(1)} %copy-done), custom_call_target="tpu_custom_call" | custom-call | flops 1000 | bytes 1000 | tf_op jit(solution)/shard_map/partial_ladder/pallas_call | solution.py:165
  15.2 1.5 %collective-permute-done.refs_0_ = bf16[128,2048]{1,0:T(8,128)(2,1)S(1)} collective-permute-done((bf16[128,2048]{1,0:T(8,128)(2,1)}, bf16[128,2048]{1,0:T(8,128)(2,1)S(1)}, u32[]{:S(2)}, u32[]{:S(2)}) %collective-permute-start) | collective-permute-done | bytes 524320 | tf_op jit(solution)/shard_map/ppermute | solution.py:109
  16.6 0.8 copy-done.3
  17.4 3.8 %collective-permute-start.5 = (bf16[128,2048]{1,0:T(8,128)(2,1)}, bf16[128,2048]{1,0:T(8,128)(2,1)}, u32[]{:S(2)}, u32[]{:S(2)}) collective-permute-start(bf16[128,2048]{1,0:T(8,128)(2,1)} %collective-permute-done.2), channel_id=1, source_target_pairs={{0,8},{1,9},{2,10},{3,11},{4,12},{5,13},{6,14},{7,15},{8,0},{9,1},... | collective-permute-start | bytes 1572872 | tf_op jit(solution)/shard_map/ppermute | solution.py:109
  21.2 1.5 %collective-permute-start.4 = (bf16[128,2048]{1,0:T(8,128)(2,1)S(1)}, bf16[128,2048]{1,0:T(8,128)(2,1)}, u32[]{:S(2)}, u32[]{:S(2)}) collective-permute-start(bf16[128,2048]{1,0:T(8,128)(2,1)S(1)} %collective-permute-done.1.refs_1_), channel_id=1, source_target_pairs={{8,16},{9,17},{10,18},{11,19},{12,20},{13,21},{14,22},{15,23},{16,... | collective-permute-start | bytes 1572872 | tf_op jit(solution)/shard_map/ppermute | solution.py:109
  23.3 3.4 %copy-done.1 = bf16[2048,2048]{1,0:T(8,128)(2,1)S(1)} copy-done((bf16[2048,2048]{1,0:T(8,128)(2,1)S(1)}, bf16[2048,2048]{1,0:T(8,128)(2,1)}, u32[]{:S(2)}) %copy-start.1) | copy-done | bytes 8388632
  26.7 1.0 copy-done.4
  27.7 3.3 %partial_ladder.6.part = f32[4,64,2048]{2,1,0:T(8,128)S(1)} custom-call(s32[2]{0:T(128)S(1)} %pad_add_fusion.place, s32[24]{0:T(128)S(1)} %copy-done.6, s32[8,2]{1,0:T(8,128)S(1)} %copy.16.product, s32[8,2]{1,0:T(8,128)S(1)} %copy.17.summed, bf16[128,2048]{1,0:T(8,128)(2,1)S(1)} %copy-done.4, bf16[128,2048]{1,0:T(8,128)(2,1)S(1)} %collective-permute-done.1.refs_1_, ...), custom_call_target="tpu_custom_call" | custom-call | flops 1000 | bytes 1000 | tf_op jit(solution)/shard_map/partial_ladder/pallas_call | solution.py:165
  31.3 1.6 %collective-permute-start.7 = (f16[528,128]{1,0:T(8,128)(2,1)S(1)}, f16[528,128]{1,0:T(8,128)(2,1)S(1)}, u32[]{:S(2)}, u32[]{:S(2)}) collective-permute-start(f16[528,128]{1,0:T(8,128)(2,1)S(1)} %convert_element_type.72), channel_id=1, source_target_pairs={{0,2},{1,3},{2,0},{3,1},{4,6},{5,7},{6,4},{7,5},{8,10},{9,11},{10,... | collective-permute-start | bytes 405512 | tf_op jit(solution)/shard_map/ppermute | solution.py:109
  32.9 1.3 %collective-permute-done.5 = bf16[128,2048]{1,0:T(8,128)(2,1)} collective-permute-done((bf16[128,2048]{1,0:T(8,128)(2,1)}, bf16[128,2048]{1,0:T(8,128)(2,1)}, u32[]{:S(2)}, u32[]{:S(2)}) %collective-permute-start.5) | collective-permute-done | bytes 524320 | tf_op jit(solution)/shard_map/ppermute | solution.py:109
  34.2 1.1 broadcast_select_fusion.1.refs_1_
  35.3 1.5 %collective-permute-done.3.refs_0_ = bf16[128,2048]{1,0:T(8,128)(2,1)S(1)} collective-permute-done((bf16[128,2048]{1,0:T(8,128)(2,1)S(1)}, bf16[128,2048]{1,0:T(8,128)(2,1)S(1)}, u32[]{:S(2)}, u32[]{:S(2)}) %collective-permute-start.3) | collective-permute-done | bytes 524320 | tf_op jit(solution)/shard_map/ppermute | solution.py:109
  36.8 2.3 %collective-permute-start.9 = (bf16[128,2048]{1,0:T(8,128)(2,1)}, bf16[128,2048]{1,0:T(8,128)(2,1)S(1)}, u32[]{:S(2)}, u32[]{:S(2)}) collective-permute-start(bf16[128,2048]{1,0:T(8,128)(2,1)} %collective-permute-done.4), channel_id=1, source_target_pairs={{0,8},{1,9},{2,10},{3,11},{4,12},{5,13},{6,14},{7,15},{8,0},{9,1},... | collective-permute-start | bytes 1572872 | tf_op jit(solution)/shard_map/ppermute | solution.py:109
  39.1 1.4 %collective-permute-start.8 = (bf16[128,2048]{1,0:T(8,128)(2,1)S(1)}, bf16[128,2048]{1,0:T(8,128)(2,1)S(1)}, u32[]{:S(2)}, u32[]{:S(2)}) collective-permute-start(bf16[128,2048]{1,0:T(8,128)(2,1)S(1)} %broadcast_select_fusion.1.refs_1_), channel_id=1, source_target_pairs={{0,4},{1,5},{2,6},{3,7},{4,0},{5,1},{6,2},{7,3},{8,12},{9,13},{10,... | collective-permute-start | bytes 1572872 | tf_op jit(solution)/shard_map/ppermute | solution.py:109
  41.4 1.6 %collective-permute-start.12 = (f16[1040,128]{1,0:T(8,128)(2,1)S(1)}, f16[1040,128]{1,0:T(8,128)(2,1)S(1)}, u32[]{:S(2)}, u32[]{:S(2)}) collective-permute-start(f16[1040,128]{1,0:T(8,128)(2,1)S(1)} %convert_element_type.75), channel_id=1, source_target_pairs={{0,2},{1,3},{2,0},{3,1},{4,6},{5,7},{6,4},{7,5},{8,10},{9,11},{10,... | collective-permute-start | bytes 798728 | tf_op jit(solution)/shard_map/ppermute | solution.py:109
  43.3 2.1 %collective-permute-start.10 = (f16[528,128]{1,0:T(8,128)(2,1)S(1)}, f16[528,128]{1,0:T(8,128)(2,1)S(1)}, u32[]{:S(2)}, u32[]{:S(2)}) collective-permute-start(f16[528,128]{1,0:T(8,128)(2,1)S(1)} %convert_element_type.74), channel_id=1, source_target_pairs={{0,16},{1,17},{2,18},{3,19},{4,20},{5,21},{6,22},{7,23},{8,24},{9,... | collective-permute-start | bytes 405512 | tf_op jit(solution)/shard_map/ppermute | solution.py:109
  46.7 3.3 %partial_ladder.7.part = f32[4,64,2048]{2,1,0:T(8,128)S(1)} custom-call(s32[2]{0:T(128)S(1)} %pad_add_fusion.place, s32[24]{0:T(128)S(1)} %copy-done.6, s32[8,2]{1,0:T(8,128)S(1)} %copy.16.product, s32[8,2]{1,0:T(8,128)S(1)} %copy.17.summed, bf16[128,2048]{1,0:T(8,128)(2,1)S(1)} %collective-permute-done.3.refs_0_, ...), custom_call_target="tpu_custom_call" | custom-call | flops 1000 | bytes 1000 | tf_op jit(solution)/shard_map/partial_ladder/pallas_call | solution.py:165
  50.0 4.0 %collective-permute-done.10 = f16[528,128]{1,0:T(8,128)(2,1)S(1)} collective-permute-done((f16[528,128]{1,0:T(8,128)(2,1)S(1)}, f16[528,128]{1,0:T(8,128)(2,1)S(1)}, u32[]{:S(2)}, u32[]{:S(2)}) %collective-permute-start.10) | collective-permute-done | bytes 135200 | tf_op jit(solution)/shard_map/ppermute | solution.py:109
  54.0 0.7 collective-permute-done.9
  54.8 1.5 %collective-permute-start.13 = (bf16[128,2048]{1,0:T(8,128)(2,1)S(1)}, bf16[128,2048]{1,0:T(8,128)(2,1)S(1)}, u32[]{:S(2)}, u32[]{:S(2)}) collective-permute-start(bf16[128,2048]{1,0:T(8,128)(2,1)S(1)} %broadcast_select_fusion.refs_1_), channel_id=1, source_target_pairs={{0,4},{1,5},{2,6},{3,7},{4,0},{5,1},{6,2},{7,3},{8,12},{9,13},{10,... | collective-permute-start | bytes 1572872 | tf_op jit(solution)/shard_map/ppermute | solution.py:109
  56.9 3.8 %collective-permute-start.14 = (f16[1040,128]{1,0:T(8,128)(2,1)S(1)}, f16[1040,128]{1,0:T(8,128)(2,1)S(1)}, u32[]{:S(2)}, u32[]{:S(2)}) collective-permute-start(f16[1040,128]{1,0:T(8,128)(2,1)S(1)} %convert_element_type.77), channel_id=1, source_target_pairs={{0,16},{1,17},{2,18},{3,19},{4,20},{5,21},{6,22},{7,23},{8,24},{9,... | collective-permute-start | bytes 798728 | tf_op jit(solution)/shard_map/ppermute | solution.py:109
  61.2 1.6 %collective-permute-start.16 = (f16[1040,128]{1,0:T(8,128)(2,1)S(1)}, f16[1040,128]{1,0:T(8,128)(2,1)S(1)}, u32[]{:S(2)}, u32[]{:S(2)}) collective-permute-start(f16[1040,128]{1,0:T(8,128)(2,1)S(1)} %convert_element_type.78), channel_id=1, source_target_pairs={{0,2},{1,3},{2,0},{3,1},{4,6},{5,7},{6,4},{7,5},{8,10},{9,11},{10,... | collective-permute-start | bytes 798728 | tf_op jit(solution)/shard_map/ppermute | solution.py:109
  63.4 0.7 sort.16.refs_0_
  64.1 3.3 %partial_ladder.8.part = f32[4,64,2048]{2,1,0:T(8,128)S(1)} custom-call(s32[2]{0:T(128)S(1)} %pad_add_fusion.place, s32[24]{0:T(128)S(1)} %copy-done.6, s32[8,2]{1,0:T(8,128)S(1)} %copy.16.product, s32[8,2]{1,0:T(8,128)S(1)} %copy.17.summed, bf16[128,2048]{1,0:T(8,128)(2,1)S(1)} %collective-permute-done.8.refs_0_, ...), custom_call_target="tpu_custom_call" | custom-call | flops 1000 | bytes 1000 | tf_op jit(solution)/shard_map/partial_ladder/pallas_call | solution.py:165
  68.1 5.1 %collective-permute-done.14 = f16[1040,128]{1,0:T(8,128)(2,1)S(1)} collective-permute-done((f16[1040,128]{1,0:T(8,128)(2,1)S(1)}, f16[1040,128]{1,0:T(8,128)(2,1)S(1)}, u32[]{:S(2)}, u32[]{:S(2)}) %collective-permute-start.14) | collective-permute-done | bytes 266272 | tf_op jit(solution)/shard_map/ppermute | solution.py:109
  73.8 3.5 %collective-permute-done.18.sibling = f32[4,64,2048]{2,1,0:T(8,128)S(1)} collective-permute-done((f32[4,64,2048]{2,1,0:T(8,128)S(1)}, f32[4,64,2048]{2,1,0:T(8,128)S(1)}, u32[]{:S(2)}, u32[]{:S(2)}) %collective-permute-start.18) | collective-permute-done | bytes 2097184 | tf_op jit(solution)/shard_map/ppermute | solution.py:109
  77.8 1.6 %collective-permute-start.19 = (f16[1040,128]{1,0:T(8,128)(2,1)S(1)}, f16[1040,128]{1,0:T(8,128)(2,1)S(1)}, u32[]{:S(2)}, u32[]{:S(2)}) collective-permute-start(f16[1040,128]{1,0:T(8,128)(2,1)S(1)} %convert_element_type.82), channel_id=1, source_target_pairs={{0,2},{1,3},{2,0},{3,1},{4,6},{5,7},{6,4},{7,5},{8,10},{9,11},{10,... | collective-permute-start | bytes 798728 | tf_op jit(solution)/shard_map/ppermute | solution.py:109
  79.4 0.9 sort.19.refs_0_
  81.0 2.1 %partial_ladder.9.part = f32[4,32,2048]{2,1,0:T(8,128)S(1)} custom-call(s32[2]{0:T(128)S(1)} %pad_add_fusion.place, s32[24]{0:T(128)S(1)} %copy-done.6, s32[8,2]{1,0:T(8,128)S(1)} %copy.16.product, s32[8,2]{1,0:T(8,128)S(1)} %copy.17.summed, bf16[128,2048]{1,0:T(8,128)(2,1)S(1)} %collective-permute-done.13.refs_0_, bf16[2048,2048]{1,0:T(8,128)(2,1)S(1)} %bitcast.3), custom_call_target="tpu_custom_call" | custom-call | flops 1000 | bytes 1000 | tf_op jit(solution)/shard_map/partial_ladder/pallas_call | solution.py:165
  83.6 1.0 sort.22.refs_0_
  85.2 2.5 %collective-permute-done.17 = f16[1040,128]{1,0:T(8,128)(2,1)S(1)} collective-permute-done((f16[1040,128]{1,0:T(8,128)(2,1)S(1)}, f16[1040,128]{1,0:T(8,128)(2,1)S(1)}, u32[]{:S(2)}, u32[]{:S(2)}) %collective-permute-start.17) | collective-permute-done | bytes 266272 | tf_op jit(solution)/shard_map/ppermute | solution.py:109
  88.3 1.6 %collective-permute-start.21 = (f16[3,528,128]{2,1,0:T(8,128)(2,1)S(1)}, f16[3,528,128]{2,1,0:T(8,128)(2,1)S(1)}, u32[]{:S(2)}, u32[]{:S(2)}) collective-permute-start(f16[3,528,128]{2,1,0:T(8,128)(2,1)S(1)} %convert_element_type.81), channel_id=1, source_target_pairs={{0,2},{1,3},{2,0},{3,1},{4,6},{5,7},{6,4},{7,5},{8,10},{9,11},{10,... | collective-permute-start | bytes 1216520 | tf_op jit(solution)/shard_map/ppermute | solution.py:109
  90.7 1.6 %collective-permute-start.23 = (f16[528,128]{1,0:T(8,128)(2,1)S(1)}, f16[528,128]{1,0:T(8,128)(2,1)S(1)}, u32[]{:S(2)}, u32[]{:S(2)}) collective-permute-start(f16[528,128]{1,0:T(8,128)(2,1)S(1)} %convert_element_type.85), channel_id=1, source_target_pairs={{0,2},{1,3},{2,0},{3,1},{4,6},{5,7},{6,4},{7,5},{8,10},{9,11},{10,... | collective-permute-start | bytes 405512 | tf_op jit(solution)/shard_map/ppermute | solution.py:109
  93.5 10.0 %collective-permute-done.23 = f16[528,128]{1,0:T(8,128)(2,1)S(1)} collective-permute-done((f16[528,128]{1,0:T(8,128)(2,1)S(1)}, f16[528,128]{1,0:T(8,128)(2,1)S(1)}, u32[]{:S(2)}, u32[]{:S(2)}) %collective-permute-start.23) | collective-permute-done | bytes 135200 | tf_op jit(solution)/shard_map/ppermute | solution.py:109
  105.1 0.8 sort.24.own
  106.6 0.7 turn.5.refs_1_
  107.3 0.7 turn.6.refs_2_
  108.0 0.7 turn.7.refs_3_
  108.8 1.3 %gather.1.sums = f32[4,64,2048]{2,1,0:T(8,128)S(1)} custom-call(s32[2]{0:T(128)S(1)} %pad_add_fusion.place, f32[4,64,2048]{2,1,0:T(8,128)S(1)} %sort.24.own, f32[3,528,128]{2,1,0:T(8,128)S(1)} %convert_element_type.87.rest, f32[32,2048]{1,0:T(8,128)S(1)} %turn.4.refs_0_, f32[64,2048]{1,0:T(8,128)S(1)} %turn.5.refs_1_, f32[64,2048]{1,0:T(8,128)S(1)} %turn.6.refs_2_, ...), custom_call_target="tpu_custom_call" | custom-call | flops 1000 | bytes 1000 | tf_op jit(solution)/shard_map/gather/pallas_call | solution.py:291
  110.1 2.9 %collective-permute-done.25 = f16[528,128]{1,0:T(8,128)(2,1)S(1)} collective-permute-done((f16[528,128]{1,0:T(8,128)(2,1)S(1)}, f16[528,128]{1,0:T(8,128)(2,1)S(1)}, u32[]{:S(2)}, u32[]{:S(2)}) %collective-permute-start.25) | collective-permute-done | bytes 135200 | tf_op jit(solution)/shard_map/ppermute | solution.py:109
  113.2 2.8 %finish.1 = bf16[256,2048]{1,0:T(8,128)(2,1)} custom-call(s32[2]{0:T(128)S(1)} %pad_add_fusion.place, f32[4,64,2048]{2,1,0:T(8,128)S(1)} %gather.1.sums, f32[3,528,128]{2,1,0:T(8,128)S(1)} %convert_element_type.93.rest, f32[528,128]{1,0:T(8,128)S(1)} %convert_element_type.95.last), custom_call_target="tpu_custom_call" | custom-call | flops 1000 | bytes 1000 | tf_op jit(solution)/shard_map/finish/pallas_call | solution.py:321
  (86 shorter events, 14.6 us)
Async XLA Ops:
  0.0 15.2 %collective-permute-start.1 = (bf16[128,2048]{1,0:T(8,128)(2,1)}, bf16[128,2048]{1,0:T(8,128)(2,1)S(1)}, u32[]{:S(2)}, u32[]{:S(2)}) collective-permute-start(bf16[128,2048]{1,0:T(8,128)(2,1)} %refs_0_.1), channel_id=1, source_target_pairs={{0,8},{1,9},{2,10},{3,11},{4,12},{5,13},{6,14},{7,15},{8,0},{9,1},... | collective-permute-start | bytes 1572872 | tf_op jit(solution)/shard_map/ppermute | solution.py:109
  3.0 13.6 %collective-permute-start = (bf16[128,2048]{1,0:T(8,128)(2,1)}, bf16[128,2048]{1,0:T(8,128)(2,1)S(1)}, u32[]{:S(2)}, u32[]{:S(2)}) collective-permute-start(bf16[128,2048]{1,0:T(8,128)(2,1)} %refs_0_.1), channel_id=1, source_target_pairs={{0,4},{1,5},{2,6},{3,7},{4,0},{5,1},{6,2},{7,3},{8,12},{9,13},{10,... | collective-permute-start | bytes 1572872 | tf_op jit(solution)/shard_map/ppermute | solution.py:109
  4.5 12.9 %collective-permute-start.2 = (bf16[128,2048]{1,0:T(8,128)(2,1)}, bf16[128,2048]{1,0:T(8,128)(2,1)}, u32[]{:S(2)}, u32[]{:S(2)}) collective-permute-start(bf16[128,2048]{1,0:T(8,128)(2,1)} %refs_0_.1), channel_id=1, source_target_pairs={{8,16},{9,17},{10,18},{11,19},{12,20},{13,21},{14,22},{15,23},{16,... | collective-permute-start | bytes 1572872 | tf_op jit(solution)/shard_map/ppermute | solution.py:109
  7.6 3.4 %copy-start = (bf16[2048,2048]{1,0:T(8,128)(2,1)S(1)}, bf16[2048,2048]{1,0:T(8,128)(2,1)}, u32[]{:S(2)}) copy-start(bf16[2048,2048]{1,0:T(8,128)(2,1)} %refs_1_.3) | copy-start | bytes 25165828
  10.9 1.0 copy-start.2
  12.0 0.7 copy-start.5
  12.6 10.6 %copy-start.6 = (s32[24]{0:T(128)S(1)}, s32[24]{0:T(128)}, u32[]{:S(2)}) copy-start(s32[24]{0:T(128)} %irrep.9) | copy-start | bytes 292
  16.6 0.8 copy-start.3
  17.4 13.5 %collective-permute-start.6 = (f32[4,32,2048]{2,1,0:T(8,128)S(1)}, f32[4,32,2048]{2,1,0:T(8,128)S(1)}, u32[]{:S(2)}, u32[]{:S(2)}) collective-permute-start(f32[4,32,2048]{2,1,0:T(8,128)S(1)} %partial_ladder.5.part), channel_id=1, source_target_pairs={{0,1},{1,0},{2,3},{3,2},{4,5},{5,4},{6,7},{7,6},{8,9},{9,8},{10,11... | collective-permute-start | bytes 3145736 | tf_op jit(solution)/shard_map/ppermute | solution.py:109
  17.4 16.7 %collective-permute-start.5 = (bf16[128,2048]{1,0:T(8,128)(2,1)}, bf16[128,2048]{1,0:T(8,128)(2,1)}, u32[]{:S(2)}, u32[]{:S(2)}) collective-permute-start(bf16[128,2048]{1,0:T(8,128)(2,1)} %collective-permute-done.2), channel_id=1, source_target_pairs={{0,8},{1,9},{2,10},{3,11},{4,12},{5,13},{6,14},{7,15},{8,0},{9,1},... | collective-permute-start | bytes 1572872 | tf_op jit(solution)/shard_map/ppermute | solution.py:109
  21.2 14.0 %collective-permute-start.4 = (bf16[128,2048]{1,0:T(8,128)(2,1)S(1)}, bf16[128,2048]{1,0:T(8,128)(2,1)}, u32[]{:S(2)}, u32[]{:S(2)}) collective-permute-start(bf16[128,2048]{1,0:T(8,128)(2,1)S(1)} %collective-permute-done.1.refs_1_), channel_id=1, source_target_pairs={{8,16},{9,17},{10,18},{11,19},{12,20},{13,21},{14,22},{15,23},{16,... | collective-permute-start | bytes 1572872 | tf_op jit(solution)/shard_map/ppermute | solution.py:109
  22.7 14.1 %collective-permute-start.3 = (bf16[128,2048]{1,0:T(8,128)(2,1)S(1)}, bf16[128,2048]{1,0:T(8,128)(2,1)S(1)}, u32[]{:S(2)}, u32[]{:S(2)}) collective-permute-start(bf16[128,2048]{1,0:T(8,128)(2,1)S(1)} %collective-permute-done.1.refs_1_), channel_id=1, source_target_pairs={{0,4},{1,5},{2,6},{3,7},{4,0},{5,1},{6,2},{7,3},{8,12},{9,13},{10,... | collective-permute-start | bytes 1572872 | tf_op jit(solution)/shard_map/ppermute | solution.py:109
  23.3 3.4 %copy-start.1 = (bf16[2048,2048]{1,0:T(8,128)(2,1)S(1)}, bf16[2048,2048]{1,0:T(8,128)(2,1)}, u32[]{:S(2)}) copy-start(bf16[2048,2048]{1,0:T(8,128)(2,1)} %refs_1_.3) | copy-start | bytes 25165828
  26.7 1.0 copy-start.4
  31.0 15.7 %slice-start = ((s8[8388608]{0:T(1024)(128)(4,1)}), s8[4194304]{0:T(1024)(128)(4,1)S(1)}, s32[]{:S(2)}) async-start(s8[8388608]{0:T(1024)(128)(4,1)} %bitcast.2), calls=%async_computation | async-start | bytes 8388608
  31.3 5.5 %collective-permute-start.7 = (f16[528,128]{1,0:T(8,128)(2,1)S(1)}, f16[528,128]{1,0:T(8,128)(2,1)S(1)}, u32[]{:S(2)}, u32[]{:S(2)}) collective-permute-start(f16[528,128]{1,0:T(8,128)(2,1)S(1)} %convert_element_type.72), channel_id=1, source_target_pairs={{0,2},{1,3},{2,0},{3,1},{4,6},{5,7},{6,4},{7,5},{8,10},{9,11},{10,... | collective-permute-start | bytes 405512 | tf_op jit(solution)/shard_map/ppermute | solution.py:109
  36.8 9.9 %slice-start.1 = ((s8[8388608]{0:T(1024)(128)(4,1)}), s8[4194304]{0:T(1024)(128)(4,1)S(1)}, s32[]{:S(2)}) async-start(s8[8388608]{0:T(1024)(128)(4,1)} %bitcast.2), calls=%async_computation.1 | async-start | bytes 8388608
  36.8 4.2 %collective-permute-start.11 = (f32[4,64,2048]{2,1,0:T(8,128)S(1)}, f32[4,64,2048]{2,1,0:T(8,128)S(1)}, u32[]{:S(2)}, u32[]{:S(2)}) collective-permute-start(f32[4,64,2048]{2,1,0:T(8,128)S(1)} %partial_ladder.6.part), channel_id=1, source_target_pairs={{0,1},{1,0},{2,3},{3,2},{4,5},{5,4},{6,7},{7,6},{8,9},{9,8},{10,11... | collective-permute-start | bytes 6291464 | tf_op jit(solution)/shard_map/ppermute | solution.py:109
  36.8 17.9 %collective-permute-start.9 = (bf16[128,2048]{1,0:T(8,128)(2,1)}, bf16[128,2048]{1,0:T(8,128)(2,1)S(1)}, u32[]{:S(2)}, u32[]{:S(2)}) collective-permute-start(bf16[128,2048]{1,0:T(8,128)(2,1)} %collective-permute-done.4), channel_id=1, source_target_pairs={{0,8},{1,9},{2,10},{3,11},{4,12},{5,13},{6,14},{7,15},{8,0},{9,1},... | collective-permute-start | bytes 1572872 | tf_op jit(solution)/shard_map/ppermute | solution.py:109
  39.1 15.6 %collective-permute-start.8 = (bf16[128,2048]{1,0:T(8,128)(2,1)S(1)}, bf16[128,2048]{1,0:T(8,128)(2,1)S(1)}, u32[]{:S(2)}, u32[]{:S(2)}) collective-permute-start(bf16[128,2048]{1,0:T(8,128)(2,1)S(1)} %broadcast_select_fusion.1.refs_1_), channel_id=1, source_target_pairs={{0,4},{1,5},{2,6},{3,7},{4,0},{5,1},{6,2},{7,3},{8,12},{9,13},{10,... | collective-permute-start | bytes 1572872 | tf_op jit(solution)/shard_map/ppermute | solution.py:109
  41.4 13.3 %collective-permute-start.12 = (f16[1040,128]{1,0:T(8,128)(2,1)S(1)}, f16[1040,128]{1,0:T(8,128)(2,1)S(1)}, u32[]{:S(2)}, u32[]{:S(2)}) collective-permute-start(f16[1040,128]{1,0:T(8,128)(2,1)S(1)} %convert_element_type.75), channel_id=1, source_target_pairs={{0,2},{1,3},{2,0},{3,1},{4,6},{5,7},{6,4},{7,5},{8,10},{9,11},{10,... | collective-permute-start | bytes 798728 | tf_op jit(solution)/shard_map/ppermute | solution.py:109
  43.3 10.7 %collective-permute-start.10 = (f16[528,128]{1,0:T(8,128)(2,1)S(1)}, f16[528,128]{1,0:T(8,128)(2,1)S(1)}, u32[]{:S(2)}, u32[]{:S(2)}) collective-permute-start(f16[528,128]{1,0:T(8,128)(2,1)S(1)} %convert_element_type.74), channel_id=1, source_target_pairs={{0,16},{1,17},{2,18},{3,19},{4,20},{5,21},{6,22},{7,23},{8,24},{9,... | collective-permute-start | bytes 405512 | tf_op jit(solution)/shard_map/ppermute | solution.py:109
  54.7 6.0 %collective-permute-start.15 = (f32[4,64,2048]{2,1,0:T(8,128)S(1)}, f32[4,64,2048]{2,1,0:T(8,128)S(1)}, u32[]{:S(2)}, u32[]{:S(2)}) collective-permute-start(f32[4,64,2048]{2,1,0:T(8,128)S(1)} %partial_ladder.7.part), channel_id=1, source_target_pairs={{0,1},{1,0},{2,3},{3,2},{4,5},{5,4},{6,7},{7,6},{8,9},{9,8},{10,11... | collective-permute-start | bytes 6291464 | tf_op jit(solution)/shard_map/ppermute | solution.py:109
  54.8 18.4 %collective-permute-start.13 = (bf16[128,2048]{1,0:T(8,128)(2,1)S(1)}, bf16[128,2048]{1,0:T(8,128)(2,1)S(1)}, u32[]{:S(2)}, u32[]{:S(2)}) collective-permute-start(bf16[128,2048]{1,0:T(8,128)(2,1)S(1)} %broadcast_select_fusion.refs_1_), channel_id=1, source_target_pairs={{0,4},{1,5},{2,6},{3,7},{4,0},{5,1},{6,2},{7,3},{8,12},{9,13},{10,... | collective-permute-start | bytes 1572872 | tf_op jit(solution)/shard_map/ppermute | solution.py:109
  56.9 16.3 %collective-permute-start.14 = (f16[1040,128]{1,0:T(8,128)(2,1)S(1)}, f16[1040,128]{1,0:T(8,128)(2,1)S(1)}, u32[]{:S(2)}, u32[]{:S(2)}) collective-permute-start(f16[1040,128]{1,0:T(8,128)(2,1)S(1)} %convert_element_type.77), channel_id=1, source_target_pairs={{0,16},{1,17},{2,18},{3,19},{4,20},{5,21},{6,22},{7,23},{8,24},{9,... | collective-permute-start | bytes 798728 | tf_op jit(solution)/shard_map/ppermute | solution.py:109
  61.2 12.0 %collective-permute-start.16 = (f16[1040,128]{1,0:T(8,128)(2,1)S(1)}, f16[1040,128]{1,0:T(8,128)(2,1)S(1)}, u32[]{:S(2)}, u32[]{:S(2)}) collective-permute-start(f16[1040,128]{1,0:T(8,128)(2,1)S(1)} %convert_element_type.78), channel_id=1, source_target_pairs={{0,2},{1,3},{2,0},{3,1},{4,6},{5,7},{6,4},{7,5},{8,10},{9,11},{10,... | collective-permute-start | bytes 798728 | tf_op jit(solution)/shard_map/ppermute | solution.py:109
  73.2 4.2 %collective-permute-start.18 = (f32[4,64,2048]{2,1,0:T(8,128)S(1)}, f32[4,64,2048]{2,1,0:T(8,128)S(1)}, u32[]{:S(2)}, u32[]{:S(2)}) collective-permute-start(f32[4,64,2048]{2,1,0:T(8,128)S(1)} %partial_ladder.8.part), channel_id=1, source_target_pairs={{0,1},{1,0},{2,3},{3,2},{4,5},{5,4},{6,7},{7,6},{8,9},{9,8},{10,11... | collective-permute-start | bytes 6291464 | tf_op jit(solution)/shard_map/ppermute | solution.py:109
  73.7 14.0 %collective-permute-start.17 = (f16[1040,128]{1,0:T(8,128)(2,1)S(1)}, f16[1040,128]{1,0:T(8,128)(2,1)S(1)}, u32[]{:S(2)}, u32[]{:S(2)}) collective-permute-start(f16[1040,128]{1,0:T(8,128)(2,1)S(1)} %convert_element_type.80), channel_id=1, source_target_pairs={{0,16},{1,17},{2,18},{3,19},{4,20},{5,21},{6,22},{7,23},{8,24},{9,... | collective-permute-start | bytes 798728 | tf_op jit(solution)/shard_map/ppermute | solution.py:109
  77.8 9.9 %collective-permute-start.19 = (f16[1040,128]{1,0:T(8,128)(2,1)S(1)}, f16[1040,128]{1,0:T(8,128)(2,1)S(1)}, u32[]{:S(2)}, u32[]{:S(2)}) collective-permute-start(f16[1040,128]{1,0:T(8,128)(2,1)S(1)} %convert_element_type.82), channel_id=1, source_target_pairs={{0,2},{1,3},{2,0},{3,1},{4,6},{5,7},{6,4},{7,5},{8,10},{9,11},{10,... | collective-permute-start | bytes 798728 | tf_op jit(solution)/shard_map/ppermute | solution.py:109
  87.7 2.7 %collective-permute-start.22 = (f32[4,32,2048]{2,1,0:T(8,128)S(1)}, f32[4,32,2048]{2,1,0:T(8,128)S(1)}, u32[]{:S(2)}, u32[]{:S(2)}) collective-permute-start(f32[4,32,2048]{2,1,0:T(8,128)S(1)} %partial_ladder.9.part), channel_id=1, source_target_pairs={{0,1},{1,0},{2,3},{3,2},{4,5},{5,4},{6,7},{7,6},{8,9},{9,8},{10,11... | collective-permute-start | bytes 3145736 | tf_op jit(solution)/shard_map/ppermute | solution.py:109
  88.3 16.6 %collective-permute-start.21 = (f16[3,528,128]{2,1,0:T(8,128)(2,1)S(1)}, f16[3,528,128]{2,1,0:T(8,128)(2,1)S(1)}, u32[]{:S(2)}, u32[]{:S(2)}) collective-permute-start(f16[3,528,128]{2,1,0:T(8,128)(2,1)S(1)} %convert_element_type.81), channel_id=1, source_target_pairs={{0,2},{1,3},{2,0},{3,1},{4,6},{5,7},{6,4},{7,5},{8,10},{9,11},{10,... | collective-permute-start | bytes 1216520 | tf_op jit(solution)/shard_map/ppermute | solution.py:109
  89.9 15.1 %collective-permute-start.20 = (f16[1040,128]{1,0:T(8,128)(2,1)S(1)}, f16[1040,128]{1,0:T(8,128)(2,1)S(1)}, u32[]{:S(2)}, u32[]{:S(2)}) collective-permute-start(f16[1040,128]{1,0:T(8,128)(2,1)S(1)} %convert_element_type.84), channel_id=1, source_target_pairs={{0,16},{1,17},{2,18},{3,19},{4,20},{5,21},{6,22},{7,23},{8,24},{9,... | collective-permute-start | bytes 798728 | tf_op jit(solution)/shard_map/ppermute | solution.py:109
  90.7 12.8 %collective-permute-start.23 = (f16[528,128]{1,0:T(8,128)(2,1)S(1)}, f16[528,128]{1,0:T(8,128)(2,1)S(1)}, u32[]{:S(2)}, u32[]{:S(2)}) collective-permute-start(f16[528,128]{1,0:T(8,128)(2,1)S(1)} %convert_element_type.85), channel_id=1, source_target_pairs={{0,2},{1,3},{2,0},{3,1},{4,6},{5,7},{6,4},{7,5},{8,10},{9,11},{10,... | collective-permute-start | bytes 405512 | tf_op jit(solution)/shard_map/ppermute | solution.py:109
  92.9 20.2 %collective-permute-start.24 = (f16[3,528,128]{2,1,0:T(8,128)(2,1)S(1)}, f16[3,528,128]{2,1,0:T(8,128)(2,1)S(1)}, u32[]{:S(2)}, u32[]{:S(2)}) collective-permute-start(f16[3,528,128]{2,1,0:T(8,128)(2,1)S(1)} %convert_element_type.92), channel_id=1, source_target_pairs={{0,2},{1,3},{2,0},{3,1},{4,6},{5,7},{6,4},{7,5},{8,10},{9,11},{10,... | collective-permute-start | bytes 1216520 | tf_op jit(solution)/shard_map/ppermute | solution.py:109
  105.0 8.1 %collective-permute-start.25 = (f16[528,128]{1,0:T(8,128)(2,1)S(1)}, f16[528,128]{1,0:T(8,128)(2,1)S(1)}, u32[]{:S(2)}, u32[]{:S(2)}) collective-permute-start(f16[528,128]{1,0:T(8,128)(2,1)S(1)} %convert_element_type.94), channel_id=1, source_target_pairs={{0,16},{1,17},{2,18},{3,19},{4,20},{5,21},{6,22},{7,23},{8,24},{9,... | collective-permute-start | bytes 405512 | tf_op jit(solution)/shard_map/ppermute | solution.py:109

commit v6 on v5

--- a/solution.py
+++ b/solution.py
@@ -299,7 +299,7 @@
     )(place, own, rest, *done)
 
 
-def finish_kernel(place, sums, rest, last, out, all_sums, total):
+def finish_kernel(place, sums, rest, last, out, all_sums, total, result, sems):
     all_sums[...] = sums[...]
     place_rest(place, all_sums, rest, 1)
     value = turn(decoded(last))
@@ -311,9 +311,14 @@
     total[...] = all_sums[...].astype(jnp.bfloat16)
     natural = natural_order()
     value = total[...].reshape(OWNED, WIDTH)
+    copies = []
     for p in range(PANELS):
         cut = slice(p * TP, (p + 1) * TP)
-        out[:, cut] = matmul(natural, value[:, cut]).astype(jnp.bfloat16)
+        result[:, cut] = matmul(natural, value[:, cut]).astype(jnp.bfloat16)
+        copies.append(pltpu.make_async_copy(result.at[:, pl.ds(p * TP, TP)], out.at[:, pl.ds(p * TP, TP)], sems.at[p]))
+        copies[-1].start()
+    for copy in copies:
+        copy.wait()
 
 
 def finish(place, sums, rest, last):
@@ -321,9 +326,14 @@
     return pl.pallas_call(
         finish_kernel,
         in_specs=[pl.BlockSpec(memory_space=pltpu.SMEM), vmem, vmem, vmem],
-        out_specs=vmem,
+        out_specs=pl.BlockSpec(memory_space=pl.ANY),
         out_shape=jax.ShapeDtypeStruct((OWNED, WIDTH), jnp.bfloat16),
-        scratch_shapes=[pltpu.VMEM((4, PART, WIDTH), jnp.float32), pltpu.VMEM((4, PART, WIDTH), jnp.bfloat16)],
+        scratch_shapes=[
+            pltpu.VMEM((4, PART, WIDTH), jnp.float32),
+            pltpu.VMEM((4, PART, WIDTH), jnp.bfloat16),
+            pltpu.VMEM((OWNED, WIDTH), jnp.bfloat16),
+            pltpu.SemaphoreType.DMA((PANELS,)),
+        ],
         compiler_params=params(14),
         cost_estimate=light(),
         name="finish",
@@ -436,10 +446,10 @@
     part2 = partial_ladder(tables, integrals, beside1, here2)
     own = sort_own(place, CHUNKS[0], pair0, mine0)
     owed_here = sort_owed(place, 0, pair0)
+    here3 = jnp.where(inner, crossed, here3)
     beside2, here3, other0, own, owed_here, pair1, over1, part2 = together(
         beside2, here3, other0, own, owed_here, pair1, over1, part2
     )
-    here3 = jnp.where(inner, crossed, here3)
 
     beside3 = across_x(here3)
     mine1, sent = add_chips(pair1, over1)
@@ -477,8 +487,8 @@
     own = sort_own(place, CHUNKS[3], pair3, mine3, own)
     owed_beside = wire(sort_owed(place, 3, pair4, owed_beside, across=1))
     mine4, ready4 = add_chips(pair4, over4)
-    other0, other1, other2, other3, own, came_here, pair4, mine4, ready4 = together(
-        other0, other1, other2, other3, own, came_here, pair4, mine4, ready4
+    other0, other1, other2, other3, own, pair4, mine4, ready4 = together(
+        other0, other1, other2, other3, own, pair4, mine4, ready4
     )
 
     sent, *others = together(ready4, other0, other1, other2, other3)

time: 116 us -> 116 us (level)
  starting transfers between devices: 33.2 us -> 30.8 us
  waiting for transfers between devices: 35.1 us -> 37.4 us
    ppermute x26, starting transfers between devices: 33.2 us -> 30.8 us  [send(): return lax.ppermute(value, ('row', 'col'), pairs)]
    ppermute x26, waiting for transfers between devices: 35.1 us -> 37.4 us  [send(): return lax.ppermute(value, ('row', 'col'), pairs)]
    unnamed x20 -> x18, local copies, waits for them, and re-layouts: 11.8 us -> 11.8 us
  transfers between devices with their start and end apart: 26 -> 26, of which waited for: 14 -> 12; matrix products, arithmetic and copies ran while one was open for 3% -> 3% of each run, Pallas kernels for 26% -> 26%
where the time goes in v6:
time: 116 us
  waiting for transfers between devices  37.4 us (32%)
  Pallas kernels  32.8 us (28%)
  starting transfers between devices  30.8 us (27%)
  local copies, waits for them, and re-layouts  11.8 us (10%)
  other arithmetic  2.24 us (2%)
    ppermute x26, waiting for transfers between devices, send(): return lax.ppermute(value, ('row', 'col'), pairs)  37.4 us
    ppermute x26, starting transfers between devices, send(): return lax.ppermute(value, ('row', 'col'), pairs)  30.8 us
    pallas_call x5, Pallas kernels, partial_ladder(): pl.pallas_call(ladder_kernel, in_specs=[pl.BlockSpec(memory_space=pltpu.S...  13.9 us
    unnamed x18, local copies, waits for them, and re-layouts  11.8 us
    pallas_call x13, Pallas kernels, sort(): pl.pallas_call(functools.partial(kernel, steps), in_specs=[pl.BlockSpec(m...  8.62 us
    pallas_call x4, Pallas kernels, turned(): pl.pallas_call(turn_kernel, out_shape=jax.ShapeDtypeStruct(((arrived.shap...  2.64 us
    pallas_call x1, Pallas kernels, finish(): pl.pallas_call(finish_kernel, in_specs=[pl.BlockSpec(memory_space=pltpu.S...  2.62 us
  transfers between devices with their start and end apart: 26, of which 12 were waited for; matrix products, arithmetic and copies ran while one was open for 3% of the time, Pallas kernels for 26%

profile of v6, /device:TPU:0, one launch (start us, length us, event | category | flops | bytes accessed | tf_op | source)
XLA Modules:
  0.0 115.7 jit_solution(710300418600412267)
XLA Ops:
  0.0 3.0 %collective-permute-start.1 = (bf16[128,2048]{1,0:T(8,128)(2,1)}, bf16[128,2048]{1,0:T(8,128)(2,1)S(1)}, u32[]{:S(2)}, u32[]{:S(2)}) collective-permute-start(bf16[128,2048]{1,0:T(8,128)(2,1)} %refs_0_.1), channel_id=1, source_target_pairs={{0,8},{1,9},{2,10},{3,11},{4,12},{5,13},{6,14},{7,15},{8,0},{9,1},... | collective-permute-start | bytes 1572872 | tf_op jit(solution)/shard_map/ppermute | solution.py:109
  3.0 1.5 %collective-permute-start = (bf16[128,2048]{1,0:T(8,128)(2,1)}, bf16[128,2048]{1,0:T(8,128)(2,1)S(1)}, u32[]{:S(2)}, u32[]{:S(2)}) collective-permute-start(bf16[128,2048]{1,0:T(8,128)(2,1)} %refs_0_.1), channel_id=1, source_target_pairs={{0,4},{1,5},{2,6},{3,7},{4,0},{5,1},{6,2},{7,3},{8,12},{9,13},{10,... | collective-permute-start | bytes 1572872 | tf_op jit(solution)/shard_map/ppermute | solution.py:109
  4.5 1.4 %collective-permute-start.2 = (bf16[128,2048]{1,0:T(8,128)(2,1)}, bf16[128,2048]{1,0:T(8,128)(2,1)}, u32[]{:S(2)}, u32[]{:S(2)}) collective-permute-start(bf16[128,2048]{1,0:T(8,128)(2,1)} %refs_0_.1), channel_id=1, source_target_pairs={{8,16},{9,17},{10,18},{11,19},{12,20},{13,21},{14,22},{15,23},{16,... | collective-permute-start | bytes 1572872 | tf_op jit(solution)/shard_map/ppermute | solution.py:109
  6.0 0.8 copy.16.product
  6.7 0.8 copy.17.summed
  7.5 3.4 %copy-done = bf16[2048,2048]{1,0:T(8,128)(2,1)S(1)} copy-done((bf16[2048,2048]{1,0:T(8,128)(2,1)S(1)}, bf16[2048,2048]{1,0:T(8,128)(2,1)}, u32[]{:S(2)}) %copy-start) | copy-done | bytes 8388632
  10.9 1.0 copy-done.3
  12.6 2.1 %partial_ladder.5.part = f32[4,32,2048]{2,1,0:T(8,128)S(1)} custom-call(s32[2]{0:T(128)S(1)} %pad_add_fusion.place, s32[24]{0:T(128)S(1)} %copy-done.6, s32[8,2]{1,0:T(8,128)S(1)} %copy.16.product, s32[8,2]{1,0:T(8,128)S(1)} %copy.17.summed, bf16[128,2048]{1,0:T(8,128)(2,1)S(1)} %copy-done.3, bf16[2048,2048]{1,0:T(8,128)(2,1)S(1)} %copy-done), custom_call_target="tpu_custom_call" | custom-call | flops 1000 | bytes 1000 | tf_op jit(solution)/shard_map/partial_ladder/pallas_call | solution.py:165
  15.2 1.5 %collective-permute-done.refs_0_ = bf16[128,2048]{1,0:T(8,128)(2,1)S(1)} collective-permute-done((bf16[128,2048]{1,0:T(8,128)(2,1)}, bf16[128,2048]{1,0:T(8,128)(2,1)S(1)}, u32[]{:S(2)}, u32[]{:S(2)}) %collective-permute-start) | collective-permute-done | bytes 524320 | tf_op jit(solution)/shard_map/ppermute | solution.py:109
  16.6 0.8 copy-done.4
  17.4 3.8 %collective-permute-start.5 = (bf16[128,2048]{1,0:T(8,128)(2,1)}, bf16[128,2048]{1,0:T(8,128)(2,1)}, u32[]{:S(2)}, u32[]{:S(2)}) collective-permute-start(bf16[128,2048]{1,0:T(8,128)(2,1)} %collective-permute-done.2), channel_id=1, source_target_pairs={{0,8},{1,9},{2,10},{3,11},{4,12},{5,13},{6,14},{7,15},{8,0},{9,1},... | collective-permute-start | bytes 1572872 | tf_op jit(solution)/shard_map/ppermute | solution.py:109
  21.2 1.5 %collective-permute-start.4 = (bf16[128,2048]{1,0:T(8,128)(2,1)S(1)}, bf16[128,2048]{1,0:T(8,128)(2,1)}, u32[]{:S(2)}, u32[]{:S(2)}) collective-permute-start(bf16[128,2048]{1,0:T(8,128)(2,1)S(1)} %collective-permute-done.1.refs_1_), channel_id=1, source_target_pairs={{8,16},{9,17},{10,18},{11,19},{12,20},{13,21},{14,22},{15,23},{16,... | collective-permute-start | bytes 1572872 | tf_op jit(solution)/shard_map/ppermute | solution.py:109
  23.3 3.4 %copy-done.1 = bf16[2048,2048]{1,0:T(8,128)(2,1)S(1)} copy-done((bf16[2048,2048]{1,0:T(8,128)(2,1)S(1)}, bf16[2048,2048]{1,0:T(8,128)(2,1)}, u32[]{:S(2)}) %copy-start.1) | copy-done | bytes 8388632
  26.6 1.0 copy-done.5
  27.7 3.3 %partial_ladder.6.part = f32[4,64,2048]{2,1,0:T(8,128)S(1)} custom-call(s32[2]{0:T(128)S(1)} %pad_add_fusion.place, s32[24]{0:T(128)S(1)} %copy-done.7, s32[8,2]{1,0:T(8,128)S(1)} %copy.16.product, s32[8,2]{1,0:T(8,128)S(1)} %copy.17.summed, bf16[128,2048]{1,0:T(8,128)(2,1)S(1)} %copy-done.5, bf16[128,2048]{1,0:T(8,128)(2,1)S(1)} %collective-permute-done.1.refs_1_, ...), custom_call_target="tpu_custom_call" | custom-call | flops 1000 | bytes 1000 | tf_op jit(solution)/shard_map/partial_ladder/pallas_call | solution.py:165
  31.2 1.6 %collective-permute-start.7 = (f16[528,128]{1,0:T(8,128)(2,1)S(1)}, f16[528,128]{1,0:T(8,128)(2,1)S(1)}, u32[]{:S(2)}, u32[]{:S(2)}) collective-permute-start(f16[528,128]{1,0:T(8,128)(2,1)S(1)} %convert_element_type.72), channel_id=1, source_target_pairs={{0,2},{1,3},{2,0},{3,1},{4,6},{5,7},{6,4},{7,5},{8,10},{9,11},{10,... | collective-permute-start | bytes 405512 | tf_op jit(solution)/shard_map/ppermute | solution.py:109
  32.8 1.3 %collective-permute-done.5 = bf16[128,2048]{1,0:T(8,128)(2,1)} collective-permute-done((bf16[128,2048]{1,0:T(8,128)(2,1)}, bf16[128,2048]{1,0:T(8,128)(2,1)}, u32[]{:S(2)}, u32[]{:S(2)}) %collective-permute-start.5) | collective-permute-done | bytes 524320 | tf_op jit(solution)/shard_map/ppermute | solution.py:109
  34.2 1.2 %broadcast_select_fusion.1.refs_1_ = bf16[128,2048]{1,0:T(8,128)(2,1)S(1)} fusion(bf16[128,2048]{1,0:T(8,128)(2,1)} %collective-permute-done.2, bf16[128,2048]{1,0:T(8,128)(2,1)} %collective-permute-done.5, pred[]{:T(512)S(6)} %or.3), kind=kLoop, calls=%fused_computation.1 | loop fusion | flops 262144 | bytes 1572865 | tf_op jit(solution)/shard_map/jit(_where)/select_n | solution.py:437
  35.4 1.4 %collective-permute-done.3.refs_0_ = bf16[128,2048]{1,0:T(8,128)(2,1)S(1)} collective-permute-done((bf16[128,2048]{1,0:T(8,128)(2,1)S(1)}, bf16[128,2048]{1,0:T(8,128)(2,1)S(1)}, u32[]{:S(2)}, u32[]{:S(2)}) %collective-permute-start.3) | collective-permute-done | bytes 524320 | tf_op jit(solution)/shard_map/ppermute | solution.py:109
  36.8 2.2 %collective-permute-start.9 = (bf16[128,2048]{1,0:T(8,128)(2,1)}, bf16[128,2048]{1,0:T(8,128)(2,1)S(1)}, u32[]{:S(2)}, u32[]{:S(2)}) collective-permute-start(bf16[128,2048]{1,0:T(8,128)(2,1)} %collective-permute-done.4), channel_id=1, source_target_pairs={{0,8},{1,9},{2,10},{3,11},{4,12},{5,13},{6,14},{7,15},{8,0},{9,1},... | collective-permute-start | bytes 1572872 | tf_op jit(solution)/shard_map/ppermute | solution.py:109
  39.0 1.4 %collective-permute-start.8 = (bf16[128,2048]{1,0:T(8,128)(2,1)S(1)}, bf16[128,2048]{1,0:T(8,128)(2,1)S(1)}, u32[]{:S(2)}, u32[]{:S(2)}) collective-permute-start(bf16[128,2048]{1,0:T(8,128)(2,1)S(1)} %broadcast_select_fusion.1.refs_1_), channel_id=1, source_target_pairs={{0,4},{1,5},{2,6},{3,7},{4,0},{5,1},{6,2},{7,3},{8,12},{9,13},{10,... | collective-permute-start | bytes 1572872 | tf_op jit(solution)/shard_map/ppermute | solution.py:109
  41.4 1.4 %collective-permute-start.10 = (f16[528,128]{1,0:T(8,128)(2,1)S(1)}, f16[528,128]{1,0:T(8,128)(2,1)S(1)}, u32[]{:S(2)}, u32[]{:S(2)}) collective-permute-start(f16[528,128]{1,0:T(8,128)(2,1)S(1)} %convert_element_type.74), channel_id=1, source_target_pairs={{0,16},{1,17},{2,18},{3,19},{4,20},{5,21},{6,22},{7,23},{8,24},{9,... | collective-permute-start | bytes 405512 | tf_op jit(solution)/shard_map/ppermute | solution.py:109
  42.8 0.7 sort.13.refs_0_
  43.5 3.3 %partial_ladder.7.part = f32[4,64,2048]{2,1,0:T(8,128)S(1)} custom-call(s32[2]{0:T(128)S(1)} %pad_add_fusion.place, s32[24]{0:T(128)S(1)} %copy-done.7, s32[8,2]{1,0:T(8,128)S(1)} %copy.16.product, s32[8,2]{1,0:T(8,128)S(1)} %copy.17.summed, bf16[128,2048]{1,0:T(8,128)(2,1)S(1)} %collective-permute-done.3.refs_0_, ...), custom_call_target="tpu_custom_call" | custom-call | flops 1000 | bytes 1000 | tf_op jit(solution)/shard_map/partial_ladder/pallas_call | solution.py:165
  47.2 1.1 collective-permute-start.12
  48.3 6.4 %collective-permute-done.9 = bf16[128,2048]{1,0:T(8,128)(2,1)S(1)} collective-permute-done((bf16[128,2048]{1,0:T(8,128)(2,1)}, bf16[128,2048]{1,0:T(8,128)(2,1)S(1)}, u32[]{:S(2)}, u32[]{:S(2)}) %collective-permute-start.9) | collective-permute-done | bytes 524320 | tf_op jit(solution)/shard_map/ppermute | solution.py:109
  54.9 1.5 %collective-permute-start.13 = (bf16[128,2048]{1,0:T(8,128)(2,1)S(1)}, bf16[128,2048]{1,0:T(8,128)(2,1)S(1)}, u32[]{:S(2)}, u32[]{:S(2)}) collective-permute-start(bf16[128,2048]{1,0:T(8,128)(2,1)S(1)} %broadcast_select_fusion.refs_1_), channel_id=1, source_target_pairs={{0,4},{1,5},{2,6},{3,7},{4,0},{5,1},{6,2},{7,3},{8,12},{9,13},{10,... | collective-permute-start | bytes 1572872 | tf_op jit(solution)/shard_map/ppermute | solution.py:109
  57.0 2.5 %collective-permute-start.14 = (f16[1040,128]{1,0:T(8,128)(2,1)S(1)}, f16[1040,128]{1,0:T(8,128)(2,1)S(1)}, u32[]{:S(2)}, u32[]{:S(2)}) collective-permute-start(f16[1040,128]{1,0:T(8,128)(2,1)S(1)} %convert_element_type.77), channel_id=1, source_target_pairs={{0,16},{1,17},{2,18},{3,19},{4,20},{5,21},{6,22},{7,23},{8,24},{9,... | collective-permute-start | bytes 798728 | tf_op jit(solution)/shard_map/ppermute | solution.py:109
  60.0 1.6 %collective-permute-start.16 = (f16[1040,128]{1,0:T(8,128)(2,1)S(1)}, f16[1040,128]{1,0:T(8,128)(2,1)S(1)}, u32[]{:S(2)}, u32[]{:S(2)}) collective-permute-start(f16[1040,128]{1,0:T(8,128)(2,1)S(1)} %convert_element_type.78), channel_id=1, source_target_pairs={{0,2},{1,3},{2,0},{3,1},{4,6},{5,7},{6,4},{7,5},{8,10},{9,11},{10,... | collective-permute-start | bytes 798728 | tf_op jit(solution)/shard_map/ppermute | solution.py:109
  62.2 0.7 sort.16.refs_0_
  62.9 3.3 %partial_ladder.8.part = f32[4,64,2048]{2,1,0:T(8,128)S(1)} custom-call(s32[2]{0:T(128)S(1)} %pad_add_fusion.place, s32[24]{0:T(128)S(1)} %copy-done.7, s32[8,2]{1,0:T(8,128)S(1)} %copy.16.product, s32[8,2]{1,0:T(8,128)S(1)} %copy.17.summed, bf16[128,2048]{1,0:T(8,128)(2,1)S(1)} %collective-permute-done.8.refs_0_, ...), custom_call_target="tpu_custom_call" | custom-call | flops 1000 | bytes 1000 | tf_op jit(solution)/shard_map/partial_ladder/pallas_call | solution.py:165
  66.2 0.7 sort.15.refs_0_
  66.9 5.2 %collective-permute-done.14 = f16[1040,128]{1,0:T(8,128)(2,1)S(1)} collective-permute-done((f16[1040,128]{1,0:T(8,128)(2,1)S(1)}, f16[1040,128]{1,0:T(8,128)(2,1)S(1)}, u32[]{:S(2)}, u32[]{:S(2)}) %collective-permute-start.14) | collective-permute-done | bytes 266272 | tf_op jit(solution)/shard_map/ppermute | solution.py:109
  72.7 3.5 %collective-permute-done.18.sibling = f32[4,64,2048]{2,1,0:T(8,128)S(1)} collective-permute-done((f32[4,64,2048]{2,1,0:T(8,128)S(1)}, f32[4,64,2048]{2,1,0:T(8,128)S(1)}, u32[]{:S(2)}, u32[]{:S(2)}) %collective-permute-start.18) | collective-permute-done | bytes 2097184 | tf_op jit(solution)/shard_map/ppermute | solution.py:109
  76.8 1.6 %collective-permute-start.19 = (f16[1040,128]{1,0:T(8,128)(2,1)S(1)}, f16[1040,128]{1,0:T(8,128)(2,1)S(1)}, u32[]{:S(2)}, u32[]{:S(2)}) collective-permute-start(f16[1040,128]{1,0:T(8,128)(2,1)S(1)} %convert_element_type.82), channel_id=1, source_target_pairs={{0,2},{1,3},{2,0},{3,1},{4,6},{5,7},{6,4},{7,5},{8,10},{9,11},{10,... | collective-permute-start | bytes 798728 | tf_op jit(solution)/shard_map/ppermute | solution.py:109
  78.3 1.0 sort.19.refs_0_
  79.9 2.1 %partial_ladder.9.part = f32[4,32,2048]{2,1,0:T(8,128)S(1)} custom-call(s32[2]{0:T(128)S(1)} %pad_add_fusion.place, s32[24]{0:T(128)S(1)} %copy-done.7, s32[8,2]{1,0:T(8,128)S(1)} %copy.16.product, s32[8,2]{1,0:T(8,128)S(1)} %copy.17.summed, bf16[128,2048]{1,0:T(8,128)(2,1)S(1)} %collective-permute-done.13.refs_0_, bf16[2048,2048]{1,0:T(8,128)(2,1)S(1)} %copy-done.2), custom_call_target="tpu_custom_call" | custom-call | flops 1000 | bytes 1000 | tf_op jit(solution)/shard_map/partial_ladder/pallas_call | solution.py:165
  82.6 1.0 sort.22.refs_0_
  84.2 3.5 %collective-permute-done.17 = f16[1040,128]{1,0:T(8,128)(2,1)S(1)} collective-permute-done((f16[1040,128]{1,0:T(8,128)(2,1)S(1)}, f16[1040,128]{1,0:T(8,128)(2,1)S(1)}, u32[]{:S(2)}, u32[]{:S(2)}) %collective-permute-start.17) | collective-permute-done | bytes 266272 | tf_op jit(solution)/shard_map/ppermute | solution.py:109
  88.2 1.6 %collective-permute-start.23 = (f16[3,528,128]{2,1,0:T(8,128)(2,1)S(1)}, f16[3,528,128]{2,1,0:T(8,128)(2,1)S(1)}, u32[]{:S(2)}, u32[]{:S(2)}) collective-permute-start(f16[3,528,128]{2,1,0:T(8,128)(2,1)S(1)} %convert_element_type.81), channel_id=1, source_target_pairs={{0,2},{1,3},{2,0},{3,1},{4,6},{5,7},{6,4},{7,5},{8,10},{9,11},{10,... | collective-permute-start | bytes 1216520 | tf_op jit(solution)/shard_map/ppermute | solution.py:109
  90.6 1.6 %collective-permute-start.22 = (f16[528,128]{1,0:T(8,128)(2,1)S(1)}, f16[528,128]{1,0:T(8,128)(2,1)S(1)}, u32[]{:S(2)}, u32[]{:S(2)}) collective-permute-start(f16[528,128]{1,0:T(8,128)(2,1)S(1)} %convert_element_type.85), channel_id=1, source_target_pairs={{0,2},{1,3},{2,0},{3,1},{4,6},{5,7},{6,4},{7,5},{8,10},{9,11},{10,... | collective-permute-start | bytes 405512 | tf_op jit(solution)/shard_map/ppermute | solution.py:109
  94.0 9.4 %collective-permute-done.22 = f16[528,128]{1,0:T(8,128)(2,1)S(1)} collective-permute-done((f16[528,128]{1,0:T(8,128)(2,1)S(1)}, f16[528,128]{1,0:T(8,128)(2,1)S(1)}, u32[]{:S(2)}, u32[]{:S(2)}) %collective-permute-start.22) | collective-permute-done | bytes 135200 | tf_op jit(solution)/shard_map/ppermute | solution.py:109
  104.7 0.7 turn.5.refs_1_
  105.4 0.7 turn.6.refs_2_
  106.1 0.7 turn.7.refs_3_
  107.4 1.3 %gather.1.sums = f32[4,64,2048]{2,1,0:T(8,128)S(1)} custom-call(s32[2]{0:T(128)S(1)} %pad_add_fusion.place, f32[4,64,2048]{2,1,0:T(8,128)S(1)} %sort.24.own, f32[3,528,128]{2,1,0:T(8,128)S(1)} %convert_element_type.87.rest, f32[32,2048]{1,0:T(8,128)S(1)} %turn.4.refs_0_, f32[64,2048]{1,0:T(8,128)S(1)} %turn.5.refs_1_, f32[64,2048]{1,0:T(8,128)S(1)} %turn.6.refs_2_, ...), custom_call_target="tpu_custom_call" | custom-call | flops 1000 | bytes 1000 | tf_op jit(solution)/shard_map/gather/pallas_call | solution.py:291
  108.8 4.1 %collective-permute-done.25 = f16[528,128]{1,0:T(8,128)(2,1)S(1)} collective-permute-done((f16[528,128]{1,0:T(8,128)(2,1)S(1)}, f16[528,128]{1,0:T(8,128)(2,1)S(1)}, u32[]{:S(2)}, u32[]{:S(2)}) %collective-permute-start.25) | collective-permute-done | bytes 135200 | tf_op jit(solution)/shard_map/ppermute | solution.py:109
  112.9 2.6 %finish.1 = bf16[256,2048]{1,0:T(8,128)(2,1)} custom-call(s32[2]{0:T(128)S(1)} %pad_add_fusion.place, f32[4,64,2048]{2,1,0:T(8,128)S(1)} %gather.1.sums, f32[3,528,128]{2,1,0:T(8,128)S(1)} %convert_element_type.93.rest, f32[528,128]{1,0:T(8,128)S(1)} %convert_element_type.95.last), custom_call_target="tpu_custom_call" | custom-call | flops 1000 | bytes 1000 | tf_op jit(solution)/shard_map/finish/pallas_call | solution.py:326
  (83 shorter events, 13.0 us)
Async XLA Ops:
  0.0 15.2 %collective-permute-start.1 = (bf16[128,2048]{1,0:T(8,128)(2,1)}, bf16[128,2048]{1,0:T(8,128)(2,1)S(1)}, u32[]{:S(2)}, u32[]{:S(2)}) collective-permute-start(bf16[128,2048]{1,0:T(8,128)(2,1)} %refs_0_.1), channel_id=1, source_target_pairs={{0,8},{1,9},{2,10},{3,11},{4,12},{5,13},{6,14},{7,15},{8,0},{9,1},... | collective-permute-start | bytes 1572872 | tf_op jit(solution)/shard_map/ppermute | solution.py:109
  3.0 13.6 %collective-permute-start = (bf16[128,2048]{1,0:T(8,128)(2,1)}, bf16[128,2048]{1,0:T(8,128)(2,1)S(1)}, u32[]{:S(2)}, u32[]{:S(2)}) collective-permute-start(bf16[128,2048]{1,0:T(8,128)(2,1)} %refs_0_.1), channel_id=1, source_target_pairs={{0,4},{1,5},{2,6},{3,7},{4,0},{5,1},{6,2},{7,3},{8,12},{9,13},{10,... | collective-permute-start | bytes 1572872 | tf_op jit(solution)/shard_map/ppermute | solution.py:109
  4.5 12.9 %collective-permute-start.2 = (bf16[128,2048]{1,0:T(8,128)(2,1)}, bf16[128,2048]{1,0:T(8,128)(2,1)}, u32[]{:S(2)}, u32[]{:S(2)}) collective-permute-start(bf16[128,2048]{1,0:T(8,128)(2,1)} %refs_0_.1), channel_id=1, source_target_pairs={{8,16},{9,17},{10,18},{11,19},{12,20},{13,21},{14,22},{15,23},{16,... | collective-permute-start | bytes 1572872 | tf_op jit(solution)/shard_map/ppermute | solution.py:109
  7.5 3.4 %copy-start = (bf16[2048,2048]{1,0:T(8,128)(2,1)S(1)}, bf16[2048,2048]{1,0:T(8,128)(2,1)}, u32[]{:S(2)}) copy-start(bf16[2048,2048]{1,0:T(8,128)(2,1)} %refs_1_.3) | copy-start | bytes 25165828
  10.9 1.0 copy-start.3
  12.0 0.7 copy-start.6
  12.6 10.6 %copy-start.7 = (s32[24]{0:T(128)S(1)}, s32[24]{0:T(128)}, u32[]{:S(2)}) copy-start(s32[24]{0:T(128)} %irrep.9) | copy-start | bytes 292
  16.6 0.8 copy-start.4
  17.4 13.5 %collective-permute-start.6 = (f32[4,32,2048]{2,1,0:T(8,128)S(1)}, f32[4,32,2048]{2,1,0:T(8,128)S(1)}, u32[]{:S(2)}, u32[]{:S(2)}) collective-permute-start(f32[4,32,2048]{2,1,0:T(8,128)S(1)} %partial_ladder.5.part), channel_id=1, source_target_pairs={{0,1},{1,0},{2,3},{3,2},{4,5},{5,4},{6,7},{7,6},{8,9},{9,8},{10,11... | collective-permute-start | bytes 3145736 | tf_op jit(solution)/shard_map/ppermute | solution.py:109
  17.4 16.7 %collective-permute-start.5 = (bf16[128,2048]{1,0:T(8,128)(2,1)}, bf16[128,2048]{1,0:T(8,128)(2,1)}, u32[]{:S(2)}, u32[]{:S(2)}) collective-permute-start(bf16[128,2048]{1,0:T(8,128)(2,1)} %collective-permute-done.2), channel_id=1, source_target_pairs={{0,8},{1,9},{2,10},{3,11},{4,12},{5,13},{6,14},{7,15},{8,0},{9,1},... | collective-permute-start | bytes 1572872 | tf_op jit(solution)/shard_map/ppermute | solution.py:109
  21.2 14.2 %collective-permute-start.4 = (bf16[128,2048]{1,0:T(8,128)(2,1)S(1)}, bf16[128,2048]{1,0:T(8,128)(2,1)}, u32[]{:S(2)}, u32[]{:S(2)}) collective-permute-start(bf16[128,2048]{1,0:T(8,128)(2,1)S(1)} %collective-permute-done.1.refs_1_), channel_id=1, source_target_pairs={{8,16},{9,17},{10,18},{11,19},{12,20},{13,21},{14,22},{15,23},{16,... | collective-permute-start | bytes 1572872 | tf_op jit(solution)/shard_map/ppermute | solution.py:109
  22.7 14.1 %collective-permute-start.3 = (bf16[128,2048]{1,0:T(8,128)(2,1)S(1)}, bf16[128,2048]{1,0:T(8,128)(2,1)S(1)}, u32[]{:S(2)}, u32[]{:S(2)}) collective-permute-start(bf16[128,2048]{1,0:T(8,128)(2,1)S(1)} %collective-permute-done.1.refs_1_), channel_id=1, source_target_pairs={{0,4},{1,5},{2,6},{3,7},{4,0},{5,1},{6,2},{7,3},{8,12},{9,13},{10,... | collective-permute-start | bytes 1572872 | tf_op jit(solution)/shard_map/ppermute | solution.py:109
  23.3 3.4 %copy-start.1 = (bf16[2048,2048]{1,0:T(8,128)(2,1)S(1)}, bf16[2048,2048]{1,0:T(8,128)(2,1)}, u32[]{:S(2)}) copy-start(bf16[2048,2048]{1,0:T(8,128)(2,1)} %refs_1_.3) | copy-start | bytes 25165828
  26.6 1.0 copy-start.5
  31.2 5.5 %collective-permute-start.7 = (f16[528,128]{1,0:T(8,128)(2,1)S(1)}, f16[528,128]{1,0:T(8,128)(2,1)S(1)}, u32[]{:S(2)}, u32[]{:S(2)}) collective-permute-start(f16[528,128]{1,0:T(8,128)(2,1)S(1)} %convert_element_type.72), channel_id=1, source_target_pairs={{0,2},{1,3},{2,0},{3,1},{4,6},{5,7},{6,4},{7,5},{8,10},{9,11},{10,... | collective-permute-start | bytes 405512 | tf_op jit(solution)/shard_map/ppermute | solution.py:109
  34.2 9.3 %copy-start.2 = (bf16[2048,2048]{1,0:T(8,128)(2,1)S(1)}, bf16[2048,2048]{1,0:T(8,128)(2,1)}, u32[]{:S(2)}) copy-start(bf16[2048,2048]{1,0:T(8,128)(2,1)} %refs_1_.3) | copy-start | bytes 25165828
  36.8 10.0 %collective-permute-start.11 = (f32[4,64,2048]{2,1,0:T(8,128)S(1)}, f32[4,64,2048]{2,1,0:T(8,128)S(1)}, u32[]{:S(2)}, u32[]{:S(2)}) collective-permute-start(f32[4,64,2048]{2,1,0:T(8,128)S(1)} %partial_ladder.6.part), channel_id=1, source_target_pairs={{0,1},{1,0},{2,3},{3,2},{4,5},{5,4},{6,7},{7,6},{8,9},{9,8},{10,11... | collective-permute-start | bytes 6291464 | tf_op jit(solution)/shard_map/ppermute | solution.py:109
  36.8 17.9 %collective-permute-start.9 = (bf16[128,2048]{1,0:T(8,128)(2,1)}, bf16[128,2048]{1,0:T(8,128)(2,1)S(1)}, u32[]{:S(2)}, u32[]{:S(2)}) collective-permute-start(bf16[128,2048]{1,0:T(8,128)(2,1)} %collective-permute-done.4), channel_id=1, source_target_pairs={{0,8},{1,9},{2,10},{3,11},{4,12},{5,13},{6,14},{7,15},{8,0},{9,1},... | collective-permute-start | bytes 1572872 | tf_op jit(solution)/shard_map/ppermute | solution.py:109
  39.0 15.8 %collective-permute-start.8 = (bf16[128,2048]{1,0:T(8,128)(2,1)S(1)}, bf16[128,2048]{1,0:T(8,128)(2,1)S(1)}, u32[]{:S(2)}, u32[]{:S(2)}) collective-permute-start(bf16[128,2048]{1,0:T(8,128)(2,1)S(1)} %broadcast_select_fusion.1.refs_1_), channel_id=1, source_target_pairs={{0,4},{1,5},{2,6},{3,7},{4,0},{5,1},{6,2},{7,3},{8,12},{9,13},{10,... | collective-permute-start | bytes 1572872 | tf_op jit(solution)/shard_map/ppermute | solution.py:109
  41.4 13.4 %collective-permute-start.10 = (f16[528,128]{1,0:T(8,128)(2,1)S(1)}, f16[528,128]{1,0:T(8,128)(2,1)S(1)}, u32[]{:S(2)}, u32[]{:S(2)}) collective-permute-start(f16[528,128]{1,0:T(8,128)(2,1)S(1)} %convert_element_type.74), channel_id=1, source_target_pairs={{0,16},{1,17},{2,18},{3,19},{4,20},{5,21},{6,22},{7,23},{8,24},{9,... | collective-permute-start | bytes 405512 | tf_op jit(solution)/shard_map/ppermute | solution.py:109
  47.2 7.6 %collective-permute-start.12 = (f16[1040,128]{1,0:T(8,128)(2,1)S(1)}, f16[1040,128]{1,0:T(8,128)(2,1)S(1)}, u32[]{:S(2)}, u32[]{:S(2)}) collective-permute-start(f16[1040,128]{1,0:T(8,128)(2,1)S(1)} %convert_element_type.75), channel_id=1, source_target_pairs={{0,2},{1,3},{2,0},{3,1},{4,6},{5,7},{6,4},{7,5},{8,10},{9,11},{10,... | collective-permute-start | bytes 798728 | tf_op jit(solution)/shard_map/ppermute | solution.py:109
  54.8 4.7 %collective-permute-start.15 = (f32[4,64,2048]{2,1,0:T(8,128)S(1)}, f32[4,64,2048]{2,1,0:T(8,128)S(1)}, u32[]{:S(2)}, u32[]{:S(2)}) collective-permute-start(f32[4,64,2048]{2,1,0:T(8,128)S(1)} %partial_ladder.7.part), channel_id=1, source_target_pairs={{0,1},{1,0},{2,3},{3,2},{4,5},{5,4},{6,7},{7,6},{8,9},{9,8},{10,11... | collective-permute-start | bytes 6291464 | tf_op jit(solution)/shard_map/ppermute | solution.py:109
  54.9 17.2 %collective-permute-start.13 = (bf16[128,2048]{1,0:T(8,128)(2,1)S(1)}, bf16[128,2048]{1,0:T(8,128)(2,1)S(1)}, u32[]{:S(2)}, u32[]{:S(2)}) collective-permute-start(bf16[128,2048]{1,0:T(8,128)(2,1)S(1)} %broadcast_select_fusion.refs_1_), channel_id=1, source_target_pairs={{0,4},{1,5},{2,6},{3,7},{4,0},{5,1},{6,2},{7,3},{8,12},{9,13},{10,... | collective-permute-start | bytes 1572872 | tf_op jit(solution)/shard_map/ppermute | solution.py:109
  57.0 15.1 %collective-permute-start.14 = (f16[1040,128]{1,0:T(8,128)(2,1)S(1)}, f16[1040,128]{1,0:T(8,128)(2,1)S(1)}, u32[]{:S(2)}, u32[]{:S(2)}) collective-permute-start(f16[1040,128]{1,0:T(8,128)(2,1)S(1)} %convert_element_type.77), channel_id=1, source_target_pairs={{0,16},{1,17},{2,18},{3,19},{4,20},{5,21},{6,22},{7,23},{8,24},{9,... | collective-permute-start | bytes 798728 | tf_op jit(solution)/shard_map/ppermute | solution.py:109
  60.0 12.1 %collective-permute-start.16 = (f16[1040,128]{1,0:T(8,128)(2,1)S(1)}, f16[1040,128]{1,0:T(8,128)(2,1)S(1)}, u32[]{:S(2)}, u32[]{:S(2)}) collective-permute-start(f16[1040,128]{1,0:T(8,128)(2,1)S(1)} %convert_element_type.78), channel_id=1, source_target_pairs={{0,2},{1,3},{2,0},{3,1},{4,6},{5,7},{6,4},{7,5},{8,10},{9,11},{10,... | collective-permute-start | bytes 798728 | tf_op jit(solution)/shard_map/ppermute | solution.py:109
  72.1 4.2 %collective-permute-start.18 = (f32[4,64,2048]{2,1,0:T(8,128)S(1)}, f32[4,64,2048]{2,1,0:T(8,128)S(1)}, u32[]{:S(2)}, u32[]{:S(2)}) collective-permute-start(f32[4,64,2048]{2,1,0:T(8,128)S(1)} %partial_ladder.8.part), channel_id=1, source_target_pairs={{0,1},{1,0},{2,3},{3,2},{4,5},{5,4},{6,7},{7,6},{8,9},{9,8},{10,11... | collective-permute-start | bytes 6291464 | tf_op jit(solution)/shard_map/ppermute | solution.py:109
  72.6 15.0 %collective-permute-start.17 = (f16[1040,128]{1,0:T(8,128)(2,1)S(1)}, f16[1040,128]{1,0:T(8,128)(2,1)S(1)}, u32[]{:S(2)}, u32[]{:S(2)}) collective-permute-start(f16[1040,128]{1,0:T(8,128)(2,1)S(1)} %convert_element_type.80), channel_id=1, source_target_pairs={{0,16},{1,17},{2,18},{3,19},{4,20},{5,21},{6,22},{7,23},{8,24},{9,... | collective-permute-start | bytes 798728 | tf_op jit(solution)/shard_map/ppermute | solution.py:109
  76.8 10.9 %collective-permute-start.19 = (f16[1040,128]{1,0:T(8,128)(2,1)S(1)}, f16[1040,128]{1,0:T(8,128)(2,1)S(1)}, u32[]{:S(2)}, u32[]{:S(2)}) collective-permute-start(f16[1040,128]{1,0:T(8,128)(2,1)S(1)} %convert_element_type.82), channel_id=1, source_target_pairs={{0,2},{1,3},{2,0},{3,1},{4,6},{5,7},{6,4},{7,5},{8,10},{9,11},{10,... | collective-permute-start | bytes 798728 | tf_op jit(solution)/shard_map/ppermute | solution.py:109
  87.6 2.7 %collective-permute-start.21 = (f32[4,32,2048]{2,1,0:T(8,128)S(1)}, f32[4,32,2048]{2,1,0:T(8,128)S(1)}, u32[]{:S(2)}, u32[]{:S(2)}) collective-permute-start(f32[4,32,2048]{2,1,0:T(8,128)S(1)} %partial_ladder.9.part), channel_id=1, source_target_pairs={{0,1},{1,0},{2,3},{3,2},{4,5},{5,4},{6,7},{7,6},{8,9},{9,8},{10,11... | collective-permute-start | bytes 3145736 | tf_op jit(solution)/shard_map/ppermute | solution.py:109
  88.2 15.2 %collective-permute-start.23 = (f16[3,528,128]{2,1,0:T(8,128)(2,1)S(1)}, f16[3,528,128]{2,1,0:T(8,128)(2,1)S(1)}, u32[]{:S(2)}, u32[]{:S(2)}) collective-permute-start(f16[3,528,128]{2,1,0:T(8,128)(2,1)S(1)} %convert_element_type.81), channel_id=1, source_target_pairs={{0,2},{1,3},{2,0},{3,1},{4,6},{5,7},{6,4},{7,5},{8,10},{9,11},{10,... | collective-permute-start | bytes 1216520 | tf_op jit(solution)/shard_map/ppermute | solution.py:109
  89.8 14.1 %collective-permute-start.20 = (f16[1040,128]{1,0:T(8,128)(2,1)S(1)}, f16[1040,128]{1,0:T(8,128)(2,1)S(1)}, u32[]{:S(2)}, u32[]{:S(2)}) collective-permute-start(f16[1040,128]{1,0:T(8,128)(2,1)S(1)} %convert_element_type.84), channel_id=1, source_target_pairs={{0,16},{1,17},{2,18},{3,19},{4,20},{5,21},{6,22},{7,23},{8,24},{9,... | collective-permute-start | bytes 798728 | tf_op jit(solution)/shard_map/ppermute | solution.py:109
  90.6 12.8 %collective-permute-start.22 = (f16[528,128]{1,0:T(8,128)(2,1)S(1)}, f16[528,128]{1,0:T(8,128)(2,1)S(1)}, u32[]{:S(2)}, u32[]{:S(2)}) collective-permute-start(f16[528,128]{1,0:T(8,128)(2,1)S(1)} %convert_element_type.85), channel_id=1, source_target_pairs={{0,2},{1,3},{2,0},{3,1},{4,6},{5,7},{6,4},{7,5},{8,10},{9,11},{10,... | collective-permute-start | bytes 405512 | tf_op jit(solution)/shard_map/ppermute | solution.py:109
  92.8 20.1 %collective-permute-start.24 = (f16[3,528,128]{2,1,0:T(8,128)(2,1)S(1)}, f16[3,528,128]{2,1,0:T(8,128)(2,1)S(1)}, u32[]{:S(2)}, u32[]{:S(2)}) collective-permute-start(f16[3,528,128]{2,1,0:T(8,128)(2,1)S(1)} %convert_element_type.92), channel_id=1, source_target_pairs={{0,2},{1,3},{2,0},{3,1},{4,6},{5,7},{6,4},{7,5},{8,10},{9,11},{10,... | collective-permute-start | bytes 1216520 | tf_op jit(solution)/shard_map/ppermute | solution.py:109
  104.0 8.9 %collective-permute-start.25 = (f16[528,128]{1,0:T(8,128)(2,1)S(1)}, f16[528,128]{1,0:T(8,128)(2,1)S(1)}, u32[]{:S(2)}, u32[]{:S(2)}) collective-permute-start(f16[528,128]{1,0:T(8,128)(2,1)S(1)} %convert_element_type.94), channel_id=1, source_target_pairs={{0,16},{1,17},{2,18},{3,19},{4,20},{5,21},{6,22},{7,23},{8,24},{9,... | collective-permute-start | bytes 405512 | tf_op jit(solution)/shard_map/ppermute | solution.py:109
